TPU v7x, 512 devices: a whole 4x8x8 slice. The times are simulated.
512 devices in a mesh: nodes: 64 (over z_hi, y, x), heads: 8 (over z_lo, core).
Axes of the slice: x: 4, y: 8, z: 8 (z_hi: 2, z_lo: 4; z = z_hi * 4 + z_lo), core: 2. Of those that a mesh axis runs over, the one named last changes fastest.
Arguments:
- features: bfloat16 [65536, 1024], P(('nodes', 'heads')), may hold values from -32 to 32
- node_order: int32 [65536], P('nodes'), may hold values from 0 to 1023, as said below
- partners: int32 [3, 512], P(None, 'nodes'), may hold values from 0 to 511, as said below
- query_weight: bfloat16 [1024, 1024], P(None, 'heads'), may hold values from -0.1875 to 0.1875
- key_weight: bfloat16 [1024, 1024], P(None, 'heads'), may hold values from -0.1875 to 0.1875
- value_weight: bfloat16 [1024, 1024], P(None, 'heads'), may hold values from -0.1875 to 0.1875
- upstream: bfloat16 [65536, 1024], P(('nodes', 'heads')), may hold values from -6 to 6
Outputs:
- attended: bfloat16 [65536, 1024], P(('nodes', 'heads'))
- feature_grad: bfloat16 [65536, 1024], P(('nodes', 'heads'))
- query_grad: float32 [1024, 1024], P(None, 'heads')
- key_grad: float32 [1024, 1024], P(None, 'heads')
- value_grad: float32 [1024, 1024], P(None, 'heads')
Inputs may be any that keep to these rules, and one draw needn't show every extreme that they name: `node_order`: each aligned block of 1024 entries, one node group, lists every index of 0 to 1023 once. `partners`: each row is a perfect matching of the blocks and its own inverse, with no block paired with itself; a block of node group g (blocks g * 8 to g * 8 + 7) is paired in rows 0, 1, 2 with a block of the group whose index differs from g in the bit of value 1, 16, 32.
All inputs are finite; a program needn't handle non-finite values.
Results may differ from a plain program's by a relative error of at most 0.02.
Values may be sent and summed in bfloat16 or wider, within the bound.
No kernel may reach another device: no remote copies, remote signals or barrier semaphores. Data moves between devices by JAX's collectives and lax.ppermute only.
A program may use at most 128 MiB of HBM per device.

v0:
```python
import math

import jax
import jax.numpy as jnp
from jax import lax
from jax.sharding import PartitionSpec as P

HDIM = 64
BLOCK = 128


def from_partner(block, axis, bit):
    count = lax.axis_size(axis)
    route = []
    for low in range(count):
        high = low | 1 << bit
        if high != low and high < count:
            route += [(low, high), (high, low)]
    return lax.ppermute(block, axis, route)


def local(features, node_order, partners, query_weight, key_weight, value_weight, upstream):
    local_width = query_weight.shape[1]
    local_heads = local_width // HDIM
    score_scale = 1.0 / math.sqrt(HDIM)
    stacked = jnp.concatenate([query_weight, key_weight, value_weight], axis=1)
    projected = jnp.dot(
        lax.all_gather(features, "heads", axis=0, tiled=True),
        stacked,
        preferred_element_type=jnp.float32,
    ).astype(jnp.bfloat16)
    group_rows = projected.shape[0]
    blocks = group_rows // BLOCK
    ordered = jnp.take(projected, node_order, axis=0)
    queries = ordered[:, :local_width].reshape(blocks, BLOCK, local_heads, HDIM)
    own_pairs = ordered[:, local_width:]
    partner_slots = partners % blocks
    levels = lax.axis_size("nodes").bit_length() - 1
    swap_bits = (0, levels - 2, levels - 1)
    key_blocks = [own_pairs.reshape(blocks, BLOCK, 2 * local_width)]
    for fetch_matching in range(3):
        fetch_arrived = from_partner(own_pairs, "nodes", swap_bits[fetch_matching])
        key_blocks.append(
            jnp.take(
                fetch_arrived.reshape(blocks, BLOCK, 2 * local_width),
                partner_slots[fetch_matching],
                axis=0,
            )
        )
    joined = jnp.concatenate(key_blocks, axis=1)
    key_sets = joined[..., :local_width].reshape(blocks, 4 * BLOCK, local_heads, HDIM)
    value_sets = joined[..., local_width:].reshape(blocks, 4 * BLOCK, local_heads, HDIM)
    key_sets, value_sets = (key_sets, value_sets)
    scores = (
        jnp.einsum("bqhd,bkhd->bhqk", queries, key_sets, preferred_element_type=jnp.float32)
        * score_scale
    )
    row_peak = jnp.max(scores, axis=-1, keepdims=True)
    logsum = row_peak + jnp.log(jnp.sum(jnp.exp(scores - row_peak), axis=-1, keepdims=True))
    softmax = jnp.exp(scores - logsum)
    weights_low = softmax.astype(jnp.bfloat16)
    mixed_rows = jnp.einsum(
        "bhqk,bkhd->bqhd", weights_low, value_sets, preferred_element_type=jnp.float32
    ).astype(jnp.bfloat16)
    node_rows = (
        jnp.zeros((group_rows, local_width), jnp.bfloat16)
        .at[node_order]
        .set(mixed_rows.reshape(group_rows, local_width))
    )
    attended = lax.all_to_all(node_rows, "heads", split_axis=0, concat_axis=1, tiled=True)
    arriving = lax.all_to_all(upstream, "heads", split_axis=1, concat_axis=0, tiled=True)
    incoming = jnp.take(arriving, node_order, axis=0).reshape(blocks, BLOCK, local_heads, HDIM)
    back_keys, back_values = (key_sets, value_sets)
    dprobs = jnp.einsum(
        "bqhd,bkhd->bhqk", incoming, back_values, preferred_element_type=jnp.float32
    )
    row_delta = jnp.sum(softmax * dprobs, axis=-1, keepdims=True)
    dscores = (softmax * (dprobs - row_delta) * score_scale).astype(jnp.bfloat16)
    dquery = jnp.einsum("bhqk,bkhd->bqhd", dscores, back_keys, preferred_element_type=jnp.float32)
    key_parts = jnp.einsum(
        "bhqk,bqhd->bkhd", dscores, queries, preferred_element_type=jnp.float32
    ).reshape(blocks, 4 * BLOCK, local_width)
    value_parts = jnp.einsum(
        "bhqk,bqhd->bkhd", weights_low, incoming, preferred_element_type=jnp.float32
    ).reshape(blocks, 4 * BLOCK, local_width)
    grad_parts = jnp.concatenate([key_parts, value_parts], axis=2)
    returned = grad_parts[:, :BLOCK]
    for matching in range(3):
        arrived = from_partner(
            grad_parts[:, (matching + 1) * BLOCK : (matching + 2) * BLOCK].astype(jnp.bfloat16),
            "nodes",
            swap_bits[matching],
        ).astype(jnp.float32)
        returned = returned + jnp.take(arrived, partner_slots[matching], axis=0)
    key_total = returned[..., :local_width]
    value_total = returned[..., local_width:]
    grad_rows = jnp.concatenate(
        [
            dquery.reshape(group_rows, local_width),
            key_total.reshape(group_rows, local_width),
            value_total.reshape(group_rows, local_width),
        ],
        axis=1,
    ).astype(jnp.bfloat16)
    grad_nodes = (
        jnp.zeros((group_rows, 3 * local_width), jnp.bfloat16).at[node_order].set(grad_rows)
    )
    block_rows = grad_nodes
    partial_grads = lax.dot_general(
        lax.all_gather(features, "heads", axis=0, tiled=True),
        block_rows,
        (((0,), (0,)), ((), ())),
        preferred_element_type=jnp.float32,
    )
    weight_grads = lax.psum(partial_grads, "nodes")
    block_rows = grad_nodes
    feature_grad = lax.psum_scatter(
        lax.dot_general(
            block_rows, stacked, (((1,), (1,)), ((), ())), preferred_element_type=jnp.float32
        ).astype(jnp.bfloat16),
        "heads",
        scatter_dimension=0,
        tiled=True,
    )
    return (
        attended,
        feature_grad,
        weight_grads[:, :local_width],
        weight_grads[:, local_width : 2 * local_width],
        weight_grads[:, 2 * local_width :],
    )


def solution(mesh):
    return jax.shard_map(
        local,
        mesh=mesh,
        in_specs=(
            P(("nodes", "heads"), None),
            P("nodes"),
            P(None, "nodes"),
            P(None, "heads"),
            P(None, "heads"),
            P(None, "heads"),
            P(("nodes", "heads"), None),
        ),
        out_specs=(
            P(("nodes", "heads"), None),
            P(("nodes", "heads"), None),
            P(None, "heads"),
            P(None, "heads"),
            P(None, "heads"),
        ),
        check_vma=False,
    )
```

profile of v0, /device:TPU:1, one launch (start us, length us, event | category | flops | bytes accessed | tf_op | source)
XLA Modules:
  0.0 1088.8 jit_solution(816792961750401966)
XLA Ops:
  8.9 10.2 all-to-all-start.1
  19.8 1.0 constant_dynamic-update-slice_fusion.2
  20.8 1.0 constant_dynamic-update-slice_fusion.1
  21.8 1.0 constant_dynamic-update-slice_fusion
  24.3 32.0 %all-gather.2.cloned.1.call-done = bf16[1024,1024]{1,0:T(8,128)(2,1)} async-done(((bf16[128,1024]{1,0:T(8,128)(2,1)}), bf16[1024,1024]{1,0:T(8,128)(2,1)}) %all-gather.2.cloned.1.call-update) | async-done | bytes 2097168 | tf_op jit(solution)/shard_map/all_gather | solution.py:28
  56.3 2.6 fusion.20
  59.3 3.9 gather_fusion
  63.5 5.7 collective-permute-start.2
  69.1 7.1 collective-permute-start.1
  76.2 3.1 collective-permute-start
  79.4 3.2 gather_fusion.1
  83.8 1.0 copy.42
  84.8 8.9 collective-permute-done.2
  93.7 1.6 gather_fusion.4
  98.6 3.7 fusion.39
  103.2 1.2 exponential_reduce_fusion
  105.2 2.2 fusion.35
  107.4 17.9 %fusion.7 = f32[8,2,64,512]{3,2,1,0:T(8,128)} fusion(bf16[8,128,2,64]{1,3,2,0:T(8,128)(2,1)S(1)} %copy-done.4, f32[8,2,128,512]{3,2,1,0:T(8,128)} %fusion.39, f32[8,2,128,512]{3,2,1,0:T(8,128)} %copy-done.1, f32[8,2,128]{2,1,0:T(2,128)S(1)} %bitcast.93), kind=kOutput, calls=%fused_computation.22 | convolution fusion | flops 143657472 | bytes 10756096 | tf_op jit(solution)/shard_map/bhqk,bqhd->bkhd/dot_general | solution.py:80
  125.3 1.9 copy.53
  127.2 2.9 copy.52
  130.1 1.8 fusion.1
  131.9 1.2 fusion.52
  133.1 3.1 collective-permute-start.3
  136.2 4.7 collective-permute-start.5
  140.9 7.3 collective-permute-start.4
  148.2 18.5 %fusion.24 = bf16[8,128,2,64]{1,3,2,0:T(8,128)(2,1)} fusion(bf16[8,512,2,64]{1,3,2,0:T(8,128)(2,1)} %bitcast.78, f32[8,2,128,512]{3,2,1,0:T(8,128)} %fusion.39, f32[8,2,128,512]{3,2,1,0:T(8,128)} %copy-done.1, f32[8,2,128]{2,1,0:T(2,128)S(1)} %bitcast.94), kind=kOutput, calls=%fused_computation.35 | convolution fusion | flops 143788544 | bytes 9707520 | tf_op jit(solution)/shard_map/bhqk,bkhd->bqhd/dot_general | solution.py:79
  166.6 1.1 copy.49
  168.5 2.1 convert_element_type.40
  170.7 2.8 gather_fusion.5
  173.5 2.1 convert_element_type.42
  175.6 2.8 gather_fusion.7
  178.4 2.2 convert_element_type.41
  180.6 2.8 gather_fusion.6
  183.4 2.4 fusion.32
  186.3 1.0 pad_maximum_fusion.2
  187.6 5.2 scatter_custom_fusion.1
  192.9 3.8 convolution_bitcast_fusion
  197.0 2.6 convolution_convert_fusion
  199.6 3.2 fusion.27
  203.5 3.2 scatter_custom_fusion
  206.7 16.4 %all_to_all.38 = bf16[8,128,128]{2,1,0:T(8,128)(2,1)S(1)} all-to-all(bf16[8,128,128]{2,1,0:T(8,128)(2,1)S(1)} %bitcast.81), channel_id=1, replica_groups=mesh['nodes'=64,'heads'=8] {'heads'}, dimensions={0} | all-to-all | bytes 524288 | tf_op jit(solution)/shard_map/all_to_all | solution.py:70
  223.3 0.9 copy.57
  224.2 770.8 %all-reduce.2.cloned.1.call-done = f32[1024,384]{0,1:T(8,128)} async-done(((f32[1024,384]{0,1:T(8,128)}), f32[1024,384]{0,1:T(8,128)}) %all-reduce.2.cloned.1.call-update) | async-done | bytes 1572880 | tf_op jit(solution)/shard_map/psum | solution.py:115
  995.0 1.5 fusion.54
  996.5 1.0 copy.60
  997.5 1.0 copy.59
  998.5 1.0 copy.58
  999.5 82.9 %reduce-scatter.2.cloned.1.call-done = bf16[128,1024]{1,0:T(8,128)(2,1)} async-done(((bf16[1024,1024]{1,0:T(8,128)(2,1)}), bf16[128,1024]{1,0:T(8,128)(2,1)}) %reduce-scatter.2.cloned.1.call-update) | async-done | bytes 262160 | tf_op jit(solution)/shard_map/reduce_scatter | solution.py:117
  (63 shorter events, 13.0 us)
Async XLA Ops:
  7.2 1.0 copy-start
  7.2 49.1 %all-gather.2.cloned.1.call-start = ((), (), s32[]{:S(2)}) async-start(), calls=%async_computation.3 | async-start | bytes 2359296 | tf_op jit(solution)/shard_map/all_gather | solution.py:28
  8.9 70.5 %all-to-all-start.1 = ((bf16[128,8,128]{2,0,1:T(8,128)(2,1)}), bf16[128,8,128]{2,0,1:T(8,128)(2,1)S(1)}, u32[]{:S(2)}, u32[]{:S(2)}) async-start(bf16[128,8,128]{2,0,1:T(8,128)(2,1)} %copy_bitcast_fusion.1), calls=%async_computation.1 | async-start | bytes 524288 | tf_op jit(solution)/shard_map/all_to_all | solution.py:71
  19.1 975.9 %all-reduce.2.cloned.1.call-start = ((), (), s32[]{:S(2)}) async-start(), calls=%async_computation.5 | async-start | bytes 3145728 | tf_op jit(solution)/shard_map/psum | solution.py:115
  22.8 33.5 %copy-start.5 = (bf16[1024,384]{1,0:T(8,128)(2,1)}, bf16[1024,384]{1,0:T(8,128)(2,1)S(1)}, u32[]{:S(2)}) copy-start(bf16[1024,384]{1,0:T(8,128)(2,1)S(1)} %constant_dynamic-update-slice_fusion) | copy-start | bytes 2359300
  59.3 20.1 %copy-start.7 = (s32[1024]{0:T(1024)S(1)}, s32[1024]{0:T(1024)}, u32[]{:S(2)}) copy-start(s32[1024]{0:T(1024)} %param.12) | copy-start | bytes 12292
  63.5 30.3 %collective-permute-start.2 = (bf16[1024,256]{1,0:T(8,128)(2,1)S(1)}, bf16[1024,256]{1,0:T(8,128)(2,1)}, u32[]{:S(2)}, u32[]{:S(2)}) collective-permute-start(bf16[1024,256]{1,0:T(8,128)(2,1)S(1)} %slice.88), channel_id=1, source_target_pairs={{0,256},{256,0},{8,264},{264,8},{16,272},{272,16},{24,280},{280,24... | collective-permute-start | bytes 1572872 | tf_op jit(solution)/shard_map/ppermute | solution.py:19
  69.1 26.2 %collective-permute-start.1 = (bf16[1024,256]{1,0:T(8,128)(2,1)S(1)}, bf16[1024,256]{1,0:T(8,128)(2,1)S(1)}, u32[]{:S(2)}, u32[]{:S(2)}) collective-permute-start(bf16[1024,256]{1,0:T(8,128)(2,1)S(1)} %slice.88), channel_id=1, source_target_pairs={{0,128},{128,0},{8,136},{136,8},{16,144},{144,16},{24,152},{152,24... | collective-permute-start | bytes 1572872 | tf_op jit(solution)/shard_map/ppermute | solution.py:19
  76.2 19.7 %collective-permute-start = (bf16[1024,256]{1,0:T(8,128)(2,1)S(1)}, bf16[1024,256]{1,0:T(8,128)(2,1)S(1)}, u32[]{:S(2)}, u32[]{:S(2)}) collective-permute-start(bf16[1024,256]{1,0:T(8,128)(2,1)S(1)} %slice.88), channel_id=1, source_target_pairs={{0,8},{8,0},{16,24},{24,16},{32,40},{40,32},{48,56},{56,48},{64,72... | collective-permute-start | bytes 1572872 | tf_op jit(solution)/shard_map/ppermute | solution.py:19
  98.1 5.1 copy-start.2
  98.6 3.7 copy-start.4
  102.4 2.8 copy-start.3
  103.2 2.0 copy-start.1
  133.1 35.4 %collective-permute-start.3 = (bf16[8,128,256]{2,1,0:T(8,128)(2,1)}, bf16[8,128,256]{2,1,0:T(8,128)(2,1)}, u32[]{:S(2)}, u32[]{:S(2)}) collective-permute-start(bf16[8,128,256]{2,1,0:T(8,128)(2,1)} %get-tuple-element.28), channel_id=1, source_target_pairs={{0,8},{8,0},{16,24},{24,16},{32,40},{40,32},{48,56},{56,48},{64,72... | collective-permute-start | bytes 1572872 | tf_op jit(solution)/shard_map/ppermute | solution.py:19
  136.2 37.3 %collective-permute-start.5 = (bf16[8,128,256]{2,1,0:T(8,128)(2,1)}, bf16[8,128,256]{2,1,0:T(8,128)(2,1)}, u32[]{:S(2)}, u32[]{:S(2)}) collective-permute-start(bf16[8,128,256]{2,1,0:T(8,128)(2,1)} %get-tuple-element.29), channel_id=1, source_target_pairs={{0,256},{256,0},{8,264},{264,8},{16,272},{272,16},{24,280},{280,24... | collective-permute-start | bytes 1572872 | tf_op jit(solution)/shard_map/ppermute | solution.py:19
  140.9 37.5 %collective-permute-start.4 = (bf16[8,128,256]{2,1,0:T(8,128)(2,1)}, bf16[8,128,256]{2,1,0:T(8,128)(2,1)}, u32[]{:S(2)}, u32[]{:S(2)}) collective-permute-start(bf16[8,128,256]{2,1,0:T(8,128)(2,1)} %get-tuple-element.30), channel_id=1, source_target_pairs={{0,128},{128,0},{8,136},{136,8},{16,144},{144,16},{24,152},{152,24... | collective-permute-start | bytes 1572872 | tf_op jit(solution)/shard_map/ppermute | solution.py:19
  192.8 4.1 copy-start.6
  196.7 885.6 %reduce-scatter.2.cloned.1.call-start = ((), (), s32[]{:S(2)}) async-start(), calls=%async_computation.4 | async-start | bytes 2359296 | tf_op jit(solution)/shard_map/reduce_scatter | solution.py:117
Sparse Core Ops, SparseCore 0:
  10.1 46.1 all-gather.1
  196.8 798.1 all-reduce.1
  998.7 83.6 reduce-scatter.1
where the time goes:
time: 1090 us
  waiting for transfers between devices  895 us (82%)
  matrix products  55.4 us (5%)
  local copies, waits for them, and re-layouts  49.7 us (5%)
  starting transfers between devices  41.4 us (4%)
  blocking collectives  16.4 us (2%)
  other arithmetic  16.3 us (1%)
  between operations  14.2 us (1%)
    psum x1, waiting for transfers between devices, local(): weight_grads = lax.psum(partial_grads, 'nodes')  771 us
    reduce_scatter x1, waiting for transfers between devices, local(): lax.psum_scatter(lax.dot_general(block_rows, stacked, (((1,), (1,)), ((),...  82.9 us
    all_gather x1, waiting for transfers between devices, local(): lax.all_gather(features, 'heads', axis=0, tiled=True)  32 us
    ppermute x6, starting transfers between devices, from_partner(): return lax.ppermute(block, axis, route)  30.9 us
  transfers between devices with their start and end apart: 10, of which 4 were waited for; matrix products, arithmetic and copies ran while one was open for 6% of the time, Pallas kernels for 0%

commit v1 on v0

--- a/solution.py
+++ b/solution.py
@@ -17,6 +17,23 @@
         if high != low and high < count:
             route += [(low, high), (high, low)]
     return lax.ppermute(block, axis, route)
+
+
+def summed_over_nodes(partial):
+    count = lax.axis_size("nodes")
+    half = count // 2
+    groups = [list(range(half)), list(range(half, count))]
+    rows, width = partial.shape
+    spread = lax.all_to_all(
+        partial.astype(jnp.bfloat16), "nodes", 0, 0, axis_index_groups=groups, tiled=True
+    )
+    share = jnp.sum(spread.reshape(half, rows // half, width).astype(jnp.float32), axis=0)
+    share = share + from_partner(share, "nodes", half.bit_length() - 1)
+    copies = jnp.broadcast_to(share.astype(jnp.bfloat16)[None], (half, rows // half, width))
+    whole = lax.all_to_all(
+        copies.reshape(rows, width), "nodes", 0, 0, axis_index_groups=groups, tiled=True
+    )
+    return whole.astype(jnp.float32)
 
 
 def local(features, node_order, partners, query_weight, key_weight, value_weight, upstream):
@@ -112,7 +129,7 @@
         (((0,), (0,)), ((), ())),
         preferred_element_type=jnp.float32,
     )
-    weight_grads = lax.psum(partial_grads, "nodes")
+    weight_grads = summed_over_nodes(partial_grads)
     block_rows = grad_nodes
     feature_grad = lax.psum_scatter(
         lax.dot_general(

time: 1090 us -> 289 us (0.27)
  waiting for transfers between devices: 895 us -> 79 us
  starting transfers between devices: 41.4 us -> 70.1 us
  blocking collectives: 16.4 us -> 0 us
    psum x1 -> x0, waiting for transfers between devices: 771 us -> none  [local(): weight_grads = lax.psum(partial_grads, 'nodes')]
    reduce_scatter x1, waiting for transfers between devices: 82.9 us -> 0.01 us  [local(): lax.psum_scatter(lax.dot_general(block_rows, stacked, (((1,), (1,)), ((),...]
    all_to_all x0 -> x3, waiting for transfers between devices: none -> 32.5 us  [the longest x1 20 us: summed_over_nodes(): lax.all_to_all(copies.reshape(rows, width), 'nodes', 0, 0, axis_index_gro...]
    all_to_all x0 -> x3, starting transfers between devices: none -> 23.7 us  [the longest x1 8.26 us: summed_over_nodes(): lax.all_to_all(copies.reshape(rows, width), 'nodes', 0, 0, axis_index_gro...]
    all_to_all x1 -> x0, blocking collectives: 16.4 us -> none  [local(): lax.all_to_all(node_rows, 'heads', split_axis=0, concat_axis=1, tiled=True)]
    ppermute x6 -> x7, starting transfers between devices: 30.9 us -> 36.2 us  [from_partner(): return lax.ppermute(block, axis, route)]
  transfers between devices with their start and end apart: 10 -> 13, of which waited for: 4 -> 5; matrix products, arithmetic and copies ran while one was open for 6% -> 23% of each run, Pallas kernels for 0% -> 0%
where the time goes in v1:
time: 289 us; the launch traced here: 286 us
  waiting for transfers between devices  79 us (27%)
  starting transfers between devices  70.1 us (24%)
  matrix products  55.5 us (19%)
  local copies, waits for them, and re-layouts  50.5 us (17%)
  other arithmetic  16.7 us (6%)
  between operations  14.5 us (5%)
    ppermute x7, starting transfers between devices, from_partner(): return lax.ppermute(block, axis, route)  36.2 us
    all_gather x1, waiting for transfers between devices, local(): lax.all_gather(features, 'heads', axis=0, tiled=True)  32 us
    all_to_all x1, waiting for transfers between devices, summed_over_nodes(): lax.all_to_all(copies.reshape(rows, width), 'nodes', 0, 0, axis_index_gro...  20 us
    dot_general x1, matrix products, local(): jnp.einsum('bhqk,bkhd->bqhd', dscores, back_keys, preferred_element_type=...  18.5 us
    dot_general x1, matrix products, local(): jnp.einsum('bhqk,bqhd->bkhd', dscores, queries, preferred_element_type=jn...  17.9 us
    ppermute x7, waiting for transfers between devices, from_partner(): return lax.ppermute(block, axis, route)  13.8 us
    all_to_all x1, waiting for transfers between devices, summed_over_nodes(): lax.all_to_all(partial.astype(jnp.bfloat16), 'nodes', 0, 0, axis_index_gr...  12.4 us
    all_to_all x1, starting transfers between devices, local(): lax.all_to_all(upstream, 'heads', split_axis=1, concat_axis=0, tiled=True)  10.2 us
  transfers between devices with their start and end apart: 13, of which 5 were waited for; matrix products, arithmetic and copies ran while one was open for 23% of the time, Pallas kernels for 0%

profile of v1, /device:TPU:1, one launch (start us, length us, event | category | flops | bytes accessed | tf_op | source)
XLA Modules:
  0.0 286.3 jit_solution(10321942688165331793)
XLA Ops:
  8.9 10.2 %all-to-all-start.1 = ((bf16[128,8,128]{2,0,1:T(8,128)(2,1)}), bf16[128,8,128]{2,0,1:T(8,128)(2,1)S(1)}, u32[]{:S(2)}, u32[]{:S(2)}) async-start(bf16[128,8,128]{2,0,1:T(8,128)(2,1)} %copy_bitcast_fusion.1), calls=%async_computation.1 | async-start | bytes 524288 | tf_op jit(solution)/shard_map/all_to_all | solution.py:88
  20.8 1.0 constant_dynamic-update-slice_fusion.1
  21.8 1.0 constant_dynamic-update-slice_fusion
  24.3 32.0 %all-gather.2.cloned.1.call-done = bf16[1024,1024]{1,0:T(8,128)(2,1)} async-done(((bf16[128,1024]{1,0:T(8,128)(2,1)}), bf16[1024,1024]{1,0:T(8,128)(2,1)}) %all-gather.2.cloned.1.call-update) | async-done | bytes 2097168 | tf_op jit(solution)/shard_map/all_gather | solution.py:45
  56.3 2.6 fusion.20
  59.3 3.9 %gather_fusion = bf16[1024,384]{1,0:T(8,128)(2,1)S(1)} fusion(bf16[1024,384]{1,0:T(8,128)(2,1)S(1)} %copy.33, s32[1024]{0:T(1024)S(1)} %get-tuple-element.28), kind=kCustom, calls=%fused_computation.6 | custom fusion | bytes 1576960 | tf_op jit(solution)/shard_map/jit(_take)/gather | solution.py:51
  63.5 5.7 %collective-permute-start.2 = (bf16[1024,256]{1,0:T(8,128)(2,1)S(1)}, bf16[1024,256]{1,0:T(8,128)(2,1)}, u32[]{:S(2)}, u32[]{:S(2)}) collective-permute-start(bf16[1024,256]{1,0:T(8,128)(2,1)S(1)} %slice.88), channel_id=1, source_target_pairs={{0,256},{256,0},{8,264},{264,8},{16,272},{272,16},{24,280},{280,24... | collective-permute-start | bytes 1572872 | tf_op jit(solution)/shard_map/ppermute | solution.py:19
  69.1 7.1 %collective-permute-start.1 = (bf16[1024,256]{1,0:T(8,128)(2,1)S(1)}, bf16[1024,256]{1,0:T(8,128)(2,1)S(1)}, u32[]{:S(2)}, u32[]{:S(2)}) collective-permute-start(bf16[1024,256]{1,0:T(8,128)(2,1)S(1)} %slice.88), channel_id=1, source_target_pairs={{0,128},{128,0},{8,136},{136,8},{16,144},{144,16},{24,152},{152,24... | collective-permute-start | bytes 1572872 | tf_op jit(solution)/shard_map/ppermute | solution.py:19
  76.2 3.1 %collective-permute-start = (bf16[1024,256]{1,0:T(8,128)(2,1)S(1)}, bf16[1024,256]{1,0:T(8,128)(2,1)S(1)}, u32[]{:S(2)}, u32[]{:S(2)}) collective-permute-start(bf16[1024,256]{1,0:T(8,128)(2,1)S(1)} %slice.88), channel_id=1, source_target_pairs={{0,8},{8,0},{16,24},{24,16},{32,40},{40,32},{48,56},{56,48},{64,72... | collective-permute-start | bytes 1572872 | tf_op jit(solution)/shard_map/ppermute | solution.py:19
  79.4 3.2 %gather_fusion.1 = bf16[1024,128]{1,0:T(8,128)(2,1)S(1)} fusion(bf16[1024,128]{1,0:T(8,128)(2,1)S(1)} %bitcast.77, s32[1024]{0:T(1024)S(1)} %get-tuple-element.28), kind=kCustom, calls=%fused_computation.7 | custom fusion | bytes 528384 | tf_op jit(solution)/shard_map/jit(_take)/gather | solution.py:89
  84.8 8.9 %collective-permute-done.2 = bf16[1024,256]{1,0:T(8,128)(2,1)} collective-permute-done((bf16[1024,256]{1,0:T(8,128)(2,1)S(1)}, bf16[1024,256]{1,0:T(8,128)(2,1)}, u32[]{:S(2)}, u32[]{:S(2)}) %collective-permute-start.2) | collective-permute-done | bytes 524320 | tf_op jit(solution)/shard_map/ppermute | solution.py:19
  93.7 1.6 gather_fusion.4
  98.6 3.7 %fusion.40 = f32[8,2,128,512]{3,2,1,0:T(8,128)} fusion(bf16[8,512,2,64]{1,3,2,0:T(8,128)(2,1)S(1)} %bitcast.78, bf16[8,128,2,64]{1,0,3,2:T(8,128)(2,1)} %broadcast_select_fusion.4), kind=kOutput, calls=%fused_computation.57 | convolution fusion | flops 134217728 | bytes 5505024 | tf_op jit(solution)/shard_map/bqhd,bkhd->bhqk/dot_general | solution.py:91
  103.2 1.2 exponential_reduce_fusion
  105.2 2.2 fusion.36
  107.4 17.9 %fusion.7 = f32[8,2,64,512]{3,2,1,0:T(8,128)} fusion(bf16[8,128,2,64]{1,3,2,0:T(8,128)(2,1)S(1)} %copy-done.4, f32[8,2,128,512]{3,2,1,0:T(8,128)} %fusion.40, f32[8,2,128,512]{3,2,1,0:T(8,128)} %copy-done.1, f32[8,2,128]{2,1,0:T(2,128)S(1)} %bitcast.96), kind=kOutput, calls=%fused_computation.22 | convolution fusion | flops 143657472 | bytes 10756096 | tf_op jit(solution)/shard_map/bhqk,bqhd->bkhd/dot_general | solution.py:97
  125.3 1.9 copy.48
  127.2 2.9 %copy.47 = f32[8,512,128]{2,1,0:T(8,128)} copy(f32[8,512,128]{1,2,0:T(8,128)} %bitcast.83) | data formatting | bytes 4194304 | tf_op jit(solution)/shard_map/reshape | solution.py:99
  130.1 1.8 fusion.1
  131.9 1.2 fusion.53
  133.1 3.1 %collective-permute-start.3 = (bf16[8,128,256]{2,1,0:T(8,128)(2,1)}, bf16[8,128,256]{2,1,0:T(8,128)(2,1)}, u32[]{:S(2)}, u32[]{:S(2)}) collective-permute-start(bf16[8,128,256]{2,1,0:T(8,128)(2,1)} %get-tuple-element.18), channel_id=1, source_target_pairs={{0,8},{8,0},{16,24},{24,16},{32,40},{40,32},{48,56},{56,48},{64,72... | collective-permute-start | bytes 1572872 | tf_op jit(solution)/shard_map/ppermute | solution.py:19
  136.2 4.7 %collective-permute-start.5 = (bf16[8,128,256]{2,1,0:T(8,128)(2,1)}, bf16[8,128,256]{2,1,0:T(8,128)(2,1)}, u32[]{:S(2)}, u32[]{:S(2)}) collective-permute-start(bf16[8,128,256]{2,1,0:T(8,128)(2,1)} %get-tuple-element.19), channel_id=1, source_target_pairs={{0,256},{256,0},{8,264},{264,8},{16,272},{272,16},{24,280},{280,24... | collective-permute-start | bytes 1572872 | tf_op jit(solution)/shard_map/ppermute | solution.py:19
  140.9 7.3 %collective-permute-start.4 = (bf16[8,128,256]{2,1,0:T(8,128)(2,1)}, bf16[8,128,256]{2,1,0:T(8,128)(2,1)}, u32[]{:S(2)}, u32[]{:S(2)}) collective-permute-start(bf16[8,128,256]{2,1,0:T(8,128)(2,1)} %get-tuple-element.20), channel_id=1, source_target_pairs={{0,128},{128,0},{8,136},{136,8},{16,144},{144,16},{24,152},{152,24... | collective-permute-start | bytes 1572872 | tf_op jit(solution)/shard_map/ppermute | solution.py:19
  148.2 18.5 %fusion.25 = bf16[8,128,2,64]{1,3,2,0:T(8,128)(2,1)} fusion(bf16[8,512,2,64]{1,3,2,0:T(8,128)(2,1)} %bitcast.82, f32[8,2,128,512]{3,2,1,0:T(8,128)} %fusion.40, f32[8,2,128,512]{3,2,1,0:T(8,128)} %copy-done.1, f32[8,2,128]{2,1,0:T(2,128)S(1)} %bitcast.97), kind=kOutput, calls=%fused_computation.37 | convolution fusion | flops 143788544 | bytes 9707520 | tf_op jit(solution)/shard_map/bhqk,bkhd->bqhd/dot_general | solution.py:96
  166.6 1.1 copy.44
  168.5 2.1 convert_element_type.58
  170.7 2.8 gather_fusion.5
  173.5 2.1 convert_element_type.60
  175.6 2.8 gather_fusion.7
  178.5 2.1 convert_element_type.59
  180.6 2.8 gather_fusion.6
  183.5 2.4 fusion.33
  186.3 1.0 pad_maximum_fusion.2
  187.3 1.2 copy.51
  188.5 5.7 %scatter_custom_fusion.1 = bf16[1024,384]{1,0:T(8,128)(2,1)S(1)} fusion(s32[1024]{0:T(1024)S(1)} %get-tuple-element.29, bf16[1024,384]{1,0:T(8,128)(2,1)} %copy.51, bf16[]{:T(256)} %constant.43.clone.1), kind=kCustom, calls=%fused_computation.50 | custom fusion | bytes 786944 | tf_op jit(solution)/shard_map/scatter | solution.py:123
  194.2 3.8 %convolution_convert_fusion = bf16[1024,1024]{1,0:T(8,128)(2,1)} fusion(bf16[1024,384]{1,0:T(8,128)(2,1)S(1)} %scatter_custom_fusion.1, bf16[1024,384]{1,0:T(8,128)(2,1)} %copy-done.5), kind=kOutput, calls=%fused_computation.29 | convolution fusion | flops 806354944 | bytes 3670016 | tf_op jit(solution)/shard_map/dot_general | solution.py:135
  197.9 2.6 fusion.21
  200.5 1.2 copy.52
  201.7 7.7 %all-to-all-start.2 = ((bf16[32,32,384]{2,1,0:T(8,128)(2,1)}), bf16[32,32,384]{2,1,0:T(8,128)(2,1)S(1)}, u32[]{:S(2)}, u32[]{:S(2)}) async-start(bf16[32,32,384]{2,1,0:T(8,128)(2,1)} %bitcast.25), calls=%async_computation.3 | async-start | bytes 1572864 | tf_op jit(solution)/shard_map/all_to_all | solution.py:27
  209.4 3.4 %fusion.28 = bf16[8,128,2,64]{1,3,2,0:T(8,128)(2,1)S(1)} fusion(bf16[8,512,2,64]{1,3,2,0:T(8,128)(2,1)S(1)} %bitcast.79, f32[8,2,128,512]{3,2,1,0:T(8,128)} %copy-done.1, f32[8,2,128]{2,1,0:T(2,128)S(1)} %bitcast.98), kind=kOutput, calls=%fused_computation.38 | convolution fusion | flops 137494528 | bytes 5513216 | tf_op jit(solution)/shard_map/bhqk,bkhd->bqhd/dot_general | solution.py:79
  213.5 3.8 %scatter_custom_fusion = bf16[1024,128]{1,0:T(8,128)(2,1)} fusion(s32[1024]{0:T(1024)S(1)} %get-tuple-element.29, bf16[1024,128]{1,0:T(8,128)(2,1)S(1)} %reshape.216, bf16[]{:T(256)} %constant.43.clone.1), kind=kCustom, calls=%fused_computation.59 | custom fusion | bytes 262146 | tf_op jit(solution)/shard_map/scatter | solution.py:85
  217.3 12.4 %all-to-all-done.2 = bf16[32,32,384]{2,1,0:T(8,128)(2,1)S(1)} async-done(((bf16[32,32,384]{2,1,0:T(8,128)(2,1)}), bf16[32,32,384]{2,1,0:T(8,128)(2,1)S(1)}, u32[]{:S(2)}, u32[]{:S(2)}) %all-to-all-start.2) | async-done | bytes 786464 | tf_op jit(solution)/shard_map/all_to_all | solution.py:27
  229.7 7.8 %all-to-all-start = ((bf16[8,128,128]{2,1,0:T(8,128)(2,1)}), bf16[8,128,128]{2,1,0:T(8,128)(2,1)S(1)}, u32[]{:S(2)}, u32[]{:S(2)}) async-start(bf16[8,128,128]{2,1,0:T(8,128)(2,1)} %bitcast.11), calls=%async_computation | async-start | bytes 524288 | tf_op jit(solution)/shard_map/all_to_all | solution.py:87
  237.6 5.2 %collective-permute-start.6 = (f32[32,384]{1,0:T(8,128)S(1)}, f32[32,384]{1,0:T(8,128)S(1)}, u32[]{:S(2)}, u32[]{:S(2)}) collective-permute-start(f32[32,384]{1,0:T(8,128)S(1)} %convert_reduce_fusion), channel_id=1, source_target_pairs={{0,256},{256,0},{8,264},{264,8},{16,272},{272,16},{24,280},{280,24... | collective-permute-start | bytes 147464 | tf_op jit(solution)/shard_map/ppermute | solution.py:19
  242.9 4.8 %collective-permute-done.6 = f32[32,384]{1,0:T(8,128)S(1)} collective-permute-done((f32[32,384]{1,0:T(8,128)S(1)}, f32[32,384]{1,0:T(8,128)S(1)}, u32[]{:S(2)}, u32[]{:S(2)}) %collective-permute-start.6) | collective-permute-done | bytes 49184 | tf_op jit(solution)/shard_map/ppermute | solution.py:19
  248.7 8.3 %all-to-all-start.3 = ((bf16[32,32,384]{2,1,0:T(8,128)(2,1)}), bf16[32,32,384]{2,1,0:T(8,128)(2,1)S(1)}, u32[]{:S(2)}, u32[]{:S(2)}) async-start(bf16[32,32,384]{2,1,0:T(8,128)(2,1)} %broadcast_in_dim.67), calls=%async_computation.4 | async-start | bytes 1572864 | tf_op jit(solution)/shard_map/all_to_all | solution.py:33
  258.0 20.0 %all-to-all-done.3 = bf16[32,32,384]{2,1,0:T(8,128)(2,1)S(1)} async-done(((bf16[32,32,384]{2,1,0:T(8,128)(2,1)}), bf16[32,32,384]{2,1,0:T(8,128)(2,1)S(1)}, u32[]{:S(2)}, u32[]{:S(2)}) %all-to-all-start.3) | async-done | bytes 786464 | tf_op jit(solution)/shard_map/all_to_all | solution.py:33
  278.2 1.2 fusion.55
  (67 shorter events, 16.5 us)
Async XLA Ops:
  7.2 1.0 copy-start
  7.2 49.1 %all-gather.2.cloned.1.call-start = ((), (), s32[]{:S(2)}) async-start(), calls=%async_computation.5 | async-start | bytes 2359296 | tf_op jit(solution)/shard_map/all_gather | solution.py:45
  8.9 70.5 %all-to-all-start.1 = ((bf16[128,8,128]{2,0,1:T(8,128)(2,1)}), bf16[128,8,128]{2,0,1:T(8,128)(2,1)S(1)}, u32[]{:S(2)}, u32[]{:S(2)}) async-start(bf16[128,8,128]{2,0,1:T(8,128)(2,1)} %copy_bitcast_fusion.1), calls=%async_computation.1 | async-start | bytes 524288 | tf_op jit(solution)/shard_map/all_to_all | solution.py:88
  19.1 260.3 %reduce-scatter.2.cloned.1.call-start = ((), (), s32[]{:S(2)}) async-start(), calls=%async_computation.6 | async-start | bytes 2359296 | tf_op jit(solution)/shard_map/reduce_scatter | solution.py:134
  22.8 33.5 %copy-start.5 = (bf16[1024,384]{1,0:T(8,128)(2,1)}, bf16[1024,384]{1,0:T(8,128)(2,1)S(1)}, u32[]{:S(2)}) copy-start(bf16[1024,384]{1,0:T(8,128)(2,1)S(1)} %constant_dynamic-update-slice_fusion) | copy-start | bytes 2359300
  59.3 20.1 %copy-start.6 = (s32[1024]{0:T(1024)S(1)}, s32[1024]{0:T(1024)}, u32[]{:S(2)}) copy-start(s32[1024]{0:T(1024)} %param.12) | copy-start | bytes 12292
  63.5 30.3 %collective-permute-start.2 = (bf16[1024,256]{1,0:T(8,128)(2,1)S(1)}, bf16[1024,256]{1,0:T(8,128)(2,1)}, u32[]{:S(2)}, u32[]{:S(2)}) collective-permute-start(bf16[1024,256]{1,0:T(8,128)(2,1)S(1)} %slice.88), channel_id=1, source_target_pairs={{0,256},{256,0},{8,264},{264,8},{16,272},{272,16},{24,280},{280,24... | collective-permute-start | bytes 1572872 | tf_op jit(solution)/shard_map/ppermute | solution.py:19
  69.1 26.2 %collective-permute-start.1 = (bf16[1024,256]{1,0:T(8,128)(2,1)S(1)}, bf16[1024,256]{1,0:T(8,128)(2,1)S(1)}, u32[]{:S(2)}, u32[]{:S(2)}) collective-permute-start(bf16[1024,256]{1,0:T(8,128)(2,1)S(1)} %slice.88), channel_id=1, source_target_pairs={{0,128},{128,0},{8,136},{136,8},{16,144},{144,16},{24,152},{152,24... | collective-permute-start | bytes 1572872 | tf_op jit(solution)/shard_map/ppermute | solution.py:19
  76.2 19.7 %collective-permute-start = (bf16[1024,256]{1,0:T(8,128)(2,1)S(1)}, bf16[1024,256]{1,0:T(8,128)(2,1)S(1)}, u32[]{:S(2)}, u32[]{:S(2)}) collective-permute-start(bf16[1024,256]{1,0:T(8,128)(2,1)S(1)} %slice.88), channel_id=1, source_target_pairs={{0,8},{8,0},{16,24},{24,16},{32,40},{40,32},{48,56},{56,48},{64,72... | collective-permute-start | bytes 1572872 | tf_op jit(solution)/shard_map/ppermute | solution.py:19
  98.1 5.1 %copy-start.2 = (bf16[8,512,128]{1,2,0:T(8,128)(2,1)}, bf16[8,512,128]{1,2,0:T(8,128)(2,1)S(1)}, u32[]{:S(2)}) copy-start(bf16[8,512,128]{1,2,0:T(8,128)(2,1)S(1)} %copy.36) | copy-start | bytes 3145732
  98.6 3.7 %copy-start.4 = (bf16[8,128,2,64]{1,3,2,0:T(8,128)(2,1)S(1)}, bf16[8,128,2,64]{1,3,2,0:T(8,128)(2,1)}, u32[]{:S(2)}) copy-start(bf16[8,128,2,64]{1,3,2,0:T(8,128)(2,1)} %copy.37) | copy-start | bytes 786436
  102.4 2.8 copy-start.3
  103.2 1.9 copy-start.1
  133.1 35.4 %collective-permute-start.3 = (bf16[8,128,256]{2,1,0:T(8,128)(2,1)}, bf16[8,128,256]{2,1,0:T(8,128)(2,1)}, u32[]{:S(2)}, u32[]{:S(2)}) collective-permute-start(bf16[8,128,256]{2,1,0:T(8,128)(2,1)} %get-tuple-element.18), channel_id=1, source_target_pairs={{0,8},{8,0},{16,24},{24,16},{32,40},{40,32},{48,56},{56,48},{64,72... | collective-permute-start | bytes 1572872 | tf_op jit(solution)/shard_map/ppermute | solution.py:19
  136.2 37.3 %collective-permute-start.5 = (bf16[8,128,256]{2,1,0:T(8,128)(2,1)}, bf16[8,128,256]{2,1,0:T(8,128)(2,1)}, u32[]{:S(2)}, u32[]{:S(2)}) collective-permute-start(bf16[8,128,256]{2,1,0:T(8,128)(2,1)} %get-tuple-element.19), channel_id=1, source_target_pairs={{0,256},{256,0},{8,264},{264,8},{16,272},{272,16},{24,280},{280,24... | collective-permute-start | bytes 1572872 | tf_op jit(solution)/shard_map/ppermute | solution.py:19
  140.9 37.6 %collective-permute-start.4 = (bf16[8,128,256]{2,1,0:T(8,128)(2,1)}, bf16[8,128,256]{2,1,0:T(8,128)(2,1)}, u32[]{:S(2)}, u32[]{:S(2)}) collective-permute-start(bf16[8,128,256]{2,1,0:T(8,128)(2,1)} %get-tuple-element.20), channel_id=1, source_target_pairs={{0,128},{128,0},{8,136},{136,8},{16,144},{144,16},{24,152},{152,24... | collective-permute-start | bytes 1572872 | tf_op jit(solution)/shard_map/ppermute | solution.py:19
  201.7 28.0 %all-to-all-start.2 = ((bf16[32,32,384]{2,1,0:T(8,128)(2,1)}), bf16[32,32,384]{2,1,0:T(8,128)(2,1)S(1)}, u32[]{:S(2)}, u32[]{:S(2)}) async-start(bf16[32,32,384]{2,1,0:T(8,128)(2,1)} %bitcast.25), calls=%async_computation.3 | async-start | bytes 1572864 | tf_op jit(solution)/shard_map/all_to_all | solution.py:27
  229.7 18.0 %all-to-all-start = ((bf16[8,128,128]{2,1,0:T(8,128)(2,1)}), bf16[8,128,128]{2,1,0:T(8,128)(2,1)S(1)}, u32[]{:S(2)}, u32[]{:S(2)}) async-start(bf16[8,128,128]{2,1,0:T(8,128)(2,1)} %bitcast.11), calls=%async_computation | async-start | bytes 524288 | tf_op jit(solution)/shard_map/all_to_all | solution.py:87
  237.6 10.1 %collective-permute-start.6 = (f32[32,384]{1,0:T(8,128)S(1)}, f32[32,384]{1,0:T(8,128)S(1)}, u32[]{:S(2)}, u32[]{:S(2)}) collective-permute-start(f32[32,384]{1,0:T(8,128)S(1)} %convert_reduce_fusion), channel_id=1, source_target_pairs={{0,256},{256,0},{8,264},{264,8},{16,272},{272,16},{24,280},{280,24... | collective-permute-start | bytes 147464 | tf_op jit(solution)/shard_map/ppermute | solution.py:19
  248.7 29.3 %all-to-all-start.3 = ((bf16[32,32,384]{2,1,0:T(8,128)(2,1)}), bf16[32,32,384]{2,1,0:T(8,128)(2,1)S(1)}, u32[]{:S(2)}, u32[]{:S(2)}) async-start(bf16[32,32,384]{2,1,0:T(8,128)(2,1)} %broadcast_in_dim.67), calls=%async_computation.4 | async-start | bytes 1572864 | tf_op jit(solution)/shard_map/all_to_all | solution.py:33
Sparse Core Ops, SparseCore 0:
  10.1 46.1 all-gather.1
  198.1 40.2 reduce-scatter.1

commit v2 on v1

v2 whole, which is shorter than its diff:
```python
import functools
import math

import jax
import jax.numpy as jnp
from jax import lax
from jax.experimental import pallas as pl
from jax.experimental.pallas import tpu as pltpu
from jax.sharding import PartitionSpec as P

HDIM = 64
BLOCK = 128
BF = jnp.bfloat16
F32 = jnp.float32
NN = (((1,), (0,)), ((), ()))
NT = (((1,), (1,)), ((), ()))
TN = (((0,), (0,)), ((), ()))
VMEM = pl.BlockSpec(memory_space=pltpu.VMEM)
SMEM = pl.BlockSpec(memory_space=pltpu.SMEM)


def mm(a, b, dims):
    return lax.dot_general(a, b, dims, preferred_element_type=F32)


def from_partner(block, axis, bit):
    count = lax.axis_size(axis)
    route = []
    for low in range(count):
        high = low | 1 << bit
        if high != low and high < count:
            route += [(low, high), (high, low)]
    return lax.ppermute(block, axis, route)


def summed_over_nodes(partial):
    count = lax.axis_size("nodes")
    half = count // 2
    groups = [list(range(half)), list(range(half, count))]
    rows, width = partial.shape
    spread = lax.all_to_all(partial, "nodes", 0, 0, axis_index_groups=groups, tiled=True)
    share = jnp.sum(spread.reshape(half, rows // half, width).astype(F32), axis=0)
    share = share + from_partner(share, "nodes", half.bit_length() - 1)
    copies = jnp.broadcast_to(share.astype(BF)[None], (half, rows // half, width))
    whole = lax.all_to_all(
        copies.reshape(rows, width), "nodes", 0, 0, axis_index_groups=groups, tiled=True
    )
    return whole.astype(F32)


def picks(order_column):
    count = order_column.shape[0]
    node = lax.broadcasted_iota(jnp.int32, (count, count), 1)
    return jnp.where(node == order_column, 1.0, 0.0).astype(BF)


def project_kernel(features, weights, order_column, upstream, queries, pairs, incoming):
    width = queries.shape[1]
    pick = picks(order_column[...])
    projected = mm(features[...], weights[...], NN).astype(BF)
    ordered = mm(pick, projected, NN).astype(BF)
    queries[...] = ordered[:, :width]
    pairs[...] = ordered[:, width:]
    incoming[...] = mm(pick, upstream[...], NN).astype(BF)


def attend_kernel(
    slots,
    queries,
    own,
    first,
    second,
    third,
    incoming,
    order_row,
    mixed_nodes,
    dquery,
    own_grads,
    first_grads,
    second_grads,
    third_grads,
    mixed,
):
    rows, width = queries.shape
    score_scale = 1.0 / math.sqrt(HDIM)
    lane = lax.broadcasted_iota(jnp.int32, (BLOCK, width), 1)
    heads = width // HDIM

    def split_heads(block):
        zero = jnp.zeros_like(block)
        return jnp.concatenate(
            [jnp.where(lane // HDIM == head, block, zero) for head in range(heads)], axis=0
        )

    def join_heads(stacked):
        joined = stacked[:BLOCK]
        for head in range(1, heads):
            joined = jnp.where(
                lane // HDIM == head, stacked[head * BLOCK : (head + 1) * BLOCK], joined
            )
        return joined

    def one_block(block, carry):
        here = pl.ds(pl.multiple_of(block * BLOCK, BLOCK), BLOCK)
        places = [here] + [
            pl.ds(pl.multiple_of(slots[which, block] * BLOCK, BLOCK), BLOCK) for which in range(3)
        ]
        sources = (own, first, second, third)
        pairs = [source[place, :] for source, place in zip(sources, places)]
        keys = jnp.concatenate([pair[:, :width] for pair in pairs], axis=0)
        values = jnp.concatenate([pair[:, width:] for pair in pairs], axis=0)
        query = split_heads(queries[here, :])
        cotangent = split_heads(incoming[here, :])
        scores = mm(query, keys, NT) * score_scale
        peak = jnp.max(scores, axis=-1, keepdims=True)
        raised = jnp.exp(scores - peak)
        softmax = raised / jnp.sum(raised, axis=-1, keepdims=True)
        weights_low = softmax.astype(BF)
        mixed[here, :] = join_heads(mm(weights_low, values, NN)).astype(BF)
        dprobs = mm(cotangent, values, NT)
        row_delta = jnp.sum(softmax * dprobs, axis=-1, keepdims=True)
        dscores = (softmax * (dprobs - row_delta) * score_scale).astype(BF)
        dquery[here, :] = join_heads(mm(dscores, keys, NN)).astype(BF)
        dkeys = mm(dscores, query, TN)
        dvalues = mm(weights_low, cotangent, TN)
        targets = (own_grads, first_grads, second_grads, third_grads)
        for which in range(4):
            part = slice(which * BLOCK, (which + 1) * BLOCK)
            targets[which][places[which], :width] = dkeys[part].astype(targets[which].dtype)
            targets[which][places[which], width:] = dvalues[part].astype(targets[which].dtype)
        return carry

    lax.fori_loop(0, rows // BLOCK, one_block, 0)
    node = lax.broadcasted_iota(jnp.int32, (rows, rows), 0)
    place = jnp.where(node == order_row[...], 1.0, 0.0).astype(BF)
    mixed_nodes[...] = mm(place, mixed[...], NN).astype(BF)


def finish_kernel(
    features, weights, order_row, dquery, own, first, second, third, weight_part, feature_part
):
    rows, width = dquery.shape
    total = own[...]
    for other in (first, second, third):
        total = total + other[...].astype(F32)
    grad_rows = jnp.concatenate([dquery[...], total.astype(BF)], axis=1)
    node = lax.broadcasted_iota(jnp.int32, (rows, rows), 0)
    place = jnp.where(node == order_row[...], 1.0, 0.0).astype(BF)
    grad_nodes = mm(place, grad_rows, NN).astype(BF)
    weight_part[...] = mm(features[...], grad_nodes, TN).astype(BF)
    feature_part[...] = mm(grad_nodes, weights[...], NT).astype(BF)


def local(features, node_order, partners, query_weight, key_weight, value_weight, upstream):
    width = query_weight.shape[1]
    stacked = jnp.concatenate([query_weight, key_weight, value_weight], axis=1)
    rows = node_order.shape[0]
    blocks = rows // BLOCK
    slots = partners % blocks
    order_column = node_order.reshape(rows, 1)
    order_row = node_order.reshape(1, rows)
    levels = lax.axis_size("nodes").bit_length() - 1
    swap_bits = (0, levels - 2, levels - 1)
    params = pltpu.CompilerParams(vmem_limit_bytes=48 * 1024 * 1024)

    arriving = lax.all_to_all(upstream, "heads", split_axis=1, concat_axis=0, tiled=True)
    gathered = lax.all_gather(features, "heads", axis=0, tiled=True)
    queries, pairs, incoming = pl.pallas_call(
        project_kernel,
        out_shape=(
            jax.ShapeDtypeStruct((rows, width), BF),
            jax.ShapeDtypeStruct((rows, 2 * width), BF),
            jax.ShapeDtypeStruct((rows, width), BF),
        ),
        in_specs=[VMEM] * 4,
        out_specs=(VMEM,) * 3,
        compiler_params=params,
        name="project",
    )(gathered, stacked, order_column, arriving)
    others = [from_partner(pairs, "nodes", bit) for bit in swap_bits]
    mixed_nodes, dquery, own_grads, *sent = pl.pallas_call(
        attend_kernel,
        out_shape=(
            jax.ShapeDtypeStruct((rows, width), BF),
            jax.ShapeDtypeStruct((rows, width), BF),
            jax.ShapeDtypeStruct((rows, 2 * width), F32),
            jax.ShapeDtypeStruct((rows, 2 * width), BF),
            jax.ShapeDtypeStruct((rows, 2 * width), BF),
            jax.ShapeDtypeStruct((rows, 2 * width), BF),
        ),
        in_specs=[SMEM] + [VMEM] * 7,
        out_specs=(VMEM,) * 6,
        scratch_shapes=[pltpu.VMEM((rows, width), BF)],
        compiler_params=params,
        name="attend",
    )(slots, queries, pairs, *others, incoming, order_row)
    returned = [from_partner(part, "nodes", bit) for part, bit in zip(sent, swap_bits)]
    attended = lax.all_to_all(mixed_nodes, "heads", split_axis=0, concat_axis=1, tiled=True)
    weight_part, feature_part = pl.pallas_call(
        finish_kernel,
        out_shape=(
            jax.ShapeDtypeStruct((stacked.shape[0], 3 * width), BF),
            jax.ShapeDtypeStruct((rows, stacked.shape[0]), BF),
        ),
        in_specs=[VMEM] * 8,
        out_specs=(VMEM,) * 2,
        compiler_params=params,
        name="finish",
    )(gathered, stacked, order_row, dquery, own_grads, *returned)
    feature_grad = lax.psum_scatter(feature_part, "heads", scatter_dimension=0, tiled=True)
    weight_grads = summed_over_nodes(weight_part)
    return (
        attended,
        feature_grad,
        weight_grads[:, :width],
        weight_grads[:, width : 2 * width],
        weight_grads[:, 2 * width :],
    )


def solution(mesh):
    return jax.shard_map(
        local,
        mesh=mesh,
        in_specs=(
            P(("nodes", "heads"), None),
            P("nodes"),
            P(None, "nodes"),
            P(None, "heads"),
            P(None, "heads"),
            P(None, "heads"),
            P(("nodes", "heads"), None),
        ),
        out_specs=(
            P(("nodes", "heads"), None),
            P(("nodes", "heads"), None),
            P(None, "heads"),
            P(None, "heads"),
            P(None, "heads"),
        ),
        check_vma=False,
    )
```

time: 289 us -> 237 us (0.82)
  matrix products: 55.5 us -> 0 us
  blocking collectives: 0 us -> 44.5 us
  local copies, waits for them, and re-layouts: 50.5 us -> 6.48 us
  Pallas kernels: 0 us -> 20 us
  other arithmetic: 16.7 us -> 0.32 us
  waiting for transfers between devices: 79 us -> 90.4 us
  starting transfers between devices: 70.1 us -> 59.1 us
    dot_general x9 -> x0, matrix products: 55.5 us -> none  [the longest x1 18.5 us: local(): jnp.einsum('bhqk,bkhd->bqhd', dscores, back_keys, preferred_element_type=...]
    all_to_all x0 -> x1, blocking collectives: none -> 44.5 us  [summed_over_nodes(): lax.all_to_all(partial, 'nodes', 0, 0, axis_index_groups=groups, tiled=True)]
    pallas_call x0 -> x3, Pallas kernels: none -> 20 us  [the longest x1 10.7 us: local(): pl.pallas_call(attend_kernel, out_shape=(jax.ShapeDtypeStruct((rows, widt...]
    ppermute x7, waiting for transfers between devices: 13.8 us -> 33.3 us  [from_partner(): return lax.ppermute(block, axis, route)]
    gather x9 -> x0, local copies, waits for them, and re-layouts: 18.5 us -> none  [the longest x3 8.5 us: local(): returned = returned + jnp.take(arrived, partner_slots[matching], axis=0)]
    all_to_all x2 -> x1, waiting for transfers between devices: 12.4 us -> 0.01 us  [local(): lax.all_to_all(mixed_nodes, 'heads', split_axis=0, concat_axis=1, tiled=T...]
    scatter x2 -> x0, local copies, waits for them, and re-layouts: 9.48 us -> none  [the longest x1 5.65 us: local(): jnp.zeros((group_rows, 3 * local_width), jnp.bfloat16).at[node_order]]
    all_to_all x2 -> x1, starting transfers between devices: 15.4 us -> 6.14 us  [local(): lax.all_to_all(mixed_nodes, 'heads', split_axis=0, concat_axis=1, tiled=T...]
  transfers between devices with their start and end apart: 13 -> 12, of which waited for: 5 -> 7; matrix products, arithmetic and copies ran while one was open for 23% -> 2% of each run, Pallas kernels for 0% -> 0%
where the time goes in v2:
time: 237 us; the launch traced here: 235 us
  waiting for transfers between devices  90.4 us (38%)
  starting transfers between devices  59.1 us (25%)
  blocking collectives  44.5 us (19%)
  Pallas kernels  20 us (8%)
  between operations  14.2 us (6%)
  local copies, waits for them, and re-layouts  6.48 us (3%)
    all_to_all x1, blocking collectives, summed_over_nodes(): lax.all_to_all(partial, 'nodes', 0, 0, axis_index_groups=groups, tiled=True)  44.5 us
    ppermute x7, starting transfers between devices, from_partner(): return lax.ppermute(block, axis, route)  34.9 us
    ppermute x7, waiting for transfers between devices, from_partner(): return lax.ppermute(block, axis, route)  33.3 us
    all_gather x1, waiting for transfers between devices, local(): gathered = lax.all_gather(features, 'heads', axis=0, tiled=True)  28.5 us
    all_to_all x1, waiting for transfers between devices, summed_over_nodes(): lax.all_to_all(copies.reshape(rows, width), 'nodes', 0, 0, axis_index_gro...  20.3 us
    pallas_call x1, Pallas kernels, local(): pl.pallas_call(attend_kernel, out_shape=(jax.ShapeDtypeStruct((rows, widt...  10.7 us
    all_to_all x1, starting transfers between devices, local(): lax.all_to_all(upstream, 'heads', split_axis=1, concat_axis=0, tiled=True)  10.2 us
    all_to_all x1, starting transfers between devices, summed_over_nodes(): lax.all_to_all(copies.reshape(rows, width), 'nodes', 0, 0, axis_index_gro...  7.81 us
  transfers between devices with their start and end apart: 12, of which 7 were waited for; matrix products, arithmetic and copies ran while one was open for 2% of the time, Pallas kernels for 0%

profile of v2, /device:TPU:1, one launch (start us, length us, event | category | flops | bytes accessed | tf_op | source)
XLA Modules:
  0.0 235.0 jit_solution(1950898468338281705)
XLA Ops:
  7.2 0.0 copy-start
  7.2 0.0 copy-start.3
  7.2 0.0 copy-start.4
  7.2 0.0 copy-start.5
  7.2 0.0 all-gather.2.cloned.1.call-start
  7.3 0.7 all-gather.2.cloned.1.call-update
  7.9 0.2 copy-done
  8.1 0.8 copy_bitcast_fusion.1
  8.9 10.2 %all-to-all-start = ((bf16[128,8,128]{2,0,1:T(8,128)(2,1)}), bf16[128,8,128]{2,0,1:T(8,128)(2,1)S(1)}, u32[]{:S(2)}, u32[]{:S(2)}) async-start(bf16[128,8,128]{2,0,1:T(8,128)(2,1)} %copy_bitcast_fusion.1), calls=%async_computation | async-start | bytes 524288 | tf_op jit(solution)/shard_map/all_to_all | solution.py:166
  19.1 0.0 reduce-scatter.2.cloned.1.call-start
  19.1 0.9 copy.15.order_column
  20.0 0.0 copy-done.3
  20.0 0.0 copy-done.4
  20.1 0.1 constant_dynamic-update-slice_fusion.1
  20.1 0.0 copy-done.5
  20.1 0.1 constant_dynamic-update-slice_fusion.weights
  20.2 7.6 %all-to-all-done = bf16[128,8,128]{2,0,1:T(8,128)(2,1)S(1)} async-done(((bf16[128,8,128]{2,0,1:T(8,128)(2,1)}), bf16[128,8,128]{2,0,1:T(8,128)(2,1)S(1)}, u32[]{:S(2)}, u32[]{:S(2)}) %all-to-all-start) | async-done | bytes 262176 | tf_op jit(solution)/shard_map/all_to_all | solution.py:166
  27.8 28.5 %all-gather.2.cloned.1.call-done.features = bf16[1024,1024]{1,0:T(8,128)(2,1)} async-done(((bf16[128,1024]{1,0:T(8,128)(2,1)}), bf16[1024,1024]{1,0:T(8,128)(2,1)}) %all-gather.2.cloned.1.call-update) | async-done | bytes 2097168 | tf_op jit(solution)/shard_map/all_gather | solution.py:167
  56.3 1.6 copy-done.1
  57.9 2.9 %project.1 = (bf16[1024,128]{1,0:T(8,128)(2,1)S(1)}, bf16[1024,256]{1,0:T(8,128)(2,1)S(1)}, bf16[1024,128]{1,0:T(8,128)(2,1)S(1)}) custom-call(bf16[1024,1024]{1,0:T(8,128)(2,1)S(1)} %copy-done.1, bf16[1024,384]{1,0:T(8,128)(2,1)S(1)} %constant_dynamic-update-slice_fusion.weights, s32[1024,1]{1,0:T(8,128)S(1)} %copy.15.order_column, ...), custom_call_target="tpu_custom_call" | custom-call | tf_op jit(solution)/shard_map/project/pallas_call | solution.py:168
  60.8 5.7 %collective-permute-start.2 = (bf16[1024,256]{1,0:T(8,128)(2,1)S(1)}, bf16[1024,256]{1,0:T(8,128)(2,1)S(1)}, u32[]{:S(2)}, u32[]{:S(2)}) collective-permute-start(bf16[1024,256]{1,0:T(8,128)(2,1)S(1)} %get-tuple-element.17.own), channel_id=1, source_target_pairs={{0,256},{256,0},{8,264},{264,8},{16,272},{272,16},{24,280},{280,24... | collective-permute-start | bytes 1572872 | tf_op jit(solution)/shard_map/ppermute | solution.py:33
  66.5 7.1 %collective-permute-start.1 = (bf16[1024,256]{1,0:T(8,128)(2,1)S(1)}, bf16[1024,256]{1,0:T(8,128)(2,1)S(1)}, u32[]{:S(2)}, u32[]{:S(2)}) collective-permute-start(bf16[1024,256]{1,0:T(8,128)(2,1)S(1)} %get-tuple-element.17.own), channel_id=1, source_target_pairs={{0,128},{128,0},{8,136},{136,8},{16,144},{144,16},{24,152},{152,24... | collective-permute-start | bytes 1572872 | tf_op jit(solution)/shard_map/ppermute | solution.py:33
  73.5 3.1 %collective-permute-start = (bf16[1024,256]{1,0:T(8,128)(2,1)S(1)}, bf16[1024,256]{1,0:T(8,128)(2,1)S(1)}, u32[]{:S(2)}, u32[]{:S(2)}) collective-permute-start(bf16[1024,256]{1,0:T(8,128)(2,1)S(1)} %get-tuple-element.17.own), channel_id=1, source_target_pairs={{0,8},{8,0},{16,24},{24,16},{32,40},{40,32},{48,56},{56,48},{64,72... | collective-permute-start | bytes 1572872 | tf_op jit(solution)/shard_map/ppermute | solution.py:33
  76.7 0.0 copy-done.6
  76.7 14.2 %collective-permute-done.2.third = bf16[1024,256]{1,0:T(8,128)(2,1)S(1)} collective-permute-done((bf16[1024,256]{1,0:T(8,128)(2,1)S(1)}, bf16[1024,256]{1,0:T(8,128)(2,1)S(1)}, u32[]{:S(2)}, u32[]{:S(2)}) %collective-permute-start.2) | collective-permute-done | bytes 524320 | tf_op jit(solution)/shard_map/ppermute | solution.py:33
  90.9 0.0 collective-permute-done.1.second
  90.9 0.0 collective-permute-done.first
  91.0 10.7 %attend.1 = (bf16[1024,128]{1,0:T(8,128)(2,1)}, bf16[1024,128]{1,0:T(8,128)(2,1)S(1)}, f32[1024,256]{1,0:T(8,128)S(1)}, bf16[1024,256]{1,0:T(8,128)(2,1)S(1)}, b...) custom-call(s32[3,8]{1,0:T(4,128)S(1)} %add_select_fusion.slots, ...), custom_call_target="tpu_custom_call" | custom-call | tf_op jit(solution)/shard_map/attend/pallas_call | solution.py:181
  101.7 3.1 %collective-permute-start.3 = (bf16[1024,256]{1,0:T(8,128)(2,1)S(1)}, bf16[1024,256]{1,0:T(8,128)(2,1)S(1)}, u32[]{:S(2)}, u32[]{:S(2)}) collective-permute-start(bf16[1024,256]{1,0:T(8,128)(2,1)S(1)} %get-tuple-element.22), channel_id=1, source_target_pairs={{0,8},{8,0},{16,24},{24,16},{32,40},{40,32},{48,56},{56,48},{64,72... | collective-permute-start | bytes 1572872 | tf_op jit(solution)/shard_map/ppermute | solution.py:33
  104.8 7.1 %collective-permute-start.4 = (bf16[1024,256]{1,0:T(8,128)(2,1)S(1)}, bf16[1024,256]{1,0:T(8,128)(2,1)S(1)}, u32[]{:S(2)}, u32[]{:S(2)}) collective-permute-start(bf16[1024,256]{1,0:T(8,128)(2,1)S(1)} %get-tuple-element.23), channel_id=1, source_target_pairs={{0,128},{128,0},{8,136},{136,8},{16,144},{144,16},{24,152},{152,24... | collective-permute-start | bytes 1572872 | tf_op jit(solution)/shard_map/ppermute | solution.py:33
  111.9 4.7 %collective-permute-start.5 = (bf16[1024,256]{1,0:T(8,128)(2,1)S(1)}, bf16[1024,256]{1,0:T(8,128)(2,1)S(1)}, u32[]{:S(2)}, u32[]{:S(2)}) collective-permute-start(bf16[1024,256]{1,0:T(8,128)(2,1)S(1)} %get-tuple-element.24), channel_id=1, source_target_pairs={{0,256},{256,0},{8,264},{264,8},{16,272},{272,16},{24,280},{280,24... | collective-permute-start | bytes 1572872 | tf_op jit(solution)/shard_map/ppermute | solution.py:33
  116.6 0.0 collective-permute-done.3.first
  116.6 2.0 collective-permute-done.4.second
  118.6 10.2 %collective-permute-done.5.third = bf16[1024,256]{1,0:T(8,128)(2,1)S(1)} collective-permute-done((bf16[1024,256]{1,0:T(8,128)(2,1)S(1)}, bf16[1024,256]{1,0:T(8,128)(2,1)S(1)}, u32[]{:S(2)}, u32[]{:S(2)}) %collective-permute-start.5) | collective-permute-done | bytes 524320 | tf_op jit(solution)/shard_map/ppermute | solution.py:33
  128.8 6.4 %finish.1 = (bf16[1024,384]{1,0:T(8,128)(2,1)S(1)}, bf16[1024,1024]{1,0:T(8,128)(2,1)}) custom-call(bf16[1024,1024]{1,0:T(8,128)(2,1)} %all-gather.2.cloned.1.call-done.features, bf16[1024,384]{1,0:T(8,128)(2,1)S(1)} %constant_dynamic-update-slice_fusion.weights, s32[1,1024]{1,0:T(1,128)S(1)} %bitcast.25, bf16[1024,128]{1,0:T(8,128)(2,1)S(1)} %get-tuple-element.20.dquery, ...), custom_call_target="tpu_custom_call" | custom-call | tf_op jit(solution)/shard_map/finish/pallas_call | solution.py:199
  135.2 0.0 reduce-scatter.2.cloned.1.call-update
  135.2 44.5 %all_to_all.53 = bf16[32,32,384]{2,1,0:T(8,128)(2,1)S(1)} all-to-all(bf16[32,32,384]{2,1,0:T(8,128)(2,1)S(1)} %bitcast.22), channel_id=1, replica_groups={{0,8,16,24,32,40,48,56,64,72,80,88,96,104,112,120,128,136,144,152,160,1..., dimensions={0} | all-to-all | bytes 1572864 | tf_op jit(solution)/shard_map/all_to_all | solution.py:41
  179.7 6.1 %all-to-all-start.1 = ((bf16[8,128,128]{2,1,0:T(8,128)(2,1)}), bf16[8,128,128]{2,1,0:T(8,128)(2,1)S(1)}, u32[]{:S(2)}, u32[]{:S(2)}) async-start(bf16[8,128,128]{2,1,0:T(8,128)(2,1)} %bitcast.4), calls=%async_computation.1 | async-start | bytes 524288 | tf_op jit(solution)/shard_map/all_to_all | solution.py:198
  185.9 0.1 convert_reduce_fusion
  186.0 4.2 %collective-permute-start.6 = (f32[32,384]{1,0:T(8,128)S(1)}, f32[32,384]{1,0:T(8,128)S(1)}, u32[]{:S(2)}, u32[]{:S(2)}) collective-permute-start(f32[32,384]{1,0:T(8,128)S(1)} %convert_reduce_fusion), channel_id=1, source_target_pairs={{0,256},{256,0},{8,264},{264,8},{16,272},{272,16},{24,280},{280,24... | collective-permute-start | bytes 147464 | tf_op jit(solution)/shard_map/ppermute | solution.py:33
  190.2 6.8 %collective-permute-done.6 = f32[32,384]{1,0:T(8,128)S(1)} collective-permute-done((f32[32,384]{1,0:T(8,128)S(1)}, f32[32,384]{1,0:T(8,128)S(1)}, u32[]{:S(2)}, u32[]{:S(2)}) %collective-permute-start.6) | collective-permute-done | bytes 49184 | tf_op jit(solution)/shard_map/ppermute | solution.py:33
  197.0 0.0 all-to-all-done.1
  197.0 0.9 broadcast_in_dim.2
  198.0 7.8 %all-to-all-start.3 = ((bf16[32,32,384]{2,1,0:T(8,128)(2,1)}), bf16[32,32,384]{2,1,0:T(8,128)(2,1)S(1)}, u32[]{:S(2)}, u32[]{:S(2)}) async-start(bf16[32,32,384]{2,1,0:T(8,128)(2,1)} %broadcast_in_dim.2), calls=%async_computation.4 | async-start | bytes 1572864 | tf_op jit(solution)/shard_map/all_to_all | solution.py:45
  205.8 0.7 copy_bitcast_fusion
  206.5 20.3 %all-to-all-done.3 = bf16[32,32,384]{2,1,0:T(8,128)(2,1)S(1)} async-done(((bf16[32,32,384]{2,1,0:T(8,128)(2,1)}), bf16[32,32,384]{2,1,0:T(8,128)(2,1)S(1)}, u32[]{:S(2)}, u32[]{:S(2)}) %all-to-all-start.3) | async-done | bytes 786464 | tf_op jit(solution)/shard_map/all_to_all | solution.py:45
  226.8 0.2 bitcast_convert_fusion
  227.0 1.2 fusion.1
  (8 shorter events, 0.1 us)
Async XLA Ops:
  7.2 1.0 copy-start
  7.2 12.8 %copy-start.3 = (bf16[1024,128]{1,0:T(8,128)(2,1)S(1)}, bf16[1024,128]{1,0:T(8,128)(2,1)}, u32[]{:S(2)}) copy-start(bf16[1024,128]{1,0:T(8,128)(2,1)} %param.10) | copy-start | bytes 786436
  7.2 12.9 %copy-start.4 = (bf16[1024,128]{1,0:T(8,128)(2,1)S(1)}, bf16[1024,128]{1,0:T(8,128)(2,1)}, u32[]{:S(2)}) copy-start(bf16[1024,128]{1,0:T(8,128)(2,1)} %param.11) | copy-start | bytes 786436
  7.2 12.9 %copy-start.5 = (bf16[1024,128]{1,0:T(8,128)(2,1)S(1)}, bf16[1024,128]{1,0:T(8,128)(2,1)}, u32[]{:S(2)}) copy-start(bf16[1024,128]{1,0:T(8,128)(2,1)} %param.12) | copy-start | bytes 786436
  7.2 49.1 %all-gather.2.cloned.1.call-start = ((), (), s32[]{:S(2)}) async-start(), calls=%async_computation.5 | async-start | bytes 2359296 | tf_op jit(solution)/shard_map/all_gather | solution.py:167
  8.9 18.9 %all-to-all-start = ((bf16[128,8,128]{2,0,1:T(8,128)(2,1)}), bf16[128,8,128]{2,0,1:T(8,128)(2,1)S(1)}, u32[]{:S(2)}, u32[]{:S(2)}) async-start(bf16[128,8,128]{2,0,1:T(8,128)(2,1)} %copy_bitcast_fusion.1), calls=%async_computation | async-start | bytes 524288 | tf_op jit(solution)/shard_map/all_to_all | solution.py:166
  19.1 209.1 %reduce-scatter.2.cloned.1.call-start = ((), (), s32[]{:S(2)}) async-start(), calls=%async_computation.6 | async-start | bytes 2359296 | tf_op jit(solution)/shard_map/reduce_scatter | solution.py:210
  56.3 1.6 copy-start.1
  57.9 18.8 %copy-start.6 = (s32[3,8]{1,0:T(4,128)S(1)}, s32[3,8]{1,0:T(4,128)}, u32[]{:S(2)}) copy-start(s32[3,8]{1,0:T(4,128)} %param.9) | copy-start | bytes 292
  57.9 33.0 %copy-start.2 = (s32[1024]{0:T(1024)S(1)}, s32[1024]{0:T(1024)}, u32[]{:S(2)}) copy-start(s32[1024]{0:T(1024)} %param.8) | copy-start | bytes 12292
  60.8 30.2 %collective-permute-start.2 = (bf16[1024,256]{1,0:T(8,128)(2,1)S(1)}, bf16[1024,256]{1,0:T(8,128)(2,1)S(1)}, u32[]{:S(2)}, u32[]{:S(2)}) collective-permute-start(bf16[1024,256]{1,0:T(8,128)(2,1)S(1)} %get-tuple-element.17.own), channel_id=1, source_target_pairs={{0,256},{256,0},{8,264},{264,8},{16,272},{272,16},{24,280},{280,24... | collective-permute-start | bytes 1572872 | tf_op jit(solution)/shard_map/ppermute | solution.py:33
  66.5 24.5 %collective-permute-start.1 = (bf16[1024,256]{1,0:T(8,128)(2,1)S(1)}, bf16[1024,256]{1,0:T(8,128)(2,1)S(1)}, u32[]{:S(2)}, u32[]{:S(2)}) collective-permute-start(bf16[1024,256]{1,0:T(8,128)(2,1)S(1)} %get-tuple-element.17.own), channel_id=1, source_target_pairs={{0,128},{128,0},{8,136},{136,8},{16,144},{144,16},{24,152},{152,24... | collective-permute-start | bytes 1572872 | tf_op jit(solution)/shard_map/ppermute | solution.py:33
  73.5 17.4 %collective-permute-start = (bf16[1024,256]{1,0:T(8,128)(2,1)S(1)}, bf16[1024,256]{1,0:T(8,128)(2,1)S(1)}, u32[]{:S(2)}, u32[]{:S(2)}) collective-permute-start(bf16[1024,256]{1,0:T(8,128)(2,1)S(1)} %get-tuple-element.17.own), channel_id=1, source_target_pairs={{0,8},{8,0},{16,24},{24,16},{32,40},{40,32},{48,56},{56,48},{64,72... | collective-permute-start | bytes 1572872 | tf_op jit(solution)/shard_map/ppermute | solution.py:33
  101.7 14.9 %collective-permute-start.3 = (bf16[1024,256]{1,0:T(8,128)(2,1)S(1)}, bf16[1024,256]{1,0:T(8,128)(2,1)S(1)}, u32[]{:S(2)}, u32[]{:S(2)}) collective-permute-start(bf16[1024,256]{1,0:T(8,128)(2,1)S(1)} %get-tuple-element.22), channel_id=1, source_target_pairs={{0,8},{8,0},{16,24},{24,16},{32,40},{40,32},{48,56},{56,48},{64,72... | collective-permute-start | bytes 1572872 | tf_op jit(solution)/shard_map/ppermute | solution.py:33
  104.8 13.8 %collective-permute-start.4 = (bf16[1024,256]{1,0:T(8,128)(2,1)S(1)}, bf16[1024,256]{1,0:T(8,128)(2,1)S(1)}, u32[]{:S(2)}, u32[]{:S(2)}) collective-permute-start(bf16[1024,256]{1,0:T(8,128)(2,1)S(1)} %get-tuple-element.23), channel_id=1, source_target_pairs={{0,128},{128,0},{8,136},{136,8},{16,144},{144,16},{24,152},{152,24... | collective-permute-start | bytes 1572872 | tf_op jit(solution)/shard_map/ppermute | solution.py:33
  111.9 16.9 %collective-permute-start.5 = (bf16[1024,256]{1,0:T(8,128)(2,1)S(1)}, bf16[1024,256]{1,0:T(8,128)(2,1)S(1)}, u32[]{:S(2)}, u32[]{:S(2)}) collective-permute-start(bf16[1024,256]{1,0:T(8,128)(2,1)S(1)} %get-tuple-element.24), channel_id=1, source_target_pairs={{0,256},{256,0},{8,264},{264,8},{16,272},{272,16},{24,280},{280,24... | collective-permute-start | bytes 1572872 | tf_op jit(solution)/shard_map/ppermute | solution.py:33
  179.7 17.3 %all-to-all-start.1 = ((bf16[8,128,128]{2,1,0:T(8,128)(2,1)}), bf16[8,128,128]{2,1,0:T(8,128)(2,1)S(1)}, u32[]{:S(2)}, u32[]{:S(2)}) async-start(bf16[8,128,128]{2,1,0:T(8,128)(2,1)} %bitcast.4), calls=%async_computation.1 | async-start | bytes 524288 | tf_op jit(solution)/shard_map/all_to_all | solution.py:198
  186.0 11.0 %collective-permute-start.6 = (f32[32,384]{1,0:T(8,128)S(1)}, f32[32,384]{1,0:T(8,128)S(1)}, u32[]{:S(2)}, u32[]{:S(2)}) collective-permute-start(f32[32,384]{1,0:T(8,128)S(1)} %convert_reduce_fusion), channel_id=1, source_target_pairs={{0,256},{256,0},{8,264},{264,8},{16,272},{272,16},{24,280},{280,24... | collective-permute-start | bytes 147464 | tf_op jit(solution)/shard_map/ppermute | solution.py:33
  198.0 28.9 %all-to-all-start.3 = ((bf16[32,32,384]{2,1,0:T(8,128)(2,1)}), bf16[32,32,384]{2,1,0:T(8,128)(2,1)S(1)}, u32[]{:S(2)}, u32[]{:S(2)}) async-start(bf16[32,32,384]{2,1,0:T(8,128)(2,1)} %broadcast_in_dim.2), calls=%async_computation.4 | async-start | bytes 1572864 | tf_op jit(solution)/shard_map/all_to_all | solution.py:45
Sparse Core Ops, SparseCore 0:
  10.1 46.1 all-gather.1
  135.3 53.8 reduce-scatter.1

commit v3 on v2

v3 whole, which is shorter than its diff:
```python
import math

import jax
import jax.numpy as jnp
from jax import lax
from jax.experimental import pallas as pl
from jax.experimental.pallas import tpu as pltpu
from jax.sharding import PartitionSpec as P

HDIM = 64
BLOCK = 128
CORES = 2
KERNEL_VMEM = 12 * 1024 * 1024
FETCH_ORDER = (1, 2, 0)
RETURN_ORDER = (0, 1, 2)
BF = jnp.bfloat16
F32 = jnp.float32
NN = (((1,), (0,)), ((), ()))
NT = (((1,), (1,)), ((), ()))
TN = (((0,), (0,)), ((), ()))
VMEM = pl.BlockSpec(memory_space=pltpu.VMEM)
SMEM = pl.BlockSpec(memory_space=pltpu.SMEM)
ANY = pl.BlockSpec(memory_space=pl.ANY)


def mm(a, b, dims):
    return lax.dot_general(a, b, dims, preferred_element_type=F32)


def from_partner(block, axis, bit):
    count = lax.axis_size(axis)
    route = []
    for low in range(count):
        high = low | 1 << bit
        if high != low and high < count:
            route += [(low, high), (high, low)]
    return lax.ppermute(block, axis, route)


def neighbours():
    count = lax.axis_size("heads")
    up = [(at, (at + CORES) % count) for at in range(count)]
    down = [((at + CORES) % count, at) for at in range(count)]
    across = [(at, at ^ 1) for at in range(count)]
    return up, down, across


def added(*terms):
    return sum(term.astype(F32) for term in terms).astype(BF)


def summed(weight_part, keep, give):
    count = lax.axis_size("nodes")
    split = count // 2
    groups = [list(range(split)), list(range(split, count))]
    rows, width = weight_part.shape
    up, down, across = neighbours()
    step = keep.shape[0] // 4
    half = step // 2

    def exchange(block):
        return lax.all_to_all(block, "nodes", 0, 0, axis_index_groups=groups, tiled=True)

    spread = exchange(weight_part)
    chip = added(keep, lax.ppermute(give, "heads", across))
    mine, high, far, low = (chip[at * step : (at + 1) * step] for at in range(4))
    from_low = lax.ppermute(far[:half], "heads", up)
    from_high = lax.ppermute(far[half:], "heads", down)
    spread, from_low, from_high = lax.optimization_barrier((spread, from_low, from_high))
    share = jnp.sum(spread.reshape(split, rows // split, width).astype(F32), axis=0)
    share = share + from_partner(share, "nodes", split.bit_length() - 1)
    high = jnp.concatenate([added(high[:half], from_low), high[half:]], axis=0)
    low = jnp.concatenate([low[:half], added(low[half:], from_high)], axis=0)
    from_low = lax.ppermute(high, "heads", up)
    from_high = lax.ppermute(low, "heads", down)
    copies = jnp.broadcast_to(share.astype(BF)[None], (split,) + share.shape)
    whole = exchange(copies.reshape(rows, width))
    return whole.astype(F32), added(mine, from_low, from_high)


def gather_pieces(block):
    up, down, across = neighbours()
    half = block.shape[0] // 2
    from_low = lax.ppermute(block, "heads", up)
    from_high = lax.ppermute(block, "heads", down)
    far_low = lax.ppermute(from_low[:half], "heads", up)
    far_high = lax.ppermute(from_high[half:], "heads", down)
    near = jnp.concatenate([block, from_low, from_high], axis=0)
    far = jnp.concatenate([far_low, far_high], axis=0)
    near_across = lax.ppermute(near, "heads", across)
    return near, far, near_across, lax.ppermute(far, "heads", across)


def ones_where(rows_index, columns_index):
    return jnp.where(rows_index == columns_index, 1.0, 0.0).astype(BF)


def head_splitter(width):
    lane = lax.broadcasted_iota(jnp.int32, (BLOCK, width), 1) // HDIM
    heads = width // HDIM

    def split_heads(block):
        zero = jnp.zeros_like(block)
        return jnp.concatenate([jnp.where(lane == head, block, zero) for head in range(heads)], axis=0)

    def join_heads(stacked):
        joined = stacked[:BLOCK]
        for head in range(1, heads):
            joined = jnp.where(lane == head, stacked[head * BLOCK : (head + 1) * BLOCK], joined)
        return joined

    return split_heads, join_heads


def owners(place, flip):
    core = place % CORES
    return place - core + (core + flip) % CORES


def picks_of(order_column, bases, share):
    columns = lax.broadcasted_iota(jnp.int32, (order_column.shape[0], share), 1)
    return jnp.concatenate([ones_where(order_column - base, columns) for base in bases], axis=1)


def near_kernel(place, near, near_across, weights, order_column, pairs):
    share = near.shape[0] // 3
    devices = order_column.shape[0] // share
    picks, projected = [], []
    for flip, piece in ((0, near), (1, near_across)):
        own = owners(place[0], flip)
        bases = [(own + step) % devices * share for step in (0, devices - CORES, CORES)]
        picks.append(picks_of(order_column[...], bases, share))
        projected.append(mm(piece[...], weights[...], NN).astype(BF))
    picked = jnp.concatenate(picks, axis=1)
    pairs[...] = mm(picked, jnp.concatenate(projected, axis=0), NN).astype(BF)


def far_kernel(place, far, far_across, weights, order_column, near_pairs, pairs):
    share = far.shape[0]
    devices = order_column.shape[0] // share
    bases = [(owners(place[0], flip) + devices // 2) % devices * share for flip in (0, 1)]
    both = jnp.concatenate([far[...], far_across[...]], axis=0)
    projected = mm(both, weights[...], NN).astype(BF)
    picked = mm(picks_of(order_column[...], bases, share), projected, NN).astype(BF)
    pairs[...] = near_pairs[...] + picked


def order_kernel(
    place, near, far, near_across, far_across, weights, order_column, upstream, gathered, asks, arrived
):
    rows = gathered.shape[0]
    share = far.shape[0]
    devices = rows // share
    copies = []
    for flip, close, distant in ((0, near, far), (1, near_across, far_across)):
        own = owners(place[0], flip)
        for step, source in (
            (0, close.at[pl.ds(0, share)]),
            (devices - CORES, close.at[pl.ds(share, share)]),
            (CORES, close.at[pl.ds(2 * share, share)]),
            (devices // 2, distant),
        ):
            at = pl.multiple_of((own + step) % devices * share, share)
            target = gathered.at[pl.ds(at, share)]
            copies.append(pltpu.make_async_copy(source, target, arrived.at[len(copies)]))
    for copy in copies:
        copy.start()
    node = lax.broadcasted_iota(jnp.int32, (rows, rows), 1)
    pick = ones_where(order_column[...], node)
    for copy in copies:
        copy.wait()
    queries = mm(gathered[...], weights[...], NN).astype(BF)
    asks[...] = mm(pick, jnp.concatenate([queries, upstream[...]], axis=1), NN).astype(BF)


def attend_kernel(
    slots,
    asks,
    own,
    one,
    two,
    three,
    mixed,
    dquery,
    own_grads,
    one_grads,
    two_grads,
    three_grads,
):
    rows = asks.shape[0]
    width = asks.shape[1] // 2
    score_scale = 1.0 / math.sqrt(HDIM)
    split_heads, join_heads = head_splitter(width)

    def one_block(block, carry):
        here = pl.ds(pl.multiple_of(block * BLOCK, BLOCK), BLOCK)
        places = [here] + [
            pl.ds(pl.multiple_of(slots[which, block] * BLOCK, BLOCK), BLOCK)
            for which in FETCH_ORDER
        ]
        pairs = [source[place, :] for source, place in zip((own, one, two, three), places)]
        keys = jnp.concatenate([pair[:, :width] for pair in pairs], axis=0)
        values = jnp.concatenate([pair[:, width:] for pair in pairs], axis=0)
        query = split_heads(asks[here, :width])
        cotangent = split_heads(asks[here, width:])
        scores = mm(query, keys, NT) * score_scale
        peak = jnp.max(scores, axis=-1, keepdims=True)
        raised = jnp.exp(scores - peak)
        softmax = raised * (1.0 / jnp.sum(raised, axis=-1, keepdims=True))
        weights_low = softmax.astype(BF)
        mixed[here, :] = join_heads(mm(weights_low, values, NN)).astype(BF)
        dprobs = mm(cotangent, values, NT)
        row_delta = jnp.sum(softmax * dprobs, axis=-1, keepdims=True)
        dscores = (softmax * (dprobs - row_delta) * score_scale).astype(BF)
        dquery[here, :] = join_heads(mm(dscores, keys, NN)).astype(BF)
        dkeys = mm(dscores, query, TN)
        dvalues = mm(weights_low, cotangent, TN)
        targets = (own_grads, one_grads, two_grads, three_grads)
        for which, target in enumerate(targets):
            part = slice(which * BLOCK, (which + 1) * BLOCK)
            target[places[which], :width] = dkeys[part].astype(target.dtype)
            target[places[which], width:] = dvalues[part].astype(target.dtype)
        return carry

    lax.fori_loop(0, rows // BLOCK, one_block, 0)


def restore_kernel(mixed, order_row, mixed_nodes):
    rows = mixed.shape[0]
    node = lax.broadcasted_iota(jnp.int32, (rows, rows), 0)
    mixed_nodes[...] = mm(ones_where(node, order_row[...]), mixed[...], NN).astype(BF)


def query_kernel(features, order_row, dquery, dquery_nodes, weight_part):
    rows = dquery.shape[0]
    node = lax.broadcasted_iota(jnp.int32, (rows, rows), 0)
    dquery_nodes[...] = mm(ones_where(node, order_row[...]), dquery[...], NN).astype(BF)
    weight_part[...] = mm(features[...], dquery_nodes[...], TN).astype(BF)


def finish_kernel(
    place,
    features,
    weights,
    order_row,
    dquery_nodes,
    query_part,
    own,
    first,
    second,
    third,
    weight_part,
    keep,
    give,
    grad_nodes,
    chosen,
    own_held,
    others_held,
    arrived,
):
    rows, width = dquery_nodes.shape
    copies = [pltpu.make_async_copy(own, own_held, arrived.at[3])]
    for at, source in enumerate((first, second, third)):
        copies.append(pltpu.make_async_copy(source, others_held.at[at], arrived.at[at]))
    for copy in copies:
        copy.start()
    node = lax.broadcasted_iota(jnp.int32, (rows, rows), 0)
    restore = ones_where(node, order_row[...])
    for copy in copies:
        copy.wait()
    total = own_held[...]
    for at in range(3):
        total = total + others_held[at].astype(F32)
    pair_nodes = mm(restore, total.astype(BF), NN).astype(BF)
    weight_part[:, :width] = query_part[...]
    weight_part[:, width:] = mm(features[...], pair_nodes, TN).astype(BF)
    grad_nodes[:, :width] = dquery_nodes[...]
    grad_nodes[:, width:] = pair_nodes
    here = place[0]
    core = here % CORES
    chips = keep.shape[0] // BLOCK
    devices = chips * CORES
    share = rows // devices
    for flip, target in ((0, keep), (1, give)):
        own_row = here - core + (core + flip) % CORES
        for step in range(chips):
            at = pl.multiple_of((own_row + CORES * step) % devices * share, share)
            chosen[step * share : (step + 1) * share, :] = grad_nodes[pl.ds(at, share), :]
        target[...] = mm(chosen[...], weights[...], NT).astype(BF)


def local(features, node_order, partners, query_weight, key_weight, value_weight, upstream):
    width = query_weight.shape[1]
    depth = query_weight.shape[0]
    pair_weights = jnp.concatenate([key_weight, value_weight], axis=1)
    stacked = jnp.concatenate([query_weight, pair_weights], axis=1)
    rows = node_order.shape[0]
    blocks = rows // BLOCK
    slots = partners % blocks
    order_column = node_order.reshape(rows, 1)
    order_row = node_order.reshape(1, rows)
    levels = lax.axis_size("nodes").bit_length() - 1
    swap_bits = (0, levels - 2, levels - 1)
    params = pltpu.CompilerParams(vmem_limit_bytes=KERNEL_VMEM)
    place = lax.axis_index("heads").astype(jnp.int32).reshape(1)

    def shape(*dims, dtype=BF):
        return jax.ShapeDtypeStruct(dims, dtype)

    def swapped(blocks_for):
        return [
            from_partner(block, "nodes", swap_bits[which])
            for block, which in zip(blocks_for, FETCH_ORDER)
        ]

    arriving = lax.all_to_all(upstream, "heads", split_axis=1, concat_axis=0, tiled=True)
    pieces = gather_pieces(features)
    near, far, near_across, far_across = pieces
    near_pairs = pl.pallas_call(
        near_kernel,
        out_shape=shape(rows, 2 * width),
        in_specs=[SMEM] + [VMEM] * 4,
        out_specs=VMEM,
        compiler_params=params,
        name="project_near",
    )(place, near, near_across, pair_weights, order_column)
    far_across, arriving = lax.optimization_barrier((far_across, arriving))
    pairs = pl.pallas_call(
        far_kernel,
        out_shape=shape(rows, 2 * width),
        in_specs=[SMEM] + [VMEM] * 5,
        out_specs=VMEM,
        compiler_params=params,
        name="project_far",
    )(place, far, far_across, pair_weights, order_column, near_pairs)
    others = swapped([pairs] * 3)
    gathered, asks = pl.pallas_call(
        order_kernel,
        out_shape=(shape(rows, depth), shape(rows, 2 * width)),
        in_specs=[SMEM] + [ANY] * 4 + [VMEM] * 3,
        out_specs=(VMEM,) * 2,
        scratch_shapes=[pltpu.SemaphoreType.DMA((2 * CORES * CORES,))],
        compiler_params=params,
        name="order",
    )(place, near, far, near_across, far_across, query_weight, order_column, arriving)
    mixed, dquery, own_grads, *sent = pl.pallas_call(
        attend_kernel,
        out_shape=(
            shape(rows, width),
            shape(rows, width),
            shape(rows, 2 * width, dtype=F32),
            shape(rows, 2 * width),
            shape(rows, 2 * width),
            shape(rows, 2 * width),
        ),
        in_specs=[SMEM] + [VMEM] * 5,
        out_specs=(VMEM,) * 6,
        compiler_params=params,
        name="attend",
    )(slots, asks, pairs, *others)
    mixed_nodes = pl.pallas_call(
        restore_kernel,
        out_shape=shape(rows, width),
        in_specs=[VMEM] * 2,
        out_specs=VMEM,
        compiler_params=params,
        name="restore",
    )(mixed, order_row)
    returned = swapped(sent)
    mixed_nodes, *returned = lax.optimization_barrier((mixed_nodes, *returned))
    attended = lax.all_to_all(mixed_nodes, "heads", split_axis=0, concat_axis=1, tiled=True)
    dquery_nodes, query_part = pl.pallas_call(
        query_kernel,
        out_shape=(shape(rows, width), shape(depth, width)),
        in_specs=[VMEM] * 3,
        out_specs=(VMEM,) * 2,
        compiler_params=params,
        name="query_grads",
    )(gathered, order_row, dquery)
    weight_part, keep, give = pl.pallas_call(
        finish_kernel,
        out_shape=(
            shape(depth, 3 * width),
            shape(rows // CORES, depth),
            shape(rows // CORES, depth),
        ),
        in_specs=[SMEM] + [VMEM] * 5 + [ANY] * 4,
        out_specs=(VMEM,) * 3,
        scratch_shapes=[
            pltpu.VMEM((rows, 3 * width), BF),
            pltpu.VMEM((rows // CORES, 3 * width), BF),
            pltpu.VMEM((rows, 2 * width), F32),
            pltpu.VMEM((3, rows, 2 * width), BF),
            pltpu.SemaphoreType.DMA((4,)),
        ],
        compiler_params=params,
        name="finish",
    )(place, gathered, stacked, order_row, dquery_nodes, query_part, own_grads, *[returned[at] for at in RETURN_ORDER])
    weight_grads, feature_grad = summed(weight_part, keep, give)
    return (
        attended,
        feature_grad,
        weight_grads[:, :width],
        weight_grads[:, width : 2 * width],
        weight_grads[:, 2 * width :],
    )


def solution(mesh):
    return jax.shard_map(
        local,
        mesh=mesh,
        in_specs=(
            P(("nodes", "heads"), None),
            P("nodes"),
            P(None, "nodes"),
            P(None, "heads"),
            P(None, "heads"),
            P(None, "heads"),
            P(("nodes", "heads"), None),
        ),
        out_specs=(
            P(("nodes", "heads"), None),
            P(("nodes", "heads"), None),
            P(None, "heads"),
            P(None, "heads"),
            P(None, "heads"),
        ),
        check_vma=False,
    )
```

time: 237 us -> 210 us (0.89)
  blocking collectives: 44.5 us -> 0 us
  starting transfers between devices: 59.1 us -> 102 us
  waiting for transfers between devices: 90.4 us -> 69.7 us
  between operations: 14.2 us -> 1.07 us
  Pallas kernels: 20 us -> 24.6 us
  other arithmetic: 0.32 us -> 2.98 us
    all_to_all x1 -> x0, blocking collectives: 44.5 us -> none  [summed_over_nodes(): lax.all_to_all(partial, 'nodes', 0, 0, axis_index_groups=groups, tiled=True)]
    ppermute x0 -> x11, starting transfers between devices: none -> 42.7 us  [the longest x1 5.54 us: gather_pieces(): from_high = lax.ppermute(block, 'heads', down)]
    all_gather x1 -> x0, waiting for transfers between devices: 28.5 us -> none  [local(): gathered = lax.all_gather(features, 'heads', axis=0, tiled=True)]
    ppermute x0 -> x11, waiting for transfers between devices: none -> 17 us  [the longest x1 7.13 us: gather_pieces(): from_high = lax.ppermute(block, 'heads', down)]
    all_to_all x1 -> x2, starting transfers between devices: 7.81 us -> 16.7 us  [exchange(): lax.all_to_all(block, 'nodes', 0, 0, axis_index_groups=groups, tiled=True)]
    all_to_all x1, starting transfers between devices: 10.2 us -> 3.89 us  [local(): lax.all_to_all(upstream, 'heads', split_axis=1, concat_axis=0, tiled=True)]
    pallas_call x3 -> x7, Pallas kernels: 20 us -> 24.6 us  [the longest x1 9.32 us: local(): pl.pallas_call(attend_kernel, out_shape=(shape(rows, width), shape(rows,...]
    all_to_all x1, waiting for transfers between devices: 7.59 us -> 3.88 us  [local(): lax.all_to_all(upstream, 'heads', split_axis=1, concat_axis=0, tiled=True)]
  transfers between devices with their start and end apart: 12 -> 22, of which waited for: 7 -> 12; matrix products, arithmetic and copies ran while one was open for 2% -> 4% of each run, Pallas kernels for 0% -> 4%
where the time goes in v3:
time: 210 us; the launch traced here: 207 us
  starting transfers between devices  102 us (49%)
  waiting for transfers between devices  69.7 us (33%)
  Pallas kernels  24.6 us (12%)
  local copies, waits for them, and re-layouts  6.99 us (3%)
  other arithmetic  2.98 us (1%)
    ppermute x7, starting transfers between devices, from_partner(): return lax.ppermute(block, axis, route)  33.8 us
    ppermute x7, waiting for transfers between devices, from_partner(): return lax.ppermute(block, axis, route)  31.5 us
    all_to_all x2, waiting for transfers between devices, exchange(): lax.all_to_all(block, 'nodes', 0, 0, axis_index_groups=groups, tiled=True)  17.4 us
    all_to_all x2, starting transfers between devices, exchange(): lax.all_to_all(block, 'nodes', 0, 0, axis_index_groups=groups, tiled=True)  16.7 us
    pallas_call x1, Pallas kernels, local(): pl.pallas_call(attend_kernel, out_shape=(shape(rows, width), shape(rows,...  9.32 us
    ppermute x1, waiting for transfers between devices, gather_pieces(): from_high = lax.ppermute(block, 'heads', down)  7.13 us
    ppermute x1, waiting for transfers between devices, summed(): from_low = lax.ppermute(high, 'heads', up)  5.8 us
    ppermute x1, starting transfers between devices, gather_pieces(): from_high = lax.ppermute(block, 'heads', down)  5.54 us
  transfers between devices with their start and end apart: 22, of which 12 were waited for; matrix products, arithmetic and copies ran while one was open for 4% of the time, Pallas kernels for 4%

profile of v3, /device:TPU:1, one launch (start us, length us, event | category | flops | bytes accessed | tf_op | source)
XLA Modules:
  0.0 207.2 jit_solution(9686540434343259573)
XLA Ops:
  0.6 5.0 %collective-permute-start = (bf16[128,1024]{1,0:T(8,128)(2,1)}, bf16[128,1024]{1,0:T(8,128)(2,1)S(1)}, u32[]{:S(2)}, u32[]{:S(2)}) collective-permute-start(bf16[128,1024]{1,0:T(8,128)(2,1)} %param.7), channel_id=1, source_target_pairs={{0,2},{1,3},{2,4},{3,5},{4,6},{5,7},{6,0},{7,1},{8,10},{9,11},{10,... | collective-permute-start | bytes 786440 | tf_op jit(solution)/shard_map/ppermute | solution.py:84
  5.6 5.5 %collective-permute-start.1 = (bf16[128,1024]{1,0:T(8,128)(2,1)}, bf16[128,1024]{1,0:T(8,128)(2,1)S(1)}, u32[]{:S(2)}, u32[]{:S(2)}) collective-permute-start(bf16[128,1024]{1,0:T(8,128)(2,1)} %param.7), channel_id=1, source_target_pairs={{2,0},{3,1},{4,2},{5,3},{6,4},{7,5},{0,6},{1,7},{10,8},{11,9},{12,... | collective-permute-start | bytes 786440 | tf_op jit(solution)/shard_map/ppermute | solution.py:85
  11.2 1.0 constant_dynamic-update-slice_fusion.2
  12.2 1.2 collective-permute-done
  13.4 7.1 %collective-permute-done.1 = bf16[128,1024]{1,0:T(8,128)(2,1)S(1)} collective-permute-done((bf16[128,1024]{1,0:T(8,128)(2,1)}, bf16[128,1024]{1,0:T(8,128)(2,1)S(1)}, u32[]{:S(2)}, u32[]{:S(2)}) %collective-permute-start.1) | collective-permute-done | bytes 262176 | tf_op jit(solution)/shard_map/ppermute | solution.py:85
  20.5 3.7 %collective-permute-start.4 = (bf16[384,1024]{1,0:T(8,128)(2,1)S(1)}, bf16[384,1024]{1,0:T(8,128)(2,1)S(1)}, u32[]{:S(2)}, u32[]{:S(2)}) collective-permute-start(bf16[384,1024]{1,0:T(8,128)(2,1)S(1)} %constant_dynamic-update-slice_fusion.near), channel_id=1, source_target_pairs={{0,1},{1,0},{2,3},{3,2},{4,5},{5,4},{6,7},{7,6},{8,9},{9,8},{10,11... | collective-permute-start | bytes 2359304 | tf_op jit(solution)/shard_map/ppermute | solution.py:90
  24.3 2.2 %collective-permute-start.2 = (bf16[64,1024]{1,0:T(8,128)(2,1)S(1)}, bf16[64,1024]{1,0:T(8,128)(2,1)S(1)}, u32[]{:S(2)}, u32[]{:S(2)}) collective-permute-start(bf16[64,1024]{1,0:T(8,128)(2,1)S(1)} %slice.57), channel_id=1, source_target_pairs={{0,2},{1,3},{2,4},{3,5},{4,6},{5,7},{6,0},{7,1},{8,10},{9,11},{10,... | collective-permute-start | bytes 393224 | tf_op jit(solution)/shard_map/ppermute | solution.py:86
  26.5 4.9 %collective-permute-start.3 = (bf16[64,1024]{1,0:T(8,128)(2,1)S(1)}, bf16[64,1024]{1,0:T(8,128)(2,1)S(1)}, u32[]{:S(2)}, u32[]{:S(2)}) collective-permute-start(bf16[64,1024]{1,0:T(8,128)(2,1)S(1)} %slice.58), channel_id=1, source_target_pairs={{2,0},{3,1},{4,2},{5,3},{6,4},{7,5},{0,6},{1,7},{10,8},{11,9},{12,... | collective-permute-start | bytes 393224 | tf_op jit(solution)/shard_map/ppermute | solution.py:87
  31.4 0.8 copy_bitcast_fusion.1
  32.1 3.9 %all-to-all-start = ((bf16[128,8,128]{2,0,1:T(8,128)(2,1)}), bf16[128,8,128]{2,0,1:T(8,128)(2,1)S(1)}, u32[]{:S(2)}, u32[]{:S(2)}) async-start(bf16[128,8,128]{2,0,1:T(8,128)(2,1)} %copy_bitcast_fusion.1), calls=%async_computation | async-start | bytes 524288 | tf_op jit(solution)/shard_map/all_to_all | solution.py:316
  36.2 2.4 %collective-permute-start.5 = (bf16[128,1024]{1,0:T(8,128)(2,1)S(1)}, bf16[128,1024]{1,0:T(8,128)(2,1)}, u32[]{:S(2)}, u32[]{:S(2)}) collective-permute-start(bf16[128,1024]{1,0:T(8,128)(2,1)S(1)} %constant_dynamic-update-slice_fusion.3.far), channel_id=1, source_target_pairs={{0,1},{1,0},{2,3},{3,2},{4,5},{5,4},{6,7},{7,6},{8,9},{9,8},{10,11... | collective-permute-start | bytes 786440 | tf_op jit(solution)/shard_map/ppermute | solution.py:91
  38.8 1.0 constant_dynamic-update-slice_fusion.6
  39.9 1.0 constant_dynamic-update-slice_fusion.5.weights
  40.9 3.9 %all-to-all-done = bf16[128,8,128]{2,0,1:T(8,128)(2,1)S(1)} async-done(((bf16[128,8,128]{2,0,1:T(8,128)(2,1)}), bf16[128,8,128]{2,0,1:T(8,128)(2,1)S(1)}, u32[]{:S(2)}, u32[]{:S(2)}) %all-to-all-start) | async-done | bytes 262176 | tf_op jit(solution)/shard_map/all_to_all | solution.py:316
  44.8 1.1 project_near.1.near_pairs
  45.9 1.8 project_far.1.own
  47.7 7.5 %collective-permute-start.6 = (bf16[1024,256]{1,0:T(8,128)(2,1)S(1)}, bf16[1024,256]{1,0:T(8,128)(2,1)S(1)}, u32[]{:S(2)}, u32[]{:S(2)}) collective-permute-start(bf16[1024,256]{1,0:T(8,128)(2,1)S(1)} %project_far.1.own), channel_id=1, source_target_pairs={{0,128},{128,0},{8,136},{136,8},{16,144},{144,16},{24,152},{152,24... | collective-permute-start | bytes 1572872 | tf_op jit(solution)/shard_map/ppermute | solution.py:37
  55.2 8.2 %collective-permute-start.7 = (bf16[1024,256]{1,0:T(8,128)(2,1)S(1)}, bf16[1024,256]{1,0:T(8,128)(2,1)S(1)}, u32[]{:S(2)}, u32[]{:S(2)}) collective-permute-start(bf16[1024,256]{1,0:T(8,128)(2,1)S(1)} %project_far.1.own), channel_id=1, source_target_pairs={{0,256},{256,0},{8,264},{264,8},{16,272},{272,16},{24,280},{280,24... | collective-permute-start | bytes 1572872 | tf_op jit(solution)/shard_map/ppermute | solution.py:37
  63.4 3.1 %collective-permute-start.8 = (bf16[1024,256]{1,0:T(8,128)(2,1)S(1)}, bf16[1024,256]{1,0:T(8,128)(2,1)S(1)}, u32[]{:S(2)}, u32[]{:S(2)}) collective-permute-start(bf16[1024,256]{1,0:T(8,128)(2,1)S(1)} %project_far.1.own), channel_id=1, source_target_pairs={{0,8},{8,0},{16,24},{24,16},{32,40},{40,32},{48,56},{56,48},{64,72... | collective-permute-start | bytes 1572872 | tf_op jit(solution)/shard_map/ppermute | solution.py:37
  66.6 3.7 %order.1 = (bf16[1024,1024]{1,0:T(8,128)(2,1)S(1)}, bf16[1024,256]{1,0:T(8,128)(2,1)S(1)}) custom-call(s32[1]{0:T(128)} %bitcast.place, bf16[384,1024]{1,0:T(8,128)(2,1)S(1)} %constant_dynamic-update-slice_fusion.near, bf16[128,1024]{1,0:T(8,128)(2,1)S(1)} %constant_dynamic-update-slice_fusion.3.far, ...), custom_call_target="tpu_custom_call" | custom-call | tf_op jit(solution)/shard_map/order/pallas_call | solution.py:337
  70.3 15.3 %collective-permute-done.7.two = bf16[1024,256]{1,0:T(8,128)(2,1)S(1)} collective-permute-done((bf16[1024,256]{1,0:T(8,128)(2,1)S(1)}, bf16[1024,256]{1,0:T(8,128)(2,1)S(1)}, u32[]{:S(2)}, u32[]{:S(2)}) %collective-permute-start.7) | collective-permute-done | bytes 524320 | tf_op jit(solution)/shard_map/ppermute | solution.py:37
  85.6 9.3 %attend.1 = (bf16[1024,128]{1,0:T(8,128)(2,1)S(1)}, bf16[1024,128]{1,0:T(8,128)(2,1)S(1)}, f32[1024,256]{1,0:T(8,128)S(1)}, bf16[1024,256]{1,0:T(8,128)(2,1)S(1)...) custom-call(s32[3,8]{1,0:T(4,128)S(1)} %add_select_fusion.slots, ...), custom_call_target="tpu_custom_call" | custom-call | tf_op jit(solution)/shard_map/attend/pallas_call | solution.py:346
  94.9 2.1 %collective-permute-start.9 = (bf16[1024,256]{1,0:T(8,128)(2,1)S(1)}, bf16[1024,256]{1,0:T(8,128)(2,1)S(1)}, u32[]{:S(2)}, u32[]{:S(2)}) collective-permute-start(bf16[1024,256]{1,0:T(8,128)(2,1)S(1)} %get-tuple-element.31), channel_id=1, source_target_pairs={{0,128},{128,0},{8,136},{136,8},{16,144},{144,16},{24,152},{152,24... | collective-permute-start | bytes 1572872 | tf_op jit(solution)/shard_map/ppermute | solution.py:37
  97.1 3.9 %collective-permute-start.10 = (bf16[1024,256]{1,0:T(8,128)(2,1)S(1)}, bf16[1024,256]{1,0:T(8,128)(2,1)S(1)}, u32[]{:S(2)}, u32[]{:S(2)}) collective-permute-start(bf16[1024,256]{1,0:T(8,128)(2,1)S(1)} %get-tuple-element.32), channel_id=1, source_target_pairs={{0,256},{256,0},{8,264},{264,8},{16,272},{272,16},{24,280},{280,24... | collective-permute-start | bytes 1572872 | tf_op jit(solution)/shard_map/ppermute | solution.py:37
  100.9 3.1 %collective-permute-start.11 = (bf16[1024,256]{1,0:T(8,128)(2,1)S(1)}, bf16[1024,256]{1,0:T(8,128)(2,1)S(1)}, u32[]{:S(2)}, u32[]{:S(2)}) collective-permute-start(bf16[1024,256]{1,0:T(8,128)(2,1)S(1)} %get-tuple-element.33), channel_id=1, source_target_pairs={{0,8},{8,0},{16,24},{24,16},{32,40},{40,32},{48,56},{56,48},{64,72... | collective-permute-start | bytes 1572872 | tf_op jit(solution)/shard_map/ppermute | solution.py:37
  104.2 1.4 restore.1
  105.6 2.3 %query_grads.1 = (bf16[1024,128]{1,0:T(8,128)(2,1)S(1)}, bf16[1024,128]{1,0:T(8,128)(2,1)S(1)}) custom-call(bf16[1024,1024]{1,0:T(8,128)(2,1)S(1)} %get-tuple-element.35.features, s32[1,1024]{1,0:T(1,128)S(1)} %bitcast.28, bf16[1024,128]{1,0:T(8,128)(2,1)S(1)} %get-tuple-element.36.dquery), custom_call_target="tpu_custom_call" | custom-call | tf_op jit(solution)/shard_map/query_grads/pallas_call | solution.py:372
  107.9 8.0 %collective-permute-done.9.first = bf16[1024,256]{1,0:T(8,128)(2,1)S(1)} collective-permute-done((bf16[1024,256]{1,0:T(8,128)(2,1)S(1)}, bf16[1024,256]{1,0:T(8,128)(2,1)S(1)}, u32[]{:S(2)}, u32[]{:S(2)}) %collective-permute-start.9) | collective-permute-done | bytes 524320 | tf_op jit(solution)/shard_map/ppermute | solution.py:37
  115.9 3.7 %collective-permute-done.10.second = bf16[1024,256]{1,0:T(8,128)(2,1)S(1)} collective-permute-done((bf16[1024,256]{1,0:T(8,128)(2,1)S(1)}, bf16[1024,256]{1,0:T(8,128)(2,1)S(1)}, u32[]{:S(2)}, u32[]{:S(2)}) %collective-permute-start.10) | collective-permute-done | bytes 524320 | tf_op jit(solution)/shard_map/ppermute | solution.py:37
  119.5 5.0 %finish.1 = (bf16[1024,384]{1,0:T(8,128)(2,1)}, bf16[512,1024]{1,0:T(8,128)(2,1)S(1)}, bf16[512,1024]{1,0:T(8,128)(2,1)S(1)}) custom-call(s32[1]{0:T(128)} %bitcast.place, bf16[1024,1024]{1,0:T(8,128)(2,1)S(1)} %get-tuple-element.35.features, bf16[1024,384]{1,0:T(8,128)(2,1)S(1)} %pad_maximum_fusion.weights, s32[1,1024]{1,0:T(1,128)S(1)} %bitcast.29, ...), custom_call_target="tpu_custom_call" | custom-call | tf_op jit(solution)/shard_map/finish/pallas_call | solution.py:380
  124.5 5.2 %collective-permute-start.12 = (bf16[512,1024]{1,0:T(8,128)(2,1)S(1)}, bf16[512,1024]{1,0:T(8,128)(2,1)}, u32[]{:S(2)}, u32[]{:S(2)}) collective-permute-start(bf16[512,1024]{1,0:T(8,128)(2,1)S(1)} %get-tuple-element.44), channel_id=1, source_target_pairs={{0,1},{1,0},{2,3},{3,2},{4,5},{5,4},{6,7},{7,6},{8,9},{9,8},{10,11... | collective-permute-start | bytes 3145736 | tf_op jit(solution)/shard_map/ppermute | solution.py:65
  129.7 11.5 %all-to-all-start.2 = ((bf16[32,32,384]{2,1,0:T(8,128)(2,1)}), bf16[32,32,384]{2,1,0:T(8,128)(2,1)S(1)}, u32[]{:S(2)}, u32[]{:S(2)}) async-start(bf16[32,32,384]{2,1,0:T(8,128)(2,1)} %bitcast.7), calls=%async_computation.2 | async-start | bytes 1572864 | tf_op jit(solution)/shard_map/all_to_all | solution.py:62
  141.2 1.6 add_convert_fusion
  142.9 2.1 %collective-permute-start.13 = (bf16[64,1024]{1,0:T(8,128)(2,1)S(1)}, bf16[64,1024]{1,0:T(8,128)(2,1)S(1)}, u32[]{:S(2)}, u32[]{:S(2)}) collective-permute-start(bf16[64,1024]{1,0:T(8,128)(2,1)S(1)} %get-tuple-element.57), channel_id=1, source_target_pairs={{0,2},{1,3},{2,4},{3,5},{4,6},{5,7},{6,0},{7,1},{8,10},{9,11},{10,... | collective-permute-start | bytes 393224 | tf_op jit(solution)/shard_map/ppermute | solution.py:67
  145.1 4.9 %collective-permute-start.14 = (bf16[64,1024]{1,0:T(8,128)(2,1)S(1)}, bf16[64,1024]{1,0:T(8,128)(2,1)S(1)}, u32[]{:S(2)}, u32[]{:S(2)}) collective-permute-start(bf16[64,1024]{1,0:T(8,128)(2,1)S(1)} %get-tuple-element.56), channel_id=1, source_target_pairs={{2,0},{3,1},{4,2},{5,3},{6,4},{7,5},{0,6},{1,7},{10,8},{11,9},{12,... | collective-permute-start | bytes 393224 | tf_op jit(solution)/shard_map/ppermute | solution.py:68
  150.0 13.3 %all-to-all-done.2 = bf16[32,32,384]{2,1,0:T(8,128)(2,1)S(1)} async-done(((bf16[32,32,384]{2,1,0:T(8,128)(2,1)}), bf16[32,32,384]{2,1,0:T(8,128)(2,1)S(1)}, u32[]{:S(2)}, u32[]{:S(2)}) %all-to-all-start.2) | async-done | bytes 786464 | tf_op jit(solution)/shard_map/all_to_all | solution.py:62
  163.3 4.7 %all-to-all-start.1 = ((bf16[8,128,128]{2,1,0:T(8,128)(2,1)}), bf16[8,128,128]{2,1,0:T(8,128)(2,1)S(1)}, u32[]{:S(2)}, u32[]{:S(2)}) async-start(bf16[8,128,128]{2,1,0:T(8,128)(2,1)} %bitcast.5), calls=%async_computation.1 | async-start | bytes 524288 | tf_op jit(solution)/shard_map/all_to_all | solution.py:371
  168.2 6.0 %collective-permute-start.17 = (f32[32,384]{1,0:T(8,128)S(1)}, f32[32,384]{1,0:T(8,128)S(1)}, u32[]{:S(2)}, u32[]{:S(2)}) collective-permute-start(f32[32,384]{1,0:T(8,128)S(1)} %convert_reduce_fusion), channel_id=1, source_target_pairs={{0,256},{256,0},{8,264},{264,8},{16,272},{272,16},{24,280},{280,24... | collective-permute-start | bytes 147464 | tf_op jit(solution)/shard_map/ppermute | solution.py:37
  174.1 4.5 %collective-permute-done.17 = f32[32,384]{1,0:T(8,128)S(1)} collective-permute-done((f32[32,384]{1,0:T(8,128)S(1)}, f32[32,384]{1,0:T(8,128)S(1)}, u32[]{:S(2)}, u32[]{:S(2)}) %collective-permute-start.17) | collective-permute-done | bytes 49184 | tf_op jit(solution)/shard_map/ppermute | solution.py:37
  178.6 1.0 broadcast_in_dim.2
  179.6 5.2 %all-to-all-start.3 = ((bf16[32,32,384]{2,1,0:T(8,128)(2,1)}), bf16[32,32,384]{2,1,0:T(8,128)(2,1)S(1)}, u32[]{:S(2)}, u32[]{:S(2)}) async-start(bf16[32,32,384]{2,1,0:T(8,128)(2,1)} %broadcast_in_dim.2), calls=%async_computation.3 | async-start | bytes 1572864 | tf_op jit(solution)/shard_map/all_to_all | solution.py:62
  184.9 4.9 %collective-permute-start.16 = (bf16[128,1024]{1,0:T(8,128)(2,1)S(1)}, bf16[128,1024]{1,0:T(8,128)(2,1)S(1)}, u32[]{:S(2)}, u32[]{:S(2)}) collective-permute-start(bf16[128,1024]{1,0:T(8,128)(2,1)S(1)} %pad_maximum_fusion.2), channel_id=1, source_target_pairs={{2,0},{3,1},{4,2},{5,3},{6,4},{7,5},{0,6},{1,7},{10,8},{11,9},{12,... | collective-permute-start | bytes 786440 | tf_op jit(solution)/shard_map/ppermute | solution.py:75
  189.8 1.9 collective-permute-start.15
  192.5 2.7 %collective-permute-done.16 = bf16[128,1024]{1,0:T(8,128)(2,1)S(1)} collective-permute-done((bf16[128,1024]{1,0:T(8,128)(2,1)S(1)}, bf16[128,1024]{1,0:T(8,128)(2,1)S(1)}, u32[]{:S(2)}, u32[]{:S(2)}) %collective-permute-start.16) | collective-permute-done | bytes 262176 | tf_op jit(solution)/shard_map/ppermute | solution.py:75
  195.2 5.8 %collective-permute-done.15 = bf16[128,1024]{1,0:T(8,128)(2,1)S(1)} collective-permute-done((bf16[128,1024]{1,0:T(8,128)(2,1)S(1)}, bf16[128,1024]{1,0:T(8,128)(2,1)S(1)}, u32[]{:S(2)}, u32[]{:S(2)}) %collective-permute-start.15) | collective-permute-done | bytes 262176 | tf_op jit(solution)/shard_map/ppermute | solution.py:74
  201.0 0.8 add_convert_fusion.1
  201.8 4.1 %all-to-all-done.3 = bf16[32,32,384]{2,1,0:T(8,128)(2,1)S(1)} async-done(((bf16[32,32,384]{2,1,0:T(8,128)(2,1)}), bf16[32,32,384]{2,1,0:T(8,128)(2,1)S(1)}, u32[]{:S(2)}, u32[]{:S(2)}) %all-to-all-start.3) | async-done | bytes 786464 | tf_op jit(solution)/shard_map/all_to_all | solution.py:62
  206.1 1.2 fusion.1
  (40 shorter events, 1.8 us)
Async XLA Ops:
  0.6 30.7 %copy-start = (bf16[128,1024]{1,0:T(8,128)(2,1)S(1)}, bf16[128,1024]{1,0:T(8,128)(2,1)}, u32[]{:S(2)}) copy-start(bf16[128,1024]{1,0:T(8,128)(2,1)} %param.13) | copy-start | bytes 786436
  0.6 12.7 %collective-permute-start = (bf16[128,1024]{1,0:T(8,128)(2,1)}, bf16[128,1024]{1,0:T(8,128)(2,1)S(1)}, u32[]{:S(2)}, u32[]{:S(2)}) collective-permute-start(bf16[128,1024]{1,0:T(8,128)(2,1)} %param.7), channel_id=1, source_target_pairs={{0,2},{1,3},{2,4},{3,5},{4,6},{5,7},{6,0},{7,1},{8,10},{9,11},{10,... | collective-permute-start | bytes 786440 | tf_op jit(solution)/shard_map/ppermute | solution.py:84
  5.6 14.9 %collective-permute-start.1 = (bf16[128,1024]{1,0:T(8,128)(2,1)}, bf16[128,1024]{1,0:T(8,128)(2,1)S(1)}, u32[]{:S(2)}, u32[]{:S(2)}) collective-permute-start(bf16[128,1024]{1,0:T(8,128)(2,1)} %param.7), channel_id=1, source_target_pairs={{2,0},{3,1},{4,2},{5,3},{6,4},{7,5},{0,6},{1,7},{10,8},{11,9},{12,... | collective-permute-start | bytes 786440 | tf_op jit(solution)/shard_map/ppermute | solution.py:85
  12.1 26.5 %copy-start.2 = (s32[1024]{0:T(1024)S(1)}, s32[1024]{0:T(1024)}, u32[]{:S(2)}) copy-start(s32[1024]{0:T(1024)} %param.8) | copy-start | bytes 12292
  20.5 24.2 %collective-permute-start.4 = (bf16[384,1024]{1,0:T(8,128)(2,1)S(1)}, bf16[384,1024]{1,0:T(8,128)(2,1)S(1)}, u32[]{:S(2)}, u32[]{:S(2)}) collective-permute-start(bf16[384,1024]{1,0:T(8,128)(2,1)S(1)} %constant_dynamic-update-slice_fusion.near), channel_id=1, source_target_pairs={{0,1},{1,0},{2,3},{3,2},{4,5},{5,4},{6,7},{7,6},{8,9},{9,8},{10,11... | collective-permute-start | bytes 2359304 | tf_op jit(solution)/shard_map/ppermute | solution.py:90
  24.3 11.8 %collective-permute-start.2 = (bf16[64,1024]{1,0:T(8,128)(2,1)S(1)}, bf16[64,1024]{1,0:T(8,128)(2,1)S(1)}, u32[]{:S(2)}, u32[]{:S(2)}) collective-permute-start(bf16[64,1024]{1,0:T(8,128)(2,1)S(1)} %slice.57), channel_id=1, source_target_pairs={{0,2},{1,3},{2,4},{3,5},{4,6},{5,7},{6,0},{7,1},{8,10},{9,11},{10,... | collective-permute-start | bytes 393224 | tf_op jit(solution)/shard_map/ppermute | solution.py:86
  26.5 9.7 %collective-permute-start.3 = (bf16[64,1024]{1,0:T(8,128)(2,1)S(1)}, bf16[64,1024]{1,0:T(8,128)(2,1)S(1)}, u32[]{:S(2)}, u32[]{:S(2)}) collective-permute-start(bf16[64,1024]{1,0:T(8,128)(2,1)S(1)} %slice.58), channel_id=1, source_target_pairs={{2,0},{3,1},{4,2},{5,3},{6,4},{7,5},{0,6},{1,7},{10,8},{11,9},{12,... | collective-permute-start | bytes 393224 | tf_op jit(solution)/shard_map/ppermute | solution.py:87
  32.1 12.6 %all-to-all-start = ((bf16[128,8,128]{2,0,1:T(8,128)(2,1)}), bf16[128,8,128]{2,0,1:T(8,128)(2,1)S(1)}, u32[]{:S(2)}, u32[]{:S(2)}) async-start(bf16[128,8,128]{2,0,1:T(8,128)(2,1)} %copy_bitcast_fusion.1), calls=%async_computation | async-start | bytes 524288 | tf_op jit(solution)/shard_map/all_to_all | solution.py:316
  36.2 8.5 %collective-permute-start.5 = (bf16[128,1024]{1,0:T(8,128)(2,1)S(1)}, bf16[128,1024]{1,0:T(8,128)(2,1)}, u32[]{:S(2)}, u32[]{:S(2)}) collective-permute-start(bf16[128,1024]{1,0:T(8,128)(2,1)S(1)} %constant_dynamic-update-slice_fusion.3.far), channel_id=1, source_target_pairs={{0,1},{1,0},{2,3},{3,2},{4,5},{5,4},{6,7},{7,6},{8,9},{9,8},{10,11... | collective-permute-start | bytes 786440 | tf_op jit(solution)/shard_map/ppermute | solution.py:91
  45.9 20.6 %copy-start.5 = (s32[3,8]{1,0:T(4,128)S(1)}, s32[3,8]{1,0:T(4,128)}, u32[]{:S(2)}) copy-start(s32[3,8]{1,0:T(4,128)} %param.9) | copy-start | bytes 292
  45.9 20.6 %copy-start.1 = (bf16[1024,128]{1,0:T(8,128)(2,1)S(1)}, bf16[1024,128]{1,0:T(8,128)(2,1)}, u32[]{:S(2)}) copy-start(bf16[1024,128]{1,0:T(8,128)(2,1)} %weights.1) | copy-start | bytes 786436
  47.7 22.6 %collective-permute-start.6 = (bf16[1024,256]{1,0:T(8,128)(2,1)S(1)}, bf16[1024,256]{1,0:T(8,128)(2,1)S(1)}, u32[]{:S(2)}, u32[]{:S(2)}) collective-permute-start(bf16[1024,256]{1,0:T(8,128)(2,1)S(1)} %project_far.1.own), channel_id=1, source_target_pairs={{0,128},{128,0},{8,136},{136,8},{16,144},{144,16},{24,152},{152,24... | collective-permute-start | bytes 1572872 | tf_op jit(solution)/shard_map/ppermute | solution.py:37
  55.2 30.4 %collective-permute-start.7 = (bf16[1024,256]{1,0:T(8,128)(2,1)S(1)}, bf16[1024,256]{1,0:T(8,128)(2,1)S(1)}, u32[]{:S(2)}, u32[]{:S(2)}) collective-permute-start(bf16[1024,256]{1,0:T(8,128)(2,1)S(1)} %project_far.1.own), channel_id=1, source_target_pairs={{0,256},{256,0},{8,264},{264,8},{16,272},{272,16},{24,280},{280,24... | collective-permute-start | bytes 1572872 | tf_op jit(solution)/shard_map/ppermute | solution.py:37
  63.4 22.2 %collective-permute-start.8 = (bf16[1024,256]{1,0:T(8,128)(2,1)S(1)}, bf16[1024,256]{1,0:T(8,128)(2,1)S(1)}, u32[]{:S(2)}, u32[]{:S(2)}) collective-permute-start(bf16[1024,256]{1,0:T(8,128)(2,1)S(1)} %project_far.1.own), channel_id=1, source_target_pairs={{0,8},{8,0},{16,24},{24,16},{32,40},{40,32},{48,56},{56,48},{64,72... | collective-permute-start | bytes 1572872 | tf_op jit(solution)/shard_map/ppermute | solution.py:37
  70.3 33.8 %copy-start.3 = (bf16[1024,128]{1,0:T(8,128)(2,1)S(1)}, bf16[1024,128]{1,0:T(8,128)(2,1)}, u32[]{:S(2)}) copy-start(bf16[1024,128]{1,0:T(8,128)(2,1)} %param.11) | copy-start | bytes 786436
  70.3 33.8 %copy-start.4 = (bf16[1024,128]{1,0:T(8,128)(2,1)S(1)}, bf16[1024,128]{1,0:T(8,128)(2,1)}, u32[]{:S(2)}) copy-start(bf16[1024,128]{1,0:T(8,128)(2,1)} %param.12) | copy-start | bytes 786436
  94.9 20.9 %collective-permute-start.9 = (bf16[1024,256]{1,0:T(8,128)(2,1)S(1)}, bf16[1024,256]{1,0:T(8,128)(2,1)S(1)}, u32[]{:S(2)}, u32[]{:S(2)}) collective-permute-start(bf16[1024,256]{1,0:T(8,128)(2,1)S(1)} %get-tuple-element.31), channel_id=1, source_target_pairs={{0,128},{128,0},{8,136},{136,8},{16,144},{144,16},{24,152},{152,24... | collective-permute-start | bytes 1572872 | tf_op jit(solution)/shard_map/ppermute | solution.py:37
  97.1 22.4 %collective-permute-start.10 = (bf16[1024,256]{1,0:T(8,128)(2,1)S(1)}, bf16[1024,256]{1,0:T(8,128)(2,1)S(1)}, u32[]{:S(2)}, u32[]{:S(2)}) collective-permute-start(bf16[1024,256]{1,0:T(8,128)(2,1)S(1)} %get-tuple-element.32), channel_id=1, source_target_pairs={{0,256},{256,0},{8,264},{264,8},{16,272},{272,16},{24,280},{280,24... | collective-permute-start | bytes 1572872 | tf_op jit(solution)/shard_map/ppermute | solution.py:37
  100.9 18.6 %collective-permute-start.11 = (bf16[1024,256]{1,0:T(8,128)(2,1)S(1)}, bf16[1024,256]{1,0:T(8,128)(2,1)S(1)}, u32[]{:S(2)}, u32[]{:S(2)}) collective-permute-start(bf16[1024,256]{1,0:T(8,128)(2,1)S(1)} %get-tuple-element.33), channel_id=1, source_target_pairs={{0,8},{8,0},{16,24},{24,16},{32,40},{40,32},{48,56},{56,48},{64,72... | collective-permute-start | bytes 1572872 | tf_op jit(solution)/shard_map/ppermute | solution.py:37
  124.5 16.7 %collective-permute-start.12 = (bf16[512,1024]{1,0:T(8,128)(2,1)S(1)}, bf16[512,1024]{1,0:T(8,128)(2,1)}, u32[]{:S(2)}, u32[]{:S(2)}) collective-permute-start(bf16[512,1024]{1,0:T(8,128)(2,1)S(1)} %get-tuple-element.44), channel_id=1, source_target_pairs={{0,1},{1,0},{2,3},{3,2},{4,5},{5,4},{6,7},{7,6},{8,9},{9,8},{10,11... | collective-permute-start | bytes 3145736 | tf_op jit(solution)/shard_map/ppermute | solution.py:65
  129.7 33.6 %all-to-all-start.2 = ((bf16[32,32,384]{2,1,0:T(8,128)(2,1)}), bf16[32,32,384]{2,1,0:T(8,128)(2,1)S(1)}, u32[]{:S(2)}, u32[]{:S(2)}) async-start(bf16[32,32,384]{2,1,0:T(8,128)(2,1)} %bitcast.7), calls=%async_computation.2 | async-start | bytes 1572864 | tf_op jit(solution)/shard_map/all_to_all | solution.py:62
  142.9 25.1 %collective-permute-start.13 = (bf16[64,1024]{1,0:T(8,128)(2,1)S(1)}, bf16[64,1024]{1,0:T(8,128)(2,1)S(1)}, u32[]{:S(2)}, u32[]{:S(2)}) collective-permute-start(bf16[64,1024]{1,0:T(8,128)(2,1)S(1)} %get-tuple-element.57), channel_id=1, source_target_pairs={{0,2},{1,3},{2,4},{3,5},{4,6},{5,7},{6,0},{7,1},{8,10},{9,11},{10,... | collective-permute-start | bytes 393224 | tf_op jit(solution)/shard_map/ppermute | solution.py:67
  145.1 23.0 %collective-permute-start.14 = (bf16[64,1024]{1,0:T(8,128)(2,1)S(1)}, bf16[64,1024]{1,0:T(8,128)(2,1)S(1)}, u32[]{:S(2)}, u32[]{:S(2)}) collective-permute-start(bf16[64,1024]{1,0:T(8,128)(2,1)S(1)} %get-tuple-element.56), channel_id=1, source_target_pairs={{2,0},{3,1},{4,2},{5,3},{6,4},{7,5},{0,6},{1,7},{10,8},{11,9},{12,... | collective-permute-start | bytes 393224 | tf_op jit(solution)/shard_map/ppermute | solution.py:68
  163.3 15.3 %all-to-all-start.1 = ((bf16[8,128,128]{2,1,0:T(8,128)(2,1)}), bf16[8,128,128]{2,1,0:T(8,128)(2,1)S(1)}, u32[]{:S(2)}, u32[]{:S(2)}) async-start(bf16[8,128,128]{2,1,0:T(8,128)(2,1)} %bitcast.5), calls=%async_computation.1 | async-start | bytes 524288 | tf_op jit(solution)/shard_map/all_to_all | solution.py:371
  168.2 10.5 %collective-permute-start.17 = (f32[32,384]{1,0:T(8,128)S(1)}, f32[32,384]{1,0:T(8,128)S(1)}, u32[]{:S(2)}, u32[]{:S(2)}) collective-permute-start(f32[32,384]{1,0:T(8,128)S(1)} %convert_reduce_fusion), channel_id=1, source_target_pairs={{0,256},{256,0},{8,264},{264,8},{16,272},{272,16},{24,280},{280,24... | collective-permute-start | bytes 147464 | tf_op jit(solution)/shard_map/ppermute | solution.py:37
  179.6 26.3 %all-to-all-start.3 = ((bf16[32,32,384]{2,1,0:T(8,128)(2,1)}), bf16[32,32,384]{2,1,0:T(8,128)(2,1)S(1)}, u32[]{:S(2)}, u32[]{:S(2)}) async-start(bf16[32,32,384]{2,1,0:T(8,128)(2,1)} %broadcast_in_dim.2), calls=%async_computation.3 | async-start | bytes 1572864 | tf_op jit(solution)/shard_map/all_to_all | solution.py:62
  184.9 10.2 %collective-permute-start.16 = (bf16[128,1024]{1,0:T(8,128)(2,1)S(1)}, bf16[128,1024]{1,0:T(8,128)(2,1)S(1)}, u32[]{:S(2)}, u32[]{:S(2)}) collective-permute-start(bf16[128,1024]{1,0:T(8,128)(2,1)S(1)} %pad_maximum_fusion.2), channel_id=1, source_target_pairs={{2,0},{3,1},{4,2},{5,3},{6,4},{7,5},{0,6},{1,7},{10,8},{11,9},{12,... | collective-permute-start | bytes 786440 | tf_op jit(solution)/shard_map/ppermute | solution.py:75
  189.8 11.1 %collective-permute-start.15 = (bf16[128,1024]{1,0:T(8,128)(2,1)S(1)}, bf16[128,1024]{1,0:T(8,128)(2,1)S(1)}, u32[]{:S(2)}, u32[]{:S(2)}) collective-permute-start(bf16[128,1024]{1,0:T(8,128)(2,1)S(1)} %pad_maximum_fusion.1), channel_id=1, source_target_pairs={{0,2},{1,3},{2,4},{3,5},{4,6},{5,7},{6,0},{7,1},{8,10},{9,11},{10,... | collective-permute-start | bytes 786440 | tf_op jit(solution)/shard_map/ppermute | solution.py:74

commit v4 on v3

--- a/solution.py
+++ b/solution.py
@@ -1,5 +1,3 @@
-import math
-
 import jax
 import jax.numpy as jnp
 from jax import lax
@@ -10,9 +8,8 @@
 HDIM = 64
 BLOCK = 128
 CORES = 2
-KERNEL_VMEM = 12 * 1024 * 1024
 FETCH_ORDER = (1, 2, 0)
-RETURN_ORDER = (0, 1, 2)
+LOAD_ORDER = (0, 2, 1)
 BF = jnp.bfloat16
 F32 = jnp.float32
 NN = (((1,), (0,)), ((), ()))
@@ -23,6 +20,10 @@
 ANY = pl.BlockSpec(memory_space=pl.ANY)
 
 
+def memory(mebibytes):
+    return pltpu.CompilerParams(vmem_limit_bytes=mebibytes * 1024 * 1024)
+
+
 def mm(a, b, dims):
     return lax.dot_general(a, b, dims, preferred_element_type=F32)
 
@@ -45,37 +46,25 @@
     return up, down, across
 
 
-def added(*terms):
-    return sum(term.astype(F32) for term in terms).astype(BF)
-
-
-def summed(weight_part, keep, give):
+def halves_of_nodes():
     count = lax.axis_size("nodes")
-    split = count // 2
-    groups = [list(range(split)), list(range(split, count))]
-    rows, width = weight_part.shape
-    up, down, across = neighbours()
-    step = keep.shape[0] // 4
-    half = step // 2
-
-    def exchange(block):
-        return lax.all_to_all(block, "nodes", 0, 0, axis_index_groups=groups, tiled=True)
-
-    spread = exchange(weight_part)
-    chip = added(keep, lax.ppermute(give, "heads", across))
-    mine, high, far, low = (chip[at * step : (at + 1) * step] for at in range(4))
-    from_low = lax.ppermute(far[:half], "heads", up)
-    from_high = lax.ppermute(far[half:], "heads", down)
-    spread, from_low, from_high = lax.optimization_barrier((spread, from_low, from_high))
-    share = jnp.sum(spread.reshape(split, rows // split, width).astype(F32), axis=0)
-    share = share + from_partner(share, "nodes", split.bit_length() - 1)
-    high = jnp.concatenate([added(high[:half], from_low), high[half:]], axis=0)
-    low = jnp.concatenate([low[:half], added(low[half:], from_high)], axis=0)
-    from_low = lax.ppermute(high, "heads", up)
-    from_high = lax.ppermute(low, "heads", down)
-    copies = jnp.broadcast_to(share.astype(BF)[None], (split,) + share.shape)
-    whole = exchange(copies.reshape(rows, width))
-    return whole.astype(F32), added(mine, from_low, from_high)
+    return [list(range(count // 2)), list(range(count // 2, count))]
+
+
+def exchange(block):
+    return lax.all_to_all(block, "nodes", 0, 0, axis_index_groups=halves_of_nodes(), tiled=True)
+
+
+def summed_here(spread):
+    members = lax.axis_size("nodes") // 2
+    share = jnp.sum(spread.reshape(members, -1, spread.shape[1]).astype(F32), axis=0)
+    return share + from_partner(share, "nodes", members.bit_length() - 1)
+
+
+def copies_of(share):
+    members = lax.axis_size("nodes") // 2
+    copies = jnp.broadcast_to(share.astype(BF)[None], (members,) + share.shape)
+    return copies.reshape(-1, share.shape[1])
 
 
 def gather_pieces(block):
@@ -122,7 +111,8 @@
     return jnp.concatenate([ones_where(order_column - base, columns) for base in bases], axis=1)
 
 
-def near_kernel(place, near, near_across, weights, order_column, pairs):
+def near_kernel(place, near, near_across, key_weight, value_weight, order_column, pairs):
+    weights = jnp.concatenate([key_weight[...], value_weight[...]], axis=1)
     share = near.shape[0] // 3
     devices = order_column.shape[0] // share
     picks, projected = [], []
@@ -130,17 +120,20 @@
         own = owners(place[0], flip)
         bases = [(own + step) % devices * share for step in (0, devices - CORES, CORES)]
         picks.append(picks_of(order_column[...], bases, share))
-        projected.append(mm(piece[...], weights[...], NN).astype(BF))
+        projected.append(mm(piece[...], weights, NN).astype(BF))
     picked = jnp.concatenate(picks, axis=1)
     pairs[...] = mm(picked, jnp.concatenate(projected, axis=0), NN).astype(BF)
 
 
-def far_kernel(place, far, far_across, weights, order_column, near_pairs, pairs):
+def far_kernel(
+    place, far, far_across, key_weight, value_weight, order_column, near_pairs, pairs
+):
+    weights = jnp.concatenate([key_weight[...], value_weight[...]], axis=1)
     share = far.shape[0]
     devices = order_column.shape[0] // share
     bases = [(owners(place[0], flip) + devices // 2) % devices * share for flip in (0, 1)]
     both = jnp.concatenate([far[...], far_across[...]], axis=0)
-    projected = mm(both, weights[...], NN).astype(BF)
+    projected = mm(both, weights, NN).astype(BF)
     picked = mm(picks_of(order_column[...], bases, share), projected, NN).astype(BF)
     pairs[...] = near_pairs[...] + picked
 
@@ -189,7 +182,7 @@
 ):
     rows = asks.shape[0]
     width = asks.shape[1] // 2
-    score_scale = 1.0 / math.sqrt(HDIM)
+    score_scale = HDIM**-0.5
     split_heads, join_heads = head_splitter(width)
 
     def one_block(block, carry):
@@ -198,12 +191,14 @@
             pl.ds(pl.multiple_of(slots[which, block] * BLOCK, BLOCK), BLOCK)
             for which in FETCH_ORDER
         ]
-        pairs = [source[place, :] for source, place in zip((own, one, two, three), places)]
+        loads = dict(zip(LOAD_ORDER, (one, two, three)))
+        sources = [own] + [loads[which] for which in FETCH_ORDER]
+        pairs = [source[place, :] for source, place in zip(sources, places)]
         keys = jnp.concatenate([pair[:, :width] for pair in pairs], axis=0)
         values = jnp.concatenate([pair[:, width:] for pair in pairs], axis=0)
-        query = split_heads(asks[here, :width])
+        query = split_heads(asks[here, :width] * score_scale)
         cotangent = split_heads(asks[here, width:])
-        scores = mm(query, keys, NT) * score_scale
+        scores = mm(query, keys, NT)
         peak = jnp.max(scores, axis=-1, keepdims=True)
         raised = jnp.exp(scores - peak)
         softmax = raised * (1.0 / jnp.sum(raised, axis=-1, keepdims=True))
@@ -211,8 +206,8 @@
         mixed[here, :] = join_heads(mm(weights_low, values, NN)).astype(BF)
         dprobs = mm(cotangent, values, NT)
         row_delta = jnp.sum(softmax * dprobs, axis=-1, keepdims=True)
-        dscores = (softmax * (dprobs - row_delta) * score_scale).astype(BF)
-        dquery[here, :] = join_heads(mm(dscores, keys, NN)).astype(BF)
+        dscores = (softmax * (dprobs - row_delta)).astype(BF)
+        dquery[here, :] = (join_heads(mm(dscores, keys, NN)) * score_scale).astype(BF)
         dkeys = mm(dscores, query, TN)
         dvalues = mm(weights_low, cotangent, TN)
         targets = (own_grads, one_grads, two_grads, three_grads)
@@ -222,7 +217,7 @@
             target[places[which], width:] = dvalues[part].astype(target.dtype)
         return carry
 
-    lax.fori_loop(0, rows // BLOCK, one_block, 0)
+    lax.fori_loop(0, rows // BLOCK, one_block, 0, unroll=4)
 
 
 def restore_kernel(mixed, order_row, mixed_nodes):
@@ -239,26 +234,24 @@
 
 
 def finish_kernel(
-    place,
     features,
-    weights,
     order_row,
-    dquery_nodes,
     query_part,
     own,
     first,
     second,
     third,
     weight_part,
-    keep,
-    give,
-    grad_nodes,
-    chosen,
+    pair_nodes,
+    part_held,
     own_held,
     others_held,
     arrived,
 ):
-    rows, width = dquery_nodes.shape
+    rows, pair_width = own.shape
+    width = pair_width // 2
+    early = pltpu.make_async_copy(query_part, weight_part.at[:, pl.ds(0, width)], arrived.at[4])
+    early.start()
     copies = [pltpu.make_async_copy(own, own_held, arrived.at[3])]
     for at, source in enumerate((first, second, third)):
         copies.append(pltpu.make_async_copy(source, others_held.at[at], arrived.at[at]))
@@ -271,29 +264,94 @@
     total = own_held[...]
     for at in range(3):
         total = total + others_held[at].astype(F32)
-    pair_nodes = mm(restore, total.astype(BF), NN).astype(BF)
-    weight_part[:, :width] = query_part[...]
-    weight_part[:, width:] = mm(features[...], pair_nodes, TN).astype(BF)
-    grad_nodes[:, :width] = dquery_nodes[...]
-    grad_nodes[:, width:] = pair_nodes
-    here = place[0]
-    core = here % CORES
+    pair_nodes[...] = mm(restore, total.astype(BF), NN).astype(BF)
+    part_held[...] = mm(features[...], pair_nodes[...], TN).astype(BF)
+    last = pltpu.make_async_copy(part_held, weight_part.at[:, pl.ds(width, 2 * width)], arrived.at[0])
+    last.start()
+    last.wait()
+    early.wait()
+
+
+def features_kernel(
+    place, dquery_nodes, pair_nodes, mixed_nodes, query_weight, key_weight, value_weight, keep, give, chosen
+):
+    rows, width = mixed_nodes.shape
+    depth = query_weight.shape[0]
+    weights = jnp.concatenate([query_weight[...], key_weight[...], value_weight[...]], axis=1)
     chips = keep.shape[0] // BLOCK
     devices = chips * CORES
     share = rows // devices
     for flip, target in ((0, keep), (1, give)):
-        own_row = here - core + (core + flip) % CORES
+        own = owners(place[0], flip)
         for step in range(chips):
-            at = pl.multiple_of((own_row + CORES * step) % devices * share, share)
-            chosen[step * share : (step + 1) * share, :] = grad_nodes[pl.ds(at, share), :]
-        target[...] = mm(chosen[...], weights[...], NT).astype(BF)
+            at = pl.multiple_of((own + CORES * step) % devices * share, share)
+            to = slice(step * share, (step + 1) * share)
+            chosen[to, :width] = dquery_nodes[pl.ds(at, share), :]
+            chosen[to, width:] = pair_nodes[pl.ds(at, share), :]
+            target[to, depth:] = mixed_nodes[pl.ds(at, share), :]
+        target[:, :depth] = mm(chosen[...], weights, NT).astype(BF)
+
+
+def total_of(*terms):
+    return sum(term.astype(F32) for term in terms).astype(BF)
+
+
+def far_rows_kernel(keep, got, to_high, to_low):
+    all_width = keep.shape[1]
+    depth = 2 * all_width - to_high.shape[1]
+    half = to_high.shape[0]
+    for at, target in ((4 * half, to_high), (5 * half, to_low)):
+        part = slice(at, at + half)
+        target[:, :depth] = total_of(keep[part, :depth], got[part, :depth])
+        target[:, depth:all_width] = keep[part, depth:]
+        target[:, all_width:] = got[part, depth:]
+
+
+def near_rows_kernel(keep, got, from_low, from_high, to_high, to_low):
+    all_width = keep.shape[1]
+    both_width = from_low.shape[1]
+    depth = 2 * all_width - both_width
+    half = from_low.shape[0]
+    for at, target, came, kept in ((2 * half, to_high, from_low, 0), (6 * half, to_low, from_high, half)):
+        for step in (0, half):
+            part = slice(at + step, at + step + half)
+            to = slice(step, step + half)
+            terms = [keep[part, :depth], got[part, :depth]]
+            if step == kept:
+                terms.append(came[:, :depth])
+            target[to, :depth] = total_of(*terms)
+            target[to, depth:all_width] = keep[part, depth:]
+            target[to, all_width:both_width] = got[part, depth:]
+        target[:half, both_width:] = came[:, depth:all_width]
+        target[half:, both_width:] = came[:, all_width:]
+
+
+def collect_kernel(place, keep, got, from_low, from_high, feature_grad, attended):
+    rows, depth = feature_grad.shape
+    width = keep.shape[1] - depth
+    half = rows // 2
+    devices = depth // width
+    feature_grad[...] = total_of(
+        keep[:rows, :depth], got[:rows, :depth], from_low[:, :depth], from_high[:, :depth]
+    )
+    for flip in (0, 1):
+        own = owners(place[0], flip)
+        start = depth + flip * width
+
+        def columns(step):
+            return pl.ds(pl.multiple_of((own + step) % devices * width, width), width)
+
+        attended[:, columns(0)] = (keep, got)[flip][:rows, depth:]
+        attended[:, columns(devices - CORES)] = from_low[:, start : start + width]
+        attended[:, columns(CORES)] = from_high[:, start : start + width]
+        part = slice(flip * half, (flip + 1) * half)
+        attended[:half, columns(devices // 2)] = from_low[part, depth + 2 * width :]
+        attended[half:, columns(devices // 2)] = from_high[part, depth + 2 * width :]
 
 
 def local(features, node_order, partners, query_weight, key_weight, value_weight, upstream):
     width = query_weight.shape[1]
     depth = query_weight.shape[0]
-    pair_weights = jnp.concatenate([key_weight, value_weight], axis=1)
-    stacked = jnp.concatenate([query_weight, pair_weights], axis=1)
     rows = node_order.shape[0]
     blocks = rows // BLOCK
     slots = partners % blocks
@@ -301,7 +359,8 @@
     order_row = node_order.reshape(1, rows)
     levels = lax.axis_size("nodes").bit_length() - 1
     swap_bits = (0, levels - 2, levels - 1)
-    params = pltpu.CompilerParams(vmem_limit_bytes=KERNEL_VMEM)
+    params = memory(12)
+    up, down, across = neighbours()
     place = lax.axis_index("heads").astype(jnp.int32).reshape(1)
 
     def shape(*dims, dtype=BF):
@@ -319,21 +378,21 @@
     near_pairs = pl.pallas_call(
         near_kernel,
         out_shape=shape(rows, 2 * width),
-        in_specs=[SMEM] + [VMEM] * 4,
+        in_specs=[SMEM] + [VMEM] * 5,
         out_specs=VMEM,
         compiler_params=params,
         name="project_near",
-    )(place, near, near_across, pair_weights, order_column)
+    )(place, near, near_across, key_weight, value_weight, order_column)
     far_across, arriving = lax.optimization_barrier((far_across, arriving))
     pairs = pl.pallas_call(
         far_kernel,
         out_shape=shape(rows, 2 * width),
-        in_specs=[SMEM] + [VMEM] * 5,
+        in_specs=[SMEM] + [VMEM] * 6,
         out_specs=VMEM,
         compiler_params=params,
         name="project_far",
-    )(place, far, far_across, pair_weights, order_column, near_pairs)
-    others = swapped([pairs] * 3)
+    )(place, far, far_across, key_weight, value_weight, order_column, near_pairs)
+    others = [from_partner(pairs, "nodes", swap_bits[which]) for which in LOAD_ORDER]
     gathered, asks = pl.pallas_call(
         order_kernel,
         out_shape=(shape(rows, depth), shape(rows, 2 * width)),
@@ -363,12 +422,10 @@
         out_shape=shape(rows, width),
         in_specs=[VMEM] * 2,
         out_specs=VMEM,
-        compiler_params=params,
+        compiler_params=memory(8),
         name="restore",
     )(mixed, order_row)
     returned = swapped(sent)
-    mixed_nodes, *returned = lax.optimization_barrier((mixed_nodes, *returned))
-    attended = lax.all_to_all(mixed_nodes, "heads", split_axis=0, concat_axis=1, tiled=True)
     dquery_nodes, query_part = pl.pallas_call(
         query_kernel,
         out_shape=(shape(rows, width), shape(depth, width)),
@@ -377,33 +434,69 @@
         compiler_params=params,
         name="query_grads",
     )(gathered, order_row, dquery)
-    weight_part, keep, give = pl.pallas_call(
+    weight_part, pair_nodes = pl.pallas_call(
         finish_kernel,
-        out_shape=(
-            shape(depth, 3 * width),
-            shape(rows // CORES, depth),
-            shape(rows // CORES, depth),
-        ),
-        in_specs=[SMEM] + [VMEM] * 5 + [ANY] * 4,
-        out_specs=(VMEM,) * 3,
+        out_shape=(shape(depth, 3 * width), shape(rows, 2 * width)),
+        in_specs=[VMEM] * 3 + [ANY] * 4,
+        out_specs=(ANY, VMEM),
         scratch_shapes=[
-            pltpu.VMEM((rows, 3 * width), BF),
-            pltpu.VMEM((rows // CORES, 3 * width), BF),
+            pltpu.VMEM((depth, 2 * width), BF),
             pltpu.VMEM((rows, 2 * width), F32),
             pltpu.VMEM((3, rows, 2 * width), BF),
-            pltpu.SemaphoreType.DMA((4,)),
+            pltpu.SemaphoreType.DMA((5,)),
         ],
         compiler_params=params,
         name="finish",
-    )(place, gathered, stacked, order_row, dquery_nodes, query_part, own_grads, *[returned[at] for at in RETURN_ORDER])
-    weight_grads, feature_grad = summed(weight_part, keep, give)
-    return (
-        attended,
-        feature_grad,
-        weight_grads[:, :width],
-        weight_grads[:, width : 2 * width],
-        weight_grads[:, 2 * width :],
+    )(gathered, order_row, query_part, own_grads, *returned)
+    spread = exchange(weight_part)
+
+    share = rows // lax.axis_size("heads")
+    full = depth + width
+    keep, give = pl.pallas_call(
+        features_kernel,
+        out_shape=(shape(rows // CORES, full),) * 2,
+        in_specs=[SMEM] + [VMEM] * 6,
+        out_specs=(VMEM,) * 2,
+        scratch_shapes=[pltpu.VMEM((rows // CORES, 3 * width), BF)],
+        compiler_params=memory(6),
+        name="features",
+    )(place, dquery_nodes, pair_nodes, mixed_nodes, query_weight, key_weight, value_weight)
+    got = lax.ppermute(give, "heads", across)
+    to_high, to_low = pl.pallas_call(
+        far_rows_kernel,
+        out_shape=(shape(share // 2, full + width),) * 2,
+        in_specs=[VMEM] * 2,
+        out_specs=(VMEM,) * 2,
+        compiler_params=memory(3),
+        name="far_rows",
+    )(keep, got)
+    from_low = lax.ppermute(to_high, "heads", up)
+    from_high = lax.ppermute(to_low, "heads", down)
+    spread, from_low, from_high = lax.optimization_barrier((spread, from_low, from_high))
+    weight_share = summed_here(spread)
+    to_high, to_low = pl.pallas_call(
+        near_rows_kernel,
+        out_shape=(shape(share, full + 2 * width),) * 2,
+        in_specs=[VMEM] * 4,
+        out_specs=(VMEM,) * 2,
+        compiler_params=memory(3),
+        name="near_rows",
+    )(keep, got, from_low, from_high)
+    from_low = lax.ppermute(to_high, "heads", up)
+    from_high = lax.ppermute(to_low, "heads", down)
+    weight_grads = exchange(copies_of(weight_share))
+    feature_grad, attended = pl.pallas_call(
+        collect_kernel,
+        out_shape=(shape(share, depth),) * 2,
+        in_specs=[SMEM] + [VMEM] * 4,
+        out_specs=(VMEM,) * 2,
+        compiler_params=memory(3),
+        name="collect",
+    )(place, keep, got, from_low, from_high)
+    query_grad, key_grad, value_grad = (
+        weight_grads[:, at * width : (at + 1) * width].astype(F32) for at in range(3)
     )
+    return attended, feature_grad, query_grad, key_grad, value_grad
 
 
 def solution(mesh):

time: 210 us -> 204 us (0.971); the launches traced: 207 us -> 203 us
  local copies, waits for them, and re-layouts: 6.99 us -> 3.95 us
    all_to_all x3 -> x2, waiting for transfers between devices: 17.4 us -> 0.34 us  [exchange(): lax.all_to_all(block, 'nodes', 0, 0, axis_index_groups=halves_of_nodes(),...]
    ppermute x5, waiting for transfers between devices: 8.48 us -> 23.5 us  [the longest x2 14.1 us: local(): from_high = lax.ppermute(to_low, 'heads', down)]
    pallas_call x0 -> x4, Pallas kernels: none -> 2.45 us  [the longest x1 1.32 us: local(): pl.pallas_call(features_kernel, out_shape=(shape(rows // CORES, full),) *...]
    ppermute x5, starting transfers between devices: 19 us -> 16.8 us  [the longest x2 9.02 us: local(): from_high = lax.ppermute(to_low, 'heads', down)]
    all_to_all x3 -> x2, starting transfers between devices: 21.4 us -> 23.5 us  [exchange(): lax.all_to_all(block, 'nodes', 0, 0, axis_index_groups=halves_of_nodes(),...]
  transfers between devices with their start and end apart: 22 -> 21, of which waited for: 12 -> 14; matrix products, arithmetic and copies ran while one was open for 4% -> 1% of each run, Pallas kernels for 4% -> 4%
where the time goes in v4:
time: 204 us; the launch traced here: 203 us
  starting transfers between devices  100 us (49%)
  waiting for transfers between devices  71.1 us (35%)
  Pallas kernels  23.5 us (12%)
  local copies, waits for them, and re-layouts  3.95 us (2%)
  other arithmetic  3.55 us (2%)
    ppermute x7, waiting for transfers between devices, from_partner(): return lax.ppermute(block, axis, route)  32.9 us
    ppermute x7, starting transfers between devices, from_partner(): return lax.ppermute(block, axis, route)  32.2 us
    all_to_all x2, starting transfers between devices, exchange(): lax.all_to_all(block, 'nodes', 0, 0, axis_index_groups=halves_of_nodes(),...  23.5 us
    ppermute x2, waiting for transfers between devices, local(): from_high = lax.ppermute(to_low, 'heads', down)  14.1 us
    ppermute x2, starting transfers between devices, local(): from_high = lax.ppermute(to_low, 'heads', down)  9.02 us
    pallas_call x1, Pallas kernels, local(): pl.pallas_call(attend_kernel, out_shape=(shape(rows, width), shape(rows,...  8.3 us
    ppermute x1, waiting for transfers between devices, gather_pieces(): from_high = lax.ppermute(block, 'heads', down)  7.13 us
    ppermute x2, waiting for transfers between devices, local(): from_low = lax.ppermute(to_high, 'heads', up)  6.99 us
  transfers between devices with their start and end apart: 21, of which 14 were waited for; matrix products, arithmetic and copies ran while one was open for 1% of the time, Pallas kernels for 4%

profile of v4, /device:TPU:1, one launch (start us, length us, event | category | flops | bytes accessed | tf_op | source)
XLA Modules:
  0.0 203.4 jit_solution(7012580041107331514)
XLA Ops:
  0.6 5.0 %collective-permute-start = (bf16[128,1024]{1,0:T(8,128)(2,1)}, bf16[128,1024]{1,0:T(8,128)(2,1)S(1)}, u32[]{:S(2)}, u32[]{:S(2)}) collective-permute-start(bf16[128,1024]{1,0:T(8,128)(2,1)} %param.7), channel_id=1, source_target_pairs={{0,2},{1,3},{2,4},{3,5},{4,6},{5,7},{6,0},{7,1},{8,10},{9,11},{10,... | collective-permute-start | bytes 786440 | tf_op jit(solution)/shard_map/ppermute | solution.py:73
  5.6 5.5 %collective-permute-start.1 = (bf16[128,1024]{1,0:T(8,128)(2,1)}, bf16[128,1024]{1,0:T(8,128)(2,1)S(1)}, u32[]{:S(2)}, u32[]{:S(2)}) collective-permute-start(bf16[128,1024]{1,0:T(8,128)(2,1)} %param.7), channel_id=1, source_target_pairs={{2,0},{3,1},{4,2},{5,3},{6,4},{7,5},{0,6},{1,7},{10,8},{11,9},{12,... | collective-permute-start | bytes 786440 | tf_op jit(solution)/shard_map/ppermute | solution.py:74
  11.2 1.0 constant_dynamic-update-slice_fusion.2
  12.1 1.2 collective-permute-done
  13.4 7.1 %collective-permute-done.1 = bf16[128,1024]{1,0:T(8,128)(2,1)S(1)} collective-permute-done((bf16[128,1024]{1,0:T(8,128)(2,1)}, bf16[128,1024]{1,0:T(8,128)(2,1)S(1)}, u32[]{:S(2)}, u32[]{:S(2)}) %collective-permute-start.1) | collective-permute-done | bytes 262176 | tf_op jit(solution)/shard_map/ppermute | solution.py:74
  20.5 3.7 %collective-permute-start.4 = (bf16[384,1024]{1,0:T(8,128)(2,1)S(1)}, bf16[384,1024]{1,0:T(8,128)(2,1)S(1)}, u32[]{:S(2)}, u32[]{:S(2)}) collective-permute-start(bf16[384,1024]{1,0:T(8,128)(2,1)S(1)} %constant_dynamic-update-slice_fusion.near), channel_id=1, source_target_pairs={{0,1},{1,0},{2,3},{3,2},{4,5},{5,4},{6,7},{7,6},{8,9},{9,8},{10,11... | collective-permute-start | bytes 2359304 | tf_op jit(solution)/shard_map/ppermute | solution.py:79
  24.3 2.4 %collective-permute-start.2 = (bf16[64,1024]{1,0:T(8,128)(2,1)S(1)}, bf16[64,1024]{1,0:T(8,128)(2,1)S(1)}, u32[]{:S(2)}, u32[]{:S(2)}) collective-permute-start(bf16[64,1024]{1,0:T(8,128)(2,1)S(1)} %slice.20), channel_id=1, source_target_pairs={{0,2},{1,3},{2,4},{3,5},{4,6},{5,7},{6,0},{7,1},{8,10},{9,11},{10,... | collective-permute-start | bytes 393224 | tf_op jit(solution)/shard_map/ppermute | solution.py:75
  26.7 4.9 %collective-permute-start.3 = (bf16[64,1024]{1,0:T(8,128)(2,1)S(1)}, bf16[64,1024]{1,0:T(8,128)(2,1)S(1)}, u32[]{:S(2)}, u32[]{:S(2)}) collective-permute-start(bf16[64,1024]{1,0:T(8,128)(2,1)S(1)} %slice.21), channel_id=1, source_target_pairs={{2,0},{3,1},{4,2},{5,3},{6,4},{7,5},{0,6},{1,7},{10,8},{11,9},{12,... | collective-permute-start | bytes 393224 | tf_op jit(solution)/shard_map/ppermute | solution.py:76
  31.6 0.8 copy_bitcast_fusion
  32.3 3.9 %all-to-all-start = ((bf16[128,8,128]{2,0,1:T(8,128)(2,1)}), bf16[128,8,128]{2,0,1:T(8,128)(2,1)S(1)}, u32[]{:S(2)}, u32[]{:S(2)}) async-start(bf16[128,8,128]{2,0,1:T(8,128)(2,1)} %copy_bitcast_fusion), calls=%async_computation | async-start | bytes 524288 | tf_op jit(solution)/shard_map/all_to_all | solution.py:375
  36.4 2.4 %collective-permute-start.5 = (bf16[128,1024]{1,0:T(8,128)(2,1)S(1)}, bf16[128,1024]{1,0:T(8,128)(2,1)}, u32[]{:S(2)}, u32[]{:S(2)}) collective-permute-start(bf16[128,1024]{1,0:T(8,128)(2,1)S(1)} %constant_dynamic-update-slice_fusion.3.far), channel_id=1, source_target_pairs={{0,1},{1,0},{2,3},{3,2},{4,5},{5,4},{6,7},{7,6},{8,9},{9,8},{10,11... | collective-permute-start | bytes 786440 | tf_op jit(solution)/shard_map/ppermute | solution.py:80
  39.0 5.9 %all-to-all-done = bf16[128,8,128]{2,0,1:T(8,128)(2,1)S(1)} async-done(((bf16[128,8,128]{2,0,1:T(8,128)(2,1)}), bf16[128,8,128]{2,0,1:T(8,128)(2,1)S(1)}, u32[]{:S(2)}, u32[]{:S(2)}) %all-to-all-start) | async-done | bytes 262176 | tf_op jit(solution)/shard_map/all_to_all | solution.py:375
  44.9 1.1 project_near.1.near_pairs
  46.1 1.8 project_far.1.own
  47.9 7.5 %collective-permute-start.8 = (bf16[1024,256]{1,0:T(8,128)(2,1)S(1)}, bf16[1024,256]{1,0:T(8,128)(2,1)S(1)}, u32[]{:S(2)}, u32[]{:S(2)}) collective-permute-start(bf16[1024,256]{1,0:T(8,128)(2,1)S(1)} %project_far.1.own), channel_id=1, source_target_pairs={{0,128},{128,0},{8,136},{136,8},{16,144},{144,16},{24,152},{152,24... | collective-permute-start | bytes 1572872 | tf_op jit(solution)/shard_map/ppermute | solution.py:38
  55.4 8.2 %collective-permute-start.7 = (bf16[1024,256]{1,0:T(8,128)(2,1)S(1)}, bf16[1024,256]{1,0:T(8,128)(2,1)S(1)}, u32[]{:S(2)}, u32[]{:S(2)}) collective-permute-start(bf16[1024,256]{1,0:T(8,128)(2,1)S(1)} %project_far.1.own), channel_id=1, source_target_pairs={{0,256},{256,0},{8,264},{264,8},{16,272},{272,16},{24,280},{280,24... | collective-permute-start | bytes 1572872 | tf_op jit(solution)/shard_map/ppermute | solution.py:38
  63.6 3.1 %collective-permute-start.6 = (bf16[1024,256]{1,0:T(8,128)(2,1)S(1)}, bf16[1024,256]{1,0:T(8,128)(2,1)S(1)}, u32[]{:S(2)}, u32[]{:S(2)}) collective-permute-start(bf16[1024,256]{1,0:T(8,128)(2,1)S(1)} %project_far.1.own), channel_id=1, source_target_pairs={{0,8},{8,0},{16,24},{24,16},{32,40},{40,32},{48,56},{56,48},{64,72... | collective-permute-start | bytes 1572872 | tf_op jit(solution)/shard_map/ppermute | solution.py:38
  66.7 3.7 %order.1 = (bf16[1024,1024]{1,0:T(8,128)(2,1)S(1)}, bf16[1024,256]{1,0:T(8,128)(2,1)S(1)}) custom-call(s32[1]{0:T(128)} %bitcast.place, bf16[384,1024]{1,0:T(8,128)(2,1)S(1)} %constant_dynamic-update-slice_fusion.near, bf16[128,1024]{1,0:T(8,128)(2,1)S(1)} %constant_dynamic-update-slice_fusion.3.far, ...), custom_call_target="tpu_custom_call" | custom-call | tf_op jit(solution)/shard_map/order/pallas_call | solution.py:396
  70.5 15.3 %collective-permute-done.7.two = bf16[1024,256]{1,0:T(8,128)(2,1)S(1)} collective-permute-done((bf16[1024,256]{1,0:T(8,128)(2,1)S(1)}, bf16[1024,256]{1,0:T(8,128)(2,1)S(1)}, u32[]{:S(2)}, u32[]{:S(2)}) %collective-permute-start.7) | collective-permute-done | bytes 524320 | tf_op jit(solution)/shard_map/ppermute | solution.py:38
  85.8 8.3 %attend.1 = (bf16[1024,128]{1,0:T(8,128)(2,1)S(1)}, bf16[1024,128]{1,0:T(8,128)(2,1)S(1)}, f32[1024,256]{1,0:T(8,128)S(1)}, bf16[1024,256]{1,0:T(8,128)(2,1)S(1)...) custom-call(s32[3,8]{1,0:T(4,128)S(1)} %add_select_fusion.slots, ...), custom_call_target="tpu_custom_call" | custom-call | tf_op jit(solution)/shard_map/attend/pallas_call | solution.py:405
  94.1 2.1 %collective-permute-start.9 = (bf16[1024,256]{1,0:T(8,128)(2,1)S(1)}, bf16[1024,256]{1,0:T(8,128)(2,1)S(1)}, u32[]{:S(2)}, u32[]{:S(2)}) collective-permute-start(bf16[1024,256]{1,0:T(8,128)(2,1)S(1)} %get-tuple-element.38), channel_id=1, source_target_pairs={{0,128},{128,0},{8,136},{136,8},{16,144},{144,16},{24,152},{152,24... | collective-permute-start | bytes 1572872 | tf_op jit(solution)/shard_map/ppermute | solution.py:38
  96.2 3.9 %collective-permute-start.10 = (bf16[1024,256]{1,0:T(8,128)(2,1)S(1)}, bf16[1024,256]{1,0:T(8,128)(2,1)S(1)}, u32[]{:S(2)}, u32[]{:S(2)}) collective-permute-start(bf16[1024,256]{1,0:T(8,128)(2,1)S(1)} %get-tuple-element.39), channel_id=1, source_target_pairs={{0,256},{256,0},{8,264},{264,8},{16,272},{272,16},{24,280},{280,24... | collective-permute-start | bytes 1572872 | tf_op jit(solution)/shard_map/ppermute | solution.py:38
  100.1 3.3 %collective-permute-start.11 = (bf16[1024,256]{1,0:T(8,128)(2,1)S(1)}, bf16[1024,256]{1,0:T(8,128)(2,1)S(1)}, u32[]{:S(2)}, u32[]{:S(2)}) collective-permute-start(bf16[1024,256]{1,0:T(8,128)(2,1)S(1)} %get-tuple-element.40), channel_id=1, source_target_pairs={{0,8},{8,0},{16,24},{24,16},{32,40},{40,32},{48,56},{56,48},{64,72... | collective-permute-start | bytes 1572872 | tf_op jit(solution)/shard_map/ppermute | solution.py:38
  103.4 2.3 %query_grads.1 = (bf16[1024,128]{1,0:T(8,128)(2,1)S(1)}, bf16[1024,128]{1,0:T(8,128)(2,1)S(1)}) custom-call(bf16[1024,1024]{1,0:T(8,128)(2,1)S(1)} %get-tuple-element.32.features, s32[1,1024]{1,0:T(1,128)S(1)} %bitcast.19, bf16[1024,128]{1,0:T(8,128)(2,1)S(1)} %get-tuple-element.34.dquery), custom_call_target="tpu_custom_call" | custom-call | tf_op jit(solution)/shard_map/query_grads/pallas_call | solution.py:429
  105.7 9.3 %collective-permute-done.9.first = bf16[1024,256]{1,0:T(8,128)(2,1)S(1)} collective-permute-done((bf16[1024,256]{1,0:T(8,128)(2,1)S(1)}, bf16[1024,256]{1,0:T(8,128)(2,1)S(1)}, u32[]{:S(2)}, u32[]{:S(2)}) %collective-permute-start.9) | collective-permute-done | bytes 524320 | tf_op jit(solution)/shard_map/ppermute | solution.py:38
  115.0 3.7 %collective-permute-done.10.second = bf16[1024,256]{1,0:T(8,128)(2,1)S(1)} collective-permute-done((bf16[1024,256]{1,0:T(8,128)(2,1)S(1)}, bf16[1024,256]{1,0:T(8,128)(2,1)S(1)}, u32[]{:S(2)}, u32[]{:S(2)}) %collective-permute-start.10) | collective-permute-done | bytes 524320 | tf_op jit(solution)/shard_map/ppermute | solution.py:38
  118.7 3.1 %finish.1 = (bf16[1024,384]{1,0:T(8,128)(2,1)S(1)}, bf16[1024,256]{1,0:T(8,128)(2,1)S(1)}) custom-call(bf16[1024,1024]{1,0:T(8,128)(2,1)S(1)} %get-tuple-element.32.features, s32[1,1024]{1,0:T(1,128)S(1)} %bitcast.20, bf16[1024,128]{1,0:T(8,128)(2,1)S(1)} %get-tuple-element.36.query_part, f32[1024,256]{1,0:T(8,128)S(1)} %get-tuple-element.37.own, ...), custom_call_target="tpu_custom_call" | custom-call | tf_op jit(solution)/shard_map/finish/pallas_call | solution.py:437
  121.8 0.9 copy-done.5
  122.7 14.2 %all-to-all-start.1 = ((bf16[32,32,384]{2,1,0:T(8,128)(2,1)}), bf16[32,32,384]{2,1,0:T(8,128)(2,1)}, u32[]{:S(2)}, u32[]{:S(2)}) async-start(bf16[32,32,384]{2,1,0:T(8,128)(2,1)} %bitcast.17), calls=%async_computation.1 | async-start | bytes 1572864 | tf_op jit(solution)/shard_map/all_to_all | solution.py:55
  136.9 0.7 restore.1.mixed_nodes
  137.6 1.3 features.1
  139.0 2.7 %collective-permute-start.12 = (bf16[512,1152]{1,0:T(8,128)(2,1)S(1)}, bf16[512,1152]{1,0:T(8,128)(2,1)S(1)}, u32[]{:S(2)}, u32[]{:S(2)}) collective-permute-start(bf16[512,1152]{1,0:T(8,128)(2,1)S(1)} %get-tuple-element.44), channel_id=1, source_target_pairs={{0,1},{1,0},{2,3},{3,2},{4,5},{5,4},{6,7},{7,6},{8,9},{9,8},{10,11... | collective-permute-start | bytes 3538952 | tf_op jit(solution)/shard_map/ppermute | solution.py:464
  141.6 2.5 %collective-permute-done.12.got = bf16[512,1152]{1,0:T(8,128)(2,1)S(1)} collective-permute-done((bf16[512,1152]{1,0:T(8,128)(2,1)S(1)}, bf16[512,1152]{1,0:T(8,128)(2,1)S(1)}, u32[]{:S(2)}, u32[]{:S(2)}) %collective-permute-start.12) | collective-permute-done | bytes 1179680 | tf_op jit(solution)/shard_map/ppermute | solution.py:464
  144.2 2.2 %collective-permute-start.13 = (bf16[64,1280]{1,0:T(8,128)(2,1)S(1)}, bf16[64,1280]{1,0:T(8,128)(2,1)S(1)}, u32[]{:S(2)}, u32[]{:S(2)}) collective-permute-start(bf16[64,1280]{1,0:T(8,128)(2,1)S(1)} %get-tuple-element.46), channel_id=1, source_target_pairs={{0,2},{1,3},{2,4},{3,5},{4,6},{5,7},{6,0},{7,1},{8,10},{9,11},{10,... | collective-permute-start | bytes 491528 | tf_op jit(solution)/shard_map/ppermute | solution.py:473
  146.3 4.9 %collective-permute-start.14 = (bf16[64,1280]{1,0:T(8,128)(2,1)S(1)}, bf16[64,1280]{1,0:T(8,128)(2,1)S(1)}, u32[]{:S(2)}, u32[]{:S(2)}) collective-permute-start(bf16[64,1280]{1,0:T(8,128)(2,1)S(1)} %get-tuple-element.47), channel_id=1, source_target_pairs={{2,0},{3,1},{4,2},{5,3},{6,4},{7,5},{0,6},{1,7},{10,8},{11,9},{12,... | collective-permute-start | bytes 491528 | tf_op jit(solution)/shard_map/ppermute | solution.py:474
  151.3 2.2 %collective-permute-done.13.from_low = bf16[64,1280]{1,0:T(8,128)(2,1)S(1)} collective-permute-done((bf16[64,1280]{1,0:T(8,128)(2,1)S(1)}, bf16[64,1280]{1,0:T(8,128)(2,1)S(1)}, u32[]{:S(2)}, u32[]{:S(2)}) %collective-permute-start.13) | collective-permute-done | bytes 163872 | tf_op jit(solution)/shard_map/ppermute | solution.py:473
  153.4 4.2 %collective-permute-done.14.from_high = bf16[64,1280]{1,0:T(8,128)(2,1)S(1)} collective-permute-done((bf16[64,1280]{1,0:T(8,128)(2,1)S(1)}, bf16[64,1280]{1,0:T(8,128)(2,1)S(1)}, u32[]{:S(2)}, u32[]{:S(2)}) %collective-permute-start.14) | collective-permute-done | bytes 163872 | tf_op jit(solution)/shard_map/ppermute | solution.py:474
  157.9 1.3 convert_reduce_fusion
  159.2 4.2 %collective-permute-start.17 = (f32[32,384]{1,0:T(8,128)S(1)}, f32[32,384]{1,0:T(8,128)S(1)}, u32[]{:S(2)}, u32[]{:S(2)}) collective-permute-start(f32[32,384]{1,0:T(8,128)S(1)} %convert_reduce_fusion), channel_id=1, source_target_pairs={{0,256},{256,0},{8,264},{264,8},{16,272},{272,16},{24,280},{280,24... | collective-permute-start | bytes 147464 | tf_op jit(solution)/shard_map/ppermute | solution.py:38
  163.4 4.6 %collective-permute-done.17 = f32[32,384]{1,0:T(8,128)S(1)} collective-permute-done((f32[32,384]{1,0:T(8,128)S(1)}, f32[32,384]{1,0:T(8,128)S(1)}, u32[]{:S(2)}, u32[]{:S(2)}) %collective-permute-start.17) | collective-permute-done | bytes 49184 | tf_op jit(solution)/shard_map/ppermute | solution.py:38
  167.9 1.0 broadcast_in_dim.2
  168.9 9.3 %all-to-all-start.2 = ((bf16[32,32,384]{2,1,0:T(8,128)(2,1)}), bf16[32,32,384]{2,1,0:T(8,128)(2,1)}, u32[]{:S(2)}, u32[]{:S(2)}) async-start(bf16[32,32,384]{2,1,0:T(8,128)(2,1)} %broadcast_in_dim.2), calls=%async_computation.2 | async-start | bytes 1572864 | tf_op jit(solution)/shard_map/all_to_all | solution.py:55
  178.3 3.0 %collective-permute-start.15 = (bf16[128,1408]{1,0:T(8,128)(2,1)S(1)}, bf16[128,1408]{1,0:T(8,128)(2,1)S(1)}, u32[]{:S(2)}, u32[]{:S(2)}) collective-permute-start(bf16[128,1408]{1,0:T(8,128)(2,1)S(1)} %get-tuple-element.50), channel_id=1, source_target_pairs={{0,2},{1,3},{2,4},{3,5},{4,6},{5,7},{6,0},{7,1},{8,10},{9,11},{10,... | collective-permute-start | bytes 1081352 | tf_op jit(solution)/shard_map/ppermute | solution.py:485
  181.3 4.1 %collective-permute-start.16 = (bf16[128,1408]{1,0:T(8,128)(2,1)S(1)}, bf16[128,1408]{1,0:T(8,128)(2,1)S(1)}, u32[]{:S(2)}, u32[]{:S(2)}) collective-permute-start(bf16[128,1408]{1,0:T(8,128)(2,1)S(1)} %get-tuple-element.51), channel_id=1, source_target_pairs={{2,0},{3,1},{4,2},{5,3},{6,4},{7,5},{0,6},{1,7},{10,8},{11,9},{12,... | collective-permute-start | bytes 1081352 | tf_op jit(solution)/shard_map/ppermute | solution.py:486
  185.4 4.8 %collective-permute-done.15.from_low = bf16[128,1408]{1,0:T(8,128)(2,1)S(1)} collective-permute-done((bf16[128,1408]{1,0:T(8,128)(2,1)S(1)}, bf16[128,1408]{1,0:T(8,128)(2,1)S(1)}, u32[]{:S(2)}, u32[]{:S(2)}) %collective-permute-start.15) | collective-permute-done | bytes 360480 | tf_op jit(solution)/shard_map/ppermute | solution.py:485
  190.3 9.9 %collective-permute-done.16.from_high = bf16[128,1408]{1,0:T(8,128)(2,1)S(1)} collective-permute-done((bf16[128,1408]{1,0:T(8,128)(2,1)S(1)}, bf16[128,1408]{1,0:T(8,128)(2,1)S(1)}, u32[]{:S(2)}, u32[]{:S(2)}) %collective-permute-start.16) | collective-permute-done | bytes 360480 | tf_op jit(solution)/shard_map/ppermute | solution.py:486
  200.2 0.9 collect.1
  201.1 2.3 %slice_convert_fusion = (f32[1024,128]{1,0:T(8,128)}, f32[1024,128]{1,0:T(8,128)}, f32[1024,128]{1,0:T(8,128)}) fusion(bf16[1024,384]{1,0:T(8,128)(2,1)} %bitcast.8), kind=kLoop, calls=%fused_computation.2 | loop fusion | flops 393216 | bytes 2359296 | tf_op jit(solution)/shard_map/convert_element_type | solution.py:497
  (35 shorter events, 1.1 us)
Async XLA Ops:
  0.6 30.9 %copy-start = (bf16[128,1024]{1,0:T(8,128)(2,1)S(1)}, bf16[128,1024]{1,0:T(8,128)(2,1)}, u32[]{:S(2)}) copy-start(bf16[128,1024]{1,0:T(8,128)(2,1)} %param.13) | copy-start | bytes 786436
  0.6 12.7 %collective-permute-start = (bf16[128,1024]{1,0:T(8,128)(2,1)}, bf16[128,1024]{1,0:T(8,128)(2,1)S(1)}, u32[]{:S(2)}, u32[]{:S(2)}) collective-permute-start(bf16[128,1024]{1,0:T(8,128)(2,1)} %param.7), channel_id=1, source_target_pairs={{0,2},{1,3},{2,4},{3,5},{4,6},{5,7},{6,0},{7,1},{8,10},{9,11},{10,... | collective-permute-start | bytes 786440 | tf_op jit(solution)/shard_map/ppermute | solution.py:73
  5.6 14.9 %collective-permute-start.1 = (bf16[128,1024]{1,0:T(8,128)(2,1)}, bf16[128,1024]{1,0:T(8,128)(2,1)S(1)}, u32[]{:S(2)}, u32[]{:S(2)}) collective-permute-start(bf16[128,1024]{1,0:T(8,128)(2,1)} %param.7), channel_id=1, source_target_pairs={{2,0},{3,1},{4,2},{5,3},{6,4},{7,5},{0,6},{1,7},{10,8},{11,9},{12,... | collective-permute-start | bytes 786440 | tf_op jit(solution)/shard_map/ppermute | solution.py:74
  20.5 18.3 %copy-start.6 = (s32[1024]{0:T(1024)S(1)}, s32[1024]{0:T(1024)}, u32[]{:S(2)}) copy-start(s32[1024]{0:T(1024)} %param.8) | copy-start | bytes 12292
  20.5 24.4 %collective-permute-start.4 = (bf16[384,1024]{1,0:T(8,128)(2,1)S(1)}, bf16[384,1024]{1,0:T(8,128)(2,1)S(1)}, u32[]{:S(2)}, u32[]{:S(2)}) collective-permute-start(bf16[384,1024]{1,0:T(8,128)(2,1)S(1)} %constant_dynamic-update-slice_fusion.near), channel_id=1, source_target_pairs={{0,1},{1,0},{2,3},{3,2},{4,5},{5,4},{6,7},{7,6},{8,9},{9,8},{10,11... | collective-permute-start | bytes 2359304 | tf_op jit(solution)/shard_map/ppermute | solution.py:79
  24.3 20.7 %copy-start.1 = (bf16[1024,128]{1,0:T(8,128)(2,1)S(1)}, bf16[1024,128]{1,0:T(8,128)(2,1)}, u32[]{:S(2)}) copy-start(bf16[1024,128]{1,0:T(8,128)(2,1)} %key_weight.5) | copy-start | bytes 786436
  24.3 20.6 %copy-start.2 = (bf16[1024,128]{1,0:T(8,128)(2,1)S(1)}, bf16[1024,128]{1,0:T(8,128)(2,1)}, u32[]{:S(2)}) copy-start(bf16[1024,128]{1,0:T(8,128)(2,1)} %value_weight.5) | copy-start | bytes 786436
  24.3 11.9 %collective-permute-start.2 = (bf16[64,1024]{1,0:T(8,128)(2,1)S(1)}, bf16[64,1024]{1,0:T(8,128)(2,1)S(1)}, u32[]{:S(2)}, u32[]{:S(2)}) collective-permute-start(bf16[64,1024]{1,0:T(8,128)(2,1)S(1)} %slice.20), channel_id=1, source_target_pairs={{0,2},{1,3},{2,4},{3,5},{4,6},{5,7},{6,0},{7,1},{8,10},{9,11},{10,... | collective-permute-start | bytes 393224 | tf_op jit(solution)/shard_map/ppermute | solution.py:75
  26.7 9.7 %collective-permute-start.3 = (bf16[64,1024]{1,0:T(8,128)(2,1)S(1)}, bf16[64,1024]{1,0:T(8,128)(2,1)S(1)}, u32[]{:S(2)}, u32[]{:S(2)}) collective-permute-start(bf16[64,1024]{1,0:T(8,128)(2,1)S(1)} %slice.21), channel_id=1, source_target_pairs={{2,0},{3,1},{4,2},{5,3},{6,4},{7,5},{0,6},{1,7},{10,8},{11,9},{12,... | collective-permute-start | bytes 393224 | tf_op jit(solution)/shard_map/ppermute | solution.py:76
  32.3 12.6 %all-to-all-start = ((bf16[128,8,128]{2,0,1:T(8,128)(2,1)}), bf16[128,8,128]{2,0,1:T(8,128)(2,1)S(1)}, u32[]{:S(2)}, u32[]{:S(2)}) async-start(bf16[128,8,128]{2,0,1:T(8,128)(2,1)} %copy_bitcast_fusion), calls=%async_computation | async-start | bytes 524288 | tf_op jit(solution)/shard_map/all_to_all | solution.py:375
  36.4 8.5 %collective-permute-start.5 = (bf16[128,1024]{1,0:T(8,128)(2,1)S(1)}, bf16[128,1024]{1,0:T(8,128)(2,1)}, u32[]{:S(2)}, u32[]{:S(2)}) collective-permute-start(bf16[128,1024]{1,0:T(8,128)(2,1)S(1)} %constant_dynamic-update-slice_fusion.3.far), channel_id=1, source_target_pairs={{0,1},{1,0},{2,3},{3,2},{4,5},{5,4},{6,7},{7,6},{8,9},{9,8},{10,11... | collective-permute-start | bytes 786440 | tf_op jit(solution)/shard_map/ppermute | solution.py:80
  46.1 20.6 %copy-start.7 = (s32[3,8]{1,0:T(4,128)S(1)}, s32[3,8]{1,0:T(4,128)}, u32[]{:S(2)}) copy-start(s32[3,8]{1,0:T(4,128)} %param.9) | copy-start | bytes 292
  46.1 20.6 %copy-start.3 = (bf16[1024,128]{1,0:T(8,128)(2,1)S(1)}, bf16[1024,128]{1,0:T(8,128)(2,1)}, u32[]{:S(2)}) copy-start(bf16[1024,128]{1,0:T(8,128)(2,1)} %query_weight.1) | copy-start | bytes 786436
  47.9 22.5 %collective-permute-start.8 = (bf16[1024,256]{1,0:T(8,128)(2,1)S(1)}, bf16[1024,256]{1,0:T(8,128)(2,1)S(1)}, u32[]{:S(2)}, u32[]{:S(2)}) collective-permute-start(bf16[1024,256]{1,0:T(8,128)(2,1)S(1)} %project_far.1.own), channel_id=1, source_target_pairs={{0,128},{128,0},{8,136},{136,8},{16,144},{144,16},{24,152},{152,24... | collective-permute-start | bytes 1572872 | tf_op jit(solution)/shard_map/ppermute | solution.py:38
  55.4 30.4 %collective-permute-start.7 = (bf16[1024,256]{1,0:T(8,128)(2,1)S(1)}, bf16[1024,256]{1,0:T(8,128)(2,1)S(1)}, u32[]{:S(2)}, u32[]{:S(2)}) collective-permute-start(bf16[1024,256]{1,0:T(8,128)(2,1)S(1)} %project_far.1.own), channel_id=1, source_target_pairs={{0,256},{256,0},{8,264},{264,8},{16,272},{272,16},{24,280},{280,24... | collective-permute-start | bytes 1572872 | tf_op jit(solution)/shard_map/ppermute | solution.py:38
  63.6 22.2 %collective-permute-start.6 = (bf16[1024,256]{1,0:T(8,128)(2,1)S(1)}, bf16[1024,256]{1,0:T(8,128)(2,1)S(1)}, u32[]{:S(2)}, u32[]{:S(2)}) collective-permute-start(bf16[1024,256]{1,0:T(8,128)(2,1)S(1)} %project_far.1.own), channel_id=1, source_target_pairs={{0,8},{8,0},{16,24},{24,16},{32,40},{40,32},{48,56},{56,48},{64,72... | collective-permute-start | bytes 1572872 | tf_op jit(solution)/shard_map/ppermute | solution.py:38
  94.1 20.8 %collective-permute-start.9 = (bf16[1024,256]{1,0:T(8,128)(2,1)S(1)}, bf16[1024,256]{1,0:T(8,128)(2,1)S(1)}, u32[]{:S(2)}, u32[]{:S(2)}) collective-permute-start(bf16[1024,256]{1,0:T(8,128)(2,1)S(1)} %get-tuple-element.38), channel_id=1, source_target_pairs={{0,128},{128,0},{8,136},{136,8},{16,144},{144,16},{24,152},{152,24... | collective-permute-start | bytes 1572872 | tf_op jit(solution)/shard_map/ppermute | solution.py:38
  96.2 22.4 %collective-permute-start.10 = (bf16[1024,256]{1,0:T(8,128)(2,1)S(1)}, bf16[1024,256]{1,0:T(8,128)(2,1)S(1)}, u32[]{:S(2)}, u32[]{:S(2)}) collective-permute-start(bf16[1024,256]{1,0:T(8,128)(2,1)S(1)} %get-tuple-element.39), channel_id=1, source_target_pairs={{0,256},{256,0},{8,264},{264,8},{16,272},{272,16},{24,280},{280,24... | collective-permute-start | bytes 1572872 | tf_op jit(solution)/shard_map/ppermute | solution.py:38
  100.1 18.6 %collective-permute-start.11 = (bf16[1024,256]{1,0:T(8,128)(2,1)S(1)}, bf16[1024,256]{1,0:T(8,128)(2,1)S(1)}, u32[]{:S(2)}, u32[]{:S(2)}) collective-permute-start(bf16[1024,256]{1,0:T(8,128)(2,1)S(1)} %get-tuple-element.40), channel_id=1, source_target_pairs={{0,8},{8,0},{16,24},{24,16},{32,40},{40,32},{48,56},{56,48},{64,72... | collective-permute-start | bytes 1572872 | tf_op jit(solution)/shard_map/ppermute | solution.py:38
  121.8 0.9 copy-start.5
  121.8 15.9 %copy-start.4 = (bf16[1024,128]{1,0:T(8,128)(2,1)S(1)}, bf16[1024,128]{1,0:T(8,128)(2,1)}, u32[]{:S(2)}) copy-start(bf16[1024,128]{1,0:T(8,128)(2,1)} %query_weight.1) | copy-start | bytes 786436
  122.7 35.3 %all-to-all-start.1 = ((bf16[32,32,384]{2,1,0:T(8,128)(2,1)}), bf16[32,32,384]{2,1,0:T(8,128)(2,1)}, u32[]{:S(2)}, u32[]{:S(2)}) async-start(bf16[32,32,384]{2,1,0:T(8,128)(2,1)} %bitcast.17), calls=%async_computation.1 | async-start | bytes 1572864 | tf_op jit(solution)/shard_map/all_to_all | solution.py:55
  139.0 5.1 %collective-permute-start.12 = (bf16[512,1152]{1,0:T(8,128)(2,1)S(1)}, bf16[512,1152]{1,0:T(8,128)(2,1)S(1)}, u32[]{:S(2)}, u32[]{:S(2)}) collective-permute-start(bf16[512,1152]{1,0:T(8,128)(2,1)S(1)} %get-tuple-element.44), channel_id=1, source_target_pairs={{0,1},{1,0},{2,3},{3,2},{4,5},{5,4},{6,7},{7,6},{8,9},{9,8},{10,11... | collective-permute-start | bytes 3538952 | tf_op jit(solution)/shard_map/ppermute | solution.py:464
  144.2 9.3 %collective-permute-start.13 = (bf16[64,1280]{1,0:T(8,128)(2,1)S(1)}, bf16[64,1280]{1,0:T(8,128)(2,1)S(1)}, u32[]{:S(2)}, u32[]{:S(2)}) collective-permute-start(bf16[64,1280]{1,0:T(8,128)(2,1)S(1)} %get-tuple-element.46), channel_id=1, source_target_pairs={{0,2},{1,3},{2,4},{3,5},{4,6},{5,7},{6,0},{7,1},{8,10},{9,11},{10,... | collective-permute-start | bytes 491528 | tf_op jit(solution)/shard_map/ppermute | solution.py:473
  146.3 11.3 %collective-permute-start.14 = (bf16[64,1280]{1,0:T(8,128)(2,1)S(1)}, bf16[64,1280]{1,0:T(8,128)(2,1)S(1)}, u32[]{:S(2)}, u32[]{:S(2)}) collective-permute-start(bf16[64,1280]{1,0:T(8,128)(2,1)S(1)} %get-tuple-element.47), channel_id=1, source_target_pairs={{2,0},{3,1},{4,2},{5,3},{6,4},{7,5},{0,6},{1,7},{10,8},{11,9},{12,... | collective-permute-start | bytes 491528 | tf_op jit(solution)/shard_map/ppermute | solution.py:474
  159.2 8.7 %collective-permute-start.17 = (f32[32,384]{1,0:T(8,128)S(1)}, f32[32,384]{1,0:T(8,128)S(1)}, u32[]{:S(2)}, u32[]{:S(2)}) collective-permute-start(f32[32,384]{1,0:T(8,128)S(1)} %convert_reduce_fusion), channel_id=1, source_target_pairs={{0,256},{256,0},{8,264},{264,8},{16,272},{272,16},{24,280},{280,24... | collective-permute-start | bytes 147464 | tf_op jit(solution)/shard_map/ppermute | solution.py:38
  168.9 32.2 %all-to-all-start.2 = ((bf16[32,32,384]{2,1,0:T(8,128)(2,1)}), bf16[32,32,384]{2,1,0:T(8,128)(2,1)}, u32[]{:S(2)}, u32[]{:S(2)}) async-start(bf16[32,32,384]{2,1,0:T(8,128)(2,1)} %broadcast_in_dim.2), calls=%async_computation.2 | async-start | bytes 1572864 | tf_op jit(solution)/shard_map/all_to_all | solution.py:55
  178.3 11.9 %collective-permute-start.15 = (bf16[128,1408]{1,0:T(8,128)(2,1)S(1)}, bf16[128,1408]{1,0:T(8,128)(2,1)S(1)}, u32[]{:S(2)}, u32[]{:S(2)}) collective-permute-start(bf16[128,1408]{1,0:T(8,128)(2,1)S(1)} %get-tuple-element.50), channel_id=1, source_target_pairs={{0,2},{1,3},{2,4},{3,5},{4,6},{5,7},{6,0},{7,1},{8,10},{9,11},{10,... | collective-permute-start | bytes 1081352 | tf_op jit(solution)/shard_map/ppermute | solution.py:485
  181.3 18.9 %collective-permute-start.16 = (bf16[128,1408]{1,0:T(8,128)(2,1)S(1)}, bf16[128,1408]{1,0:T(8,128)(2,1)S(1)}, u32[]{:S(2)}, u32[]{:S(2)}) collective-permute-start(bf16[128,1408]{1,0:T(8,128)(2,1)S(1)} %get-tuple-element.51), channel_id=1, source_target_pairs={{2,0},{3,1},{4,2},{5,3},{6,4},{7,5},{0,6},{1,7},{10,8},{11,9},{12,... | collective-permute-start | bytes 1081352 | tf_op jit(solution)/shard_map/ppermute | solution.py:486

commit v5 on v4

--- a/solution.py
+++ b/solution.py
@@ -67,17 +67,19 @@
     return copies.reshape(-1, share.shape[1])
 
 
-def gather_pieces(block):
+def gather_pieces(block, upstream):
     up, down, across = neighbours()
     half = block.shape[0] // 2
     from_low = lax.ppermute(block, "heads", up)
     from_high = lax.ppermute(block, "heads", down)
+    from_low, upstream = lax.optimization_barrier((from_low, upstream))
     far_low = lax.ppermute(from_low[:half], "heads", up)
     far_high = lax.ppermute(from_high[half:], "heads", down)
     near = jnp.concatenate([block, from_low, from_high], axis=0)
     far = jnp.concatenate([far_low, far_high], axis=0)
     near_across = lax.ppermute(near, "heads", across)
-    return near, far, near_across, lax.ppermute(far, "heads", across)
+    arriving = lax.all_to_all(upstream, "heads", split_axis=0, concat_axis=0, tiled=True)
+    return near, far, near_across, lax.ppermute(far, "heads", across), arriving
 
 
 def ones_where(rows_index, columns_index):
@@ -349,6 +351,12 @@
         attended[half:, columns(devices // 2)] = from_high[part, depth + 2 * width :]
 
 
+def widen_kernel(whole, *parts):
+    width = parts[0].shape[1]
+    for at, part in enumerate(parts):
+        part[...] = whole[:, at * width : (at + 1) * width].astype(F32)
+
+
 def local(features, node_order, partners, query_weight, key_weight, value_weight, upstream):
     width = query_weight.shape[1]
     depth = query_weight.shape[0]
@@ -372,9 +380,8 @@
             for block, which in zip(blocks_for, FETCH_ORDER)
         ]
 
-    arriving = lax.all_to_all(upstream, "heads", split_axis=1, concat_axis=0, tiled=True)
-    pieces = gather_pieces(features)
-    near, far, near_across, far_across = pieces
+    by_heads = upstream.reshape(-1, depth // width, width).swapaxes(0, 1).reshape(rows, width)
+    near, far, near_across, far_across, arriving = gather_pieces(features, by_heads)
     near_pairs = pl.pallas_call(
         near_kernel,
         out_shape=shape(rows, 2 * width),
@@ -493,9 +500,16 @@
         compiler_params=memory(3),
         name="collect",
     )(place, keep, got, from_low, from_high)
-    query_grad, key_grad, value_grad = (
-        weight_grads[:, at * width : (at + 1) * width].astype(F32) for at in range(3)
-    )
+    piece = depth // 4
+    query_grad, key_grad, value_grad = pl.pallas_call(
+        widen_kernel,
+        grid=(4,),
+        out_shape=(shape(depth, width, dtype=F32),) * 3,
+        in_specs=[pl.BlockSpec((piece, 3 * width), lambda at: (at, 0))],
+        out_specs=(pl.BlockSpec((piece, width), lambda at: (at, 0)),) * 3,
+        compiler_params=memory(3),
+        name="widen",
+    )(weight_grads)
     return attended, feature_grad, query_grad, key_grad, value_grad
 
 

time: 204 us -> 202 us (level)
  other arithmetic: 3.55 us -> 1.27 us
    all_to_all x1, waiting for transfers between devices: 5.9 us -> 3.55 us  [gather_pieces(): lax.all_to_all(upstream, 'heads', split_axis=0, concat_axis=0, tiled=True)]
    convert_element_type x1 -> x0, other arithmetic: 2.28 us -> none  [local(): weight_grads[:, at * width:(at + 1) * width].astype(F32)]
  transfers between devices with their start and end apart: 21 -> 21, of which waited for: 14 -> 16; matrix products, arithmetic and copies ran while one was open for 1% -> 1% of each run, Pallas kernels for 4% -> 4%
where the time goes in v5:
time: 202 us; the launch traced here: 201 us
  starting transfers between devices  100 us (50%)
  waiting for transfers between devices  70.1 us (35%)
  Pallas kernels  24.2 us (12%)
  local copies, waits for them, and re-layouts  3.98 us (2%)
    ppermute x7, waiting for transfers between devices, from_partner(): return lax.ppermute(block, axis, route)  33.6 us
    ppermute x7, starting transfers between devices, from_partner(): return lax.ppermute(block, axis, route)  32.2 us
    all_to_all x2, starting transfers between devices, exchange(): lax.all_to_all(block, 'nodes', 0, 0, axis_index_groups=halves_of_nodes(),...  23.3 us
    ppermute x2, waiting for transfers between devices, local(): from_high = lax.ppermute(to_low, 'heads', down)  14.1 us
    ppermute x2, starting transfers between devices, local(): from_high = lax.ppermute(to_low, 'heads', down)  9 us
    pallas_call x1, Pallas kernels, local(): pl.pallas_call(attend_kernel, out_shape=(shape(rows, width), shape(rows,...  8.29 us
    ppermute x1, waiting for transfers between devices, gather_pieces(): from_high = lax.ppermute(block, 'heads', down)  7.12 us
    ppermute x2, waiting for transfers between devices, local(): from_low = lax.ppermute(to_high, 'heads', up)  6.89 us
  transfers between devices with their start and end apart: 21, of which 16 were waited for; matrix products, arithmetic and copies ran while one was open for 1% of the time, Pallas kernels for 4%

profile of v5, /device:TPU:1, one launch (start us, length us, event | category | flops | bytes accessed | tf_op | source)
XLA Modules:
  0.0 200.6 jit_solution(16581645346946804988)
XLA Ops:
  0.6 5.0 %collective-permute-start = (bf16[128,1024]{1,0:T(8,128)(2,1)}, bf16[128,1024]{1,0:T(8,128)(2,1)S(1)}, u32[]{:S(2)}, u32[]{:S(2)}) collective-permute-start(bf16[128,1024]{1,0:T(8,128)(2,1)} %param.7), channel_id=1, source_target_pairs={{0,2},{1,3},{2,4},{3,5},{4,6},{5,7},{6,0},{7,1},{8,10},{9,11},{10,... | collective-permute-start | bytes 786440 | tf_op jit(solution)/shard_map/ppermute | solution.py:73
  5.6 5.5 %collective-permute-start.1 = (bf16[128,1024]{1,0:T(8,128)(2,1)}, bf16[128,1024]{1,0:T(8,128)(2,1)S(1)}, u32[]{:S(2)}, u32[]{:S(2)}) collective-permute-start(bf16[128,1024]{1,0:T(8,128)(2,1)} %param.7), channel_id=1, source_target_pairs={{2,0},{3,1},{4,2},{5,3},{6,4},{7,5},{0,6},{1,7},{10,8},{11,9},{12,... | collective-permute-start | bytes 786440 | tf_op jit(solution)/shard_map/ppermute | solution.py:74
  11.2 1.1 copy.15
  12.3 0.9 copy.16
  13.4 7.1 %collective-permute-done.1 = bf16[128,1024]{1,0:T(8,128)(2,1)S(1)} collective-permute-done((bf16[128,1024]{1,0:T(8,128)(2,1)}, bf16[128,1024]{1,0:T(8,128)(2,1)S(1)}, u32[]{:S(2)}, u32[]{:S(2)}) %collective-permute-start.1) | collective-permute-done | bytes 262176 | tf_op jit(solution)/shard_map/ppermute | solution.py:74
  20.5 3.9 %collective-permute-start.4 = (bf16[384,1024]{1,0:T(8,128)(2,1)S(1)}, bf16[384,1024]{1,0:T(8,128)(2,1)S(1)}, u32[]{:S(2)}, u32[]{:S(2)}) collective-permute-start(bf16[384,1024]{1,0:T(8,128)(2,1)S(1)} %constant_dynamic-update-slice_fusion.near), channel_id=1, source_target_pairs={{0,1},{1,0},{2,3},{3,2},{4,5},{5,4},{6,7},{7,6},{8,9},{9,8},{10,11... | collective-permute-start | bytes 2359304 | tf_op jit(solution)/shard_map/ppermute | solution.py:80
  24.4 2.2 %collective-permute-start.2 = (bf16[64,1024]{1,0:T(8,128)(2,1)S(1)}, bf16[64,1024]{1,0:T(8,128)(2,1)S(1)}, u32[]{:S(2)}, u32[]{:S(2)}) collective-permute-start(bf16[64,1024]{1,0:T(8,128)(2,1)S(1)} %slice.6), channel_id=1, source_target_pairs={{0,2},{1,3},{2,4},{3,5},{4,6},{5,7},{6,0},{7,1},{8,10},{9,11},{10,... | collective-permute-start | bytes 393224 | tf_op jit(solution)/shard_map/ppermute | solution.py:76
  26.7 4.9 %collective-permute-start.3 = (bf16[64,1024]{1,0:T(8,128)(2,1)S(1)}, bf16[64,1024]{1,0:T(8,128)(2,1)S(1)}, u32[]{:S(2)}, u32[]{:S(2)}) collective-permute-start(bf16[64,1024]{1,0:T(8,128)(2,1)S(1)} %slice.8), channel_id=1, source_target_pairs={{2,0},{3,1},{4,2},{5,3},{6,4},{7,5},{0,6},{1,7},{10,8},{11,9},{12,... | collective-permute-start | bytes 393224 | tf_op jit(solution)/shard_map/ppermute | solution.py:77
  31.5 3.9 %all-to-all-start = ((bf16[8,128,128]{2,1,0:T(8,128)(2,1)}), bf16[8,128,128]{2,1,0:T(8,128)(2,1)S(1)}, u32[]{:S(2)}, u32[]{:S(2)}) async-start(bf16[8,128,128]{2,1,0:T(8,128)(2,1)} %bitcast.4), calls=%async_computation | async-start | bytes 524288 | tf_op jit(solution)/shard_map/all_to_all | solution.py:81
  35.4 0.9 collective-permute-done.3
  36.4 2.4 %collective-permute-start.5 = (bf16[128,1024]{1,0:T(8,128)(2,1)S(1)}, bf16[128,1024]{1,0:T(8,128)(2,1)S(1)}, u32[]{:S(2)}, u32[]{:S(2)}) collective-permute-start(bf16[128,1024]{1,0:T(8,128)(2,1)S(1)} %constant_dynamic-update-slice_fusion.3.far), channel_id=1, source_target_pairs={{0,1},{1,0},{2,3},{3,2},{4,5},{5,4},{6,7},{7,6},{8,9},{9,8},{10,11... | collective-permute-start | bytes 786440 | tf_op jit(solution)/shard_map/ppermute | solution.py:82
  39.0 0.9 collective-permute-done.5.far_across
  40.6 3.6 %all-to-all-done = bf16[8,128,128]{2,1,0:T(8,128)(2,1)S(1)} async-done(((bf16[8,128,128]{2,1,0:T(8,128)(2,1)}), bf16[8,128,128]{2,1,0:T(8,128)(2,1)S(1)}, u32[]{:S(2)}, u32[]{:S(2)}) %all-to-all-start) | async-done | bytes 262176 | tf_op jit(solution)/shard_map/all_to_all | solution.py:81
  44.2 1.1 project_near.1.near_pairs
  45.4 0.8 project_far.1.own
  46.2 7.5 %collective-permute-start.8 = (bf16[1024,256]{1,0:T(8,128)(2,1)S(1)}, bf16[1024,256]{1,0:T(8,128)(2,1)S(1)}, u32[]{:S(2)}, u32[]{:S(2)}) collective-permute-start(bf16[1024,256]{1,0:T(8,128)(2,1)S(1)} %project_far.1.own), channel_id=1, source_target_pairs={{0,128},{128,0},{8,136},{136,8},{16,144},{144,16},{24,152},{152,24... | collective-permute-start | bytes 1572872 | tf_op jit(solution)/shard_map/ppermute | solution.py:38
  53.6 8.2 %collective-permute-start.7 = (bf16[1024,256]{1,0:T(8,128)(2,1)S(1)}, bf16[1024,256]{1,0:T(8,128)(2,1)S(1)}, u32[]{:S(2)}, u32[]{:S(2)}) collective-permute-start(bf16[1024,256]{1,0:T(8,128)(2,1)S(1)} %project_far.1.own), channel_id=1, source_target_pairs={{0,256},{256,0},{8,264},{264,8},{16,272},{272,16},{24,280},{280,24... | collective-permute-start | bytes 1572872 | tf_op jit(solution)/shard_map/ppermute | solution.py:38
  61.8 3.1 %collective-permute-start.6 = (bf16[1024,256]{1,0:T(8,128)(2,1)S(1)}, bf16[1024,256]{1,0:T(8,128)(2,1)S(1)}, u32[]{:S(2)}, u32[]{:S(2)}) collective-permute-start(bf16[1024,256]{1,0:T(8,128)(2,1)S(1)} %project_far.1.own), channel_id=1, source_target_pairs={{0,8},{8,0},{16,24},{24,16},{32,40},{40,32},{48,56},{56,48},{64,72... | collective-permute-start | bytes 1572872 | tf_op jit(solution)/shard_map/ppermute | solution.py:38
  65.0 3.0 %order.1 = (bf16[1024,1024]{1,0:T(8,128)(2,1)S(1)}, bf16[1024,256]{1,0:T(8,128)(2,1)S(1)}) custom-call(s32[1]{0:T(128)} %bitcast.place, bf16[384,1024]{1,0:T(8,128)(2,1)S(1)} %constant_dynamic-update-slice_fusion.near, bf16[128,1024]{1,0:T(8,128)(2,1)S(1)} %constant_dynamic-update-slice_fusion.3.far, ...), custom_call_target="tpu_custom_call" | custom-call | tf_op jit(solution)/shard_map/order/pallas_call | solution.py:403
  68.3 15.8 %collective-permute-done.7.two = bf16[1024,256]{1,0:T(8,128)(2,1)S(1)} collective-permute-done((bf16[1024,256]{1,0:T(8,128)(2,1)S(1)}, bf16[1024,256]{1,0:T(8,128)(2,1)S(1)}, u32[]{:S(2)}, u32[]{:S(2)}) %collective-permute-start.7) | collective-permute-done | bytes 524320 | tf_op jit(solution)/shard_map/ppermute | solution.py:38
  84.1 8.3 %attend.1 = (bf16[1024,128]{1,0:T(8,128)(2,1)S(1)}, bf16[1024,128]{1,0:T(8,128)(2,1)S(1)}, f32[1024,256]{1,0:T(8,128)S(1)}, bf16[1024,256]{1,0:T(8,128)(2,1)S(1)...) custom-call(s32[3,8]{1,0:T(4,128)S(1)} %add_select_fusion.slots, ...), custom_call_target="tpu_custom_call" | custom-call | tf_op jit(solution)/shard_map/attend/pallas_call | solution.py:412
  92.4 2.1 %collective-permute-start.9 = (bf16[1024,256]{1,0:T(8,128)(2,1)S(1)}, bf16[1024,256]{1,0:T(8,128)(2,1)S(1)}, u32[]{:S(2)}, u32[]{:S(2)}) collective-permute-start(bf16[1024,256]{1,0:T(8,128)(2,1)S(1)} %get-tuple-element.45), channel_id=1, source_target_pairs={{0,128},{128,0},{8,136},{136,8},{16,144},{144,16},{24,152},{152,24... | collective-permute-start | bytes 1572872 | tf_op jit(solution)/shard_map/ppermute | solution.py:38
  94.5 3.9 %collective-permute-start.10 = (bf16[1024,256]{1,0:T(8,128)(2,1)S(1)}, bf16[1024,256]{1,0:T(8,128)(2,1)S(1)}, u32[]{:S(2)}, u32[]{:S(2)}) collective-permute-start(bf16[1024,256]{1,0:T(8,128)(2,1)S(1)} %get-tuple-element.46), channel_id=1, source_target_pairs={{0,256},{256,0},{8,264},{264,8},{16,272},{272,16},{24,280},{280,24... | collective-permute-start | bytes 1572872 | tf_op jit(solution)/shard_map/ppermute | solution.py:38
  98.4 3.3 %collective-permute-start.11 = (bf16[1024,256]{1,0:T(8,128)(2,1)S(1)}, bf16[1024,256]{1,0:T(8,128)(2,1)S(1)}, u32[]{:S(2)}, u32[]{:S(2)}) collective-permute-start(bf16[1024,256]{1,0:T(8,128)(2,1)S(1)} %get-tuple-element.47), channel_id=1, source_target_pairs={{0,8},{8,0},{16,24},{24,16},{32,40},{40,32},{48,56},{56,48},{64,72... | collective-permute-start | bytes 1572872 | tf_op jit(solution)/shard_map/ppermute | solution.py:38
  101.7 2.3 %query_grads.1 = (bf16[1024,128]{1,0:T(8,128)(2,1)S(1)}, bf16[1024,128]{1,0:T(8,128)(2,1)S(1)}) custom-call(bf16[1024,1024]{1,0:T(8,128)(2,1)S(1)} %get-tuple-element.39.features, s32[1,1024]{1,0:T(1,128)S(1)} %bitcast.17, bf16[1024,128]{1,0:T(8,128)(2,1)S(1)} %get-tuple-element.41.dquery), custom_call_target="tpu_custom_call" | custom-call | tf_op jit(solution)/shard_map/query_grads/pallas_call | solution.py:436
  103.9 9.4 %collective-permute-done.9.first = bf16[1024,256]{1,0:T(8,128)(2,1)S(1)} collective-permute-done((bf16[1024,256]{1,0:T(8,128)(2,1)S(1)}, bf16[1024,256]{1,0:T(8,128)(2,1)S(1)}, u32[]{:S(2)}, u32[]{:S(2)}) %collective-permute-start.9) | collective-permute-done | bytes 524320 | tf_op jit(solution)/shard_map/ppermute | solution.py:38
  113.3 3.6 %collective-permute-done.10.second = bf16[1024,256]{1,0:T(8,128)(2,1)S(1)} collective-permute-done((bf16[1024,256]{1,0:T(8,128)(2,1)S(1)}, bf16[1024,256]{1,0:T(8,128)(2,1)S(1)}, u32[]{:S(2)}, u32[]{:S(2)}) %collective-permute-start.10) | collective-permute-done | bytes 524320 | tf_op jit(solution)/shard_map/ppermute | solution.py:38
  117.0 3.8 %finish.1 = (bf16[1024,384]{1,0:T(8,128)(2,1)}, bf16[1024,256]{1,0:T(8,128)(2,1)S(1)}) custom-call(bf16[1024,1024]{1,0:T(8,128)(2,1)S(1)} %get-tuple-element.39.features, s32[1,1024]{1,0:T(1,128)S(1)} %bitcast.18, bf16[1024,128]{1,0:T(8,128)(2,1)S(1)} %get-tuple-element.43.query_part, f32[1024,256]{1,0:T(8,128)S(1)} %get-tuple-element.44.own, ...), custom_call_target="tpu_custom_call" | custom-call | tf_op jit(solution)/shard_map/finish/pallas_call | solution.py:444
  120.8 14.2 %all-to-all-start.1 = ((bf16[32,32,384]{2,1,0:T(8,128)(2,1)}), bf16[32,32,384]{2,1,0:T(8,128)(2,1)}, u32[]{:S(2)}, u32[]{:S(2)}) async-start(bf16[32,32,384]{2,1,0:T(8,128)(2,1)} %bitcast.8), calls=%async_computation.1 | async-start | bytes 1572864 | tf_op jit(solution)/shard_map/all_to_all | solution.py:55
  135.0 0.7 restore.1.mixed_nodes
  135.7 1.3 features.1
  137.0 2.7 %collective-permute-start.12 = (bf16[512,1152]{1,0:T(8,128)(2,1)S(1)}, bf16[512,1152]{1,0:T(8,128)(2,1)S(1)}, u32[]{:S(2)}, u32[]{:S(2)}) collective-permute-start(bf16[512,1152]{1,0:T(8,128)(2,1)S(1)} %get-tuple-element.51), channel_id=1, source_target_pairs={{0,1},{1,0},{2,3},{3,2},{4,5},{5,4},{6,7},{7,6},{8,9},{9,8},{10,11... | collective-permute-start | bytes 3538952 | tf_op jit(solution)/shard_map/ppermute | solution.py:471
  139.7 2.5 %collective-permute-done.12.got = bf16[512,1152]{1,0:T(8,128)(2,1)S(1)} collective-permute-done((bf16[512,1152]{1,0:T(8,128)(2,1)S(1)}, bf16[512,1152]{1,0:T(8,128)(2,1)S(1)}, u32[]{:S(2)}, u32[]{:S(2)}) %collective-permute-start.12) | collective-permute-done | bytes 1179680 | tf_op jit(solution)/shard_map/ppermute | solution.py:471
  142.2 2.2 %collective-permute-start.13 = (bf16[64,1280]{1,0:T(8,128)(2,1)S(1)}, bf16[64,1280]{1,0:T(8,128)(2,1)S(1)}, u32[]{:S(2)}, u32[]{:S(2)}) collective-permute-start(bf16[64,1280]{1,0:T(8,128)(2,1)S(1)} %get-tuple-element.53), channel_id=1, source_target_pairs={{0,2},{1,3},{2,4},{3,5},{4,6},{5,7},{6,0},{7,1},{8,10},{9,11},{10,... | collective-permute-start | bytes 491528 | tf_op jit(solution)/shard_map/ppermute | solution.py:480
  144.4 4.9 %collective-permute-start.14 = (bf16[64,1280]{1,0:T(8,128)(2,1)S(1)}, bf16[64,1280]{1,0:T(8,128)(2,1)S(1)}, u32[]{:S(2)}, u32[]{:S(2)}) collective-permute-start(bf16[64,1280]{1,0:T(8,128)(2,1)S(1)} %get-tuple-element.54), channel_id=1, source_target_pairs={{2,0},{3,1},{4,2},{5,3},{6,4},{7,5},{0,6},{1,7},{10,8},{11,9},{12,... | collective-permute-start | bytes 491528 | tf_op jit(solution)/shard_map/ppermute | solution.py:481
  149.3 2.2 %collective-permute-done.13.from_low = bf16[64,1280]{1,0:T(8,128)(2,1)S(1)} collective-permute-done((bf16[64,1280]{1,0:T(8,128)(2,1)S(1)}, bf16[64,1280]{1,0:T(8,128)(2,1)S(1)}, u32[]{:S(2)}, u32[]{:S(2)}) %collective-permute-start.13) | collective-permute-done | bytes 163872 | tf_op jit(solution)/shard_map/ppermute | solution.py:480
  151.5 4.2 %collective-permute-done.14.from_high = bf16[64,1280]{1,0:T(8,128)(2,1)S(1)} collective-permute-done((bf16[64,1280]{1,0:T(8,128)(2,1)S(1)}, bf16[64,1280]{1,0:T(8,128)(2,1)S(1)}, u32[]{:S(2)}, u32[]{:S(2)}) %collective-permute-start.14) | collective-permute-done | bytes 163872 | tf_op jit(solution)/shard_map/ppermute | solution.py:481
  156.0 1.3 convert_reduce_fusion
  157.3 4.2 %collective-permute-start.17 = (f32[32,384]{1,0:T(8,128)S(1)}, f32[32,384]{1,0:T(8,128)S(1)}, u32[]{:S(2)}, u32[]{:S(2)}) collective-permute-start(f32[32,384]{1,0:T(8,128)S(1)} %convert_reduce_fusion), channel_id=1, source_target_pairs={{0,256},{256,0},{8,264},{264,8},{16,272},{272,16},{24,280},{280,24... | collective-permute-start | bytes 147464 | tf_op jit(solution)/shard_map/ppermute | solution.py:38
  161.4 4.6 %collective-permute-done.17 = f32[32,384]{1,0:T(8,128)S(1)} collective-permute-done((f32[32,384]{1,0:T(8,128)S(1)}, f32[32,384]{1,0:T(8,128)S(1)}, u32[]{:S(2)}, u32[]{:S(2)}) %collective-permute-start.17) | collective-permute-done | bytes 49184 | tf_op jit(solution)/shard_map/ppermute | solution.py:38
  166.0 1.0 broadcast_in_dim.2
  167.0 9.1 %all-to-all-start.2 = ((bf16[32,32,384]{2,1,0:T(8,128)(2,1)}), bf16[32,32,384]{2,1,0:T(8,128)(2,1)S(1)}, u32[]{:S(2)}, u32[]{:S(2)}) async-start(bf16[32,32,384]{2,1,0:T(8,128)(2,1)} %broadcast_in_dim.2), calls=%async_computation.2 | async-start | bytes 1572864 | tf_op jit(solution)/shard_map/all_to_all | solution.py:55
  176.3 3.0 %collective-permute-start.15 = (bf16[128,1408]{1,0:T(8,128)(2,1)S(1)}, bf16[128,1408]{1,0:T(8,128)(2,1)S(1)}, u32[]{:S(2)}, u32[]{:S(2)}) collective-permute-start(bf16[128,1408]{1,0:T(8,128)(2,1)S(1)} %get-tuple-element.57), channel_id=1, source_target_pairs={{0,2},{1,3},{2,4},{3,5},{4,6},{5,7},{6,0},{7,1},{8,10},{9,11},{10,... | collective-permute-start | bytes 1081352 | tf_op jit(solution)/shard_map/ppermute | solution.py:492
  179.3 4.1 %collective-permute-start.16 = (bf16[128,1408]{1,0:T(8,128)(2,1)S(1)}, bf16[128,1408]{1,0:T(8,128)(2,1)S(1)}, u32[]{:S(2)}, u32[]{:S(2)}) collective-permute-start(bf16[128,1408]{1,0:T(8,128)(2,1)S(1)} %get-tuple-element.58), channel_id=1, source_target_pairs={{2,0},{3,1},{4,2},{5,3},{6,4},{7,5},{0,6},{1,7},{10,8},{11,9},{12,... | collective-permute-start | bytes 1081352 | tf_op jit(solution)/shard_map/ppermute | solution.py:493
  183.4 4.7 %collective-permute-done.15.from_low = bf16[128,1408]{1,0:T(8,128)(2,1)S(1)} collective-permute-done((bf16[128,1408]{1,0:T(8,128)(2,1)S(1)}, bf16[128,1408]{1,0:T(8,128)(2,1)S(1)}, u32[]{:S(2)}, u32[]{:S(2)}) %collective-permute-start.15) | collective-permute-done | bytes 360480 | tf_op jit(solution)/shard_map/ppermute | solution.py:492
  188.1 9.9 %collective-permute-done.16.from_high = bf16[128,1408]{1,0:T(8,128)(2,1)S(1)} collective-permute-done((bf16[128,1408]{1,0:T(8,128)(2,1)S(1)}, bf16[128,1408]{1,0:T(8,128)(2,1)S(1)}, u32[]{:S(2)}, u32[]{:S(2)}) %collective-permute-start.16) | collective-permute-done | bytes 360480 | tf_op jit(solution)/shard_map/ppermute | solution.py:493
  198.0 0.9 collect.1
  198.9 1.6 widen.1
  (36 shorter events, 2.1 us)
Async XLA Ops:
  0.6 12.5 %copy-start.6 = (bf16[128,1024]{1,0:T(8,128)(2,1)S(1)}, bf16[128,1024]{1,0:T(8,128)(2,1)}, u32[]{:S(2)}) copy-start(bf16[128,1024]{1,0:T(8,128)(2,1)} %param.7) | copy-start | bytes 786436
  0.6 12.7 %collective-permute-start = (bf16[128,1024]{1,0:T(8,128)(2,1)}, bf16[128,1024]{1,0:T(8,128)(2,1)S(1)}, u32[]{:S(2)}, u32[]{:S(2)}) collective-permute-start(bf16[128,1024]{1,0:T(8,128)(2,1)} %param.7), channel_id=1, source_target_pairs={{0,2},{1,3},{2,4},{3,5},{4,6},{5,7},{6,0},{7,1},{8,10},{9,11},{10,... | collective-permute-start | bytes 786440 | tf_op jit(solution)/shard_map/ppermute | solution.py:73
  5.6 14.9 %collective-permute-start.1 = (bf16[128,1024]{1,0:T(8,128)(2,1)}, bf16[128,1024]{1,0:T(8,128)(2,1)S(1)}, u32[]{:S(2)}, u32[]{:S(2)}) collective-permute-start(bf16[128,1024]{1,0:T(8,128)(2,1)} %param.7), channel_id=1, source_target_pairs={{2,0},{3,1},{4,2},{5,3},{6,4},{7,5},{0,6},{1,7},{10,8},{11,9},{12,... | collective-permute-start | bytes 786440 | tf_op jit(solution)/shard_map/ppermute | solution.py:74
  13.4 25.4 %copy-start.5 = (s32[1024]{0:T(1024)S(1)}, s32[1024]{0:T(1024)}, u32[]{:S(2)}) copy-start(s32[1024]{0:T(1024)} %param.8) | copy-start | bytes 12292
  20.5 23.6 %copy-start = (bf16[1024,128]{1,0:T(8,128)(2,1)S(1)}, bf16[1024,128]{1,0:T(8,128)(2,1)}, u32[]{:S(2)}) copy-start(bf16[1024,128]{1,0:T(8,128)(2,1)} %key_weight.5) | copy-start | bytes 786436
  20.5 23.6 %copy-start.1 = (bf16[1024,128]{1,0:T(8,128)(2,1)S(1)}, bf16[1024,128]{1,0:T(8,128)(2,1)}, u32[]{:S(2)}) copy-start(bf16[1024,128]{1,0:T(8,128)(2,1)} %value_weight.5) | copy-start | bytes 786436
  20.5 23.6 %collective-permute-start.4 = (bf16[384,1024]{1,0:T(8,128)(2,1)S(1)}, bf16[384,1024]{1,0:T(8,128)(2,1)S(1)}, u32[]{:S(2)}, u32[]{:S(2)}) collective-permute-start(bf16[384,1024]{1,0:T(8,128)(2,1)S(1)} %constant_dynamic-update-slice_fusion.near), channel_id=1, source_target_pairs={{0,1},{1,0},{2,3},{3,2},{4,5},{5,4},{6,7},{7,6},{8,9},{9,8},{10,11... | collective-permute-start | bytes 2359304 | tf_op jit(solution)/shard_map/ppermute | solution.py:80
  24.4 11.0 %collective-permute-start.2 = (bf16[64,1024]{1,0:T(8,128)(2,1)S(1)}, bf16[64,1024]{1,0:T(8,128)(2,1)S(1)}, u32[]{:S(2)}, u32[]{:S(2)}) collective-permute-start(bf16[64,1024]{1,0:T(8,128)(2,1)S(1)} %slice.6), channel_id=1, source_target_pairs={{0,2},{1,3},{2,4},{3,5},{4,6},{5,7},{6,0},{7,1},{8,10},{9,11},{10,... | collective-permute-start | bytes 393224 | tf_op jit(solution)/shard_map/ppermute | solution.py:76
  26.7 9.7 %collective-permute-start.3 = (bf16[64,1024]{1,0:T(8,128)(2,1)S(1)}, bf16[64,1024]{1,0:T(8,128)(2,1)S(1)}, u32[]{:S(2)}, u32[]{:S(2)}) collective-permute-start(bf16[64,1024]{1,0:T(8,128)(2,1)S(1)} %slice.8), channel_id=1, source_target_pairs={{2,0},{3,1},{4,2},{5,3},{6,4},{7,5},{0,6},{1,7},{10,8},{11,9},{12,... | collective-permute-start | bytes 393224 | tf_op jit(solution)/shard_map/ppermute | solution.py:77
  31.5 12.6 %all-to-all-start = ((bf16[8,128,128]{2,1,0:T(8,128)(2,1)}), bf16[8,128,128]{2,1,0:T(8,128)(2,1)S(1)}, u32[]{:S(2)}, u32[]{:S(2)}) async-start(bf16[8,128,128]{2,1,0:T(8,128)(2,1)} %bitcast.4), calls=%async_computation | async-start | bytes 524288 | tf_op jit(solution)/shard_map/all_to_all | solution.py:81
  36.4 3.5 %collective-permute-start.5 = (bf16[128,1024]{1,0:T(8,128)(2,1)S(1)}, bf16[128,1024]{1,0:T(8,128)(2,1)S(1)}, u32[]{:S(2)}, u32[]{:S(2)}) collective-permute-start(bf16[128,1024]{1,0:T(8,128)(2,1)S(1)} %constant_dynamic-update-slice_fusion.3.far), channel_id=1, source_target_pairs={{0,1},{1,0},{2,3},{3,2},{4,5},{5,4},{6,7},{7,6},{8,9},{9,8},{10,11... | collective-permute-start | bytes 786440 | tf_op jit(solution)/shard_map/ppermute | solution.py:82
  39.9 0.7 copy-start.3
  44.2 1.2 copy-start.4
  45.3 19.6 %copy-start.7 = (s32[3,8]{1,0:T(4,128)S(1)}, s32[3,8]{1,0:T(4,128)}, u32[]{:S(2)}) copy-start(s32[3,8]{1,0:T(4,128)} %param.9) | copy-start | bytes 292
  45.3 19.6 %copy-start.2 = (bf16[1024,128]{1,0:T(8,128)(2,1)S(1)}, bf16[1024,128]{1,0:T(8,128)(2,1)}, u32[]{:S(2)}) copy-start(bf16[1024,128]{1,0:T(8,128)(2,1)} %query_weight.1) | copy-start | bytes 786436
  46.2 22.1 %collective-permute-start.8 = (bf16[1024,256]{1,0:T(8,128)(2,1)S(1)}, bf16[1024,256]{1,0:T(8,128)(2,1)S(1)}, u32[]{:S(2)}, u32[]{:S(2)}) collective-permute-start(bf16[1024,256]{1,0:T(8,128)(2,1)S(1)} %project_far.1.own), channel_id=1, source_target_pairs={{0,128},{128,0},{8,136},{136,8},{16,144},{144,16},{24,152},{152,24... | collective-permute-start | bytes 1572872 | tf_op jit(solution)/shard_map/ppermute | solution.py:38
  53.6 30.4 %collective-permute-start.7 = (bf16[1024,256]{1,0:T(8,128)(2,1)S(1)}, bf16[1024,256]{1,0:T(8,128)(2,1)S(1)}, u32[]{:S(2)}, u32[]{:S(2)}) collective-permute-start(bf16[1024,256]{1,0:T(8,128)(2,1)S(1)} %project_far.1.own), channel_id=1, source_target_pairs={{0,256},{256,0},{8,264},{264,8},{16,272},{272,16},{24,280},{280,24... | collective-permute-start | bytes 1572872 | tf_op jit(solution)/shard_map/ppermute | solution.py:38
  61.8 22.2 %collective-permute-start.6 = (bf16[1024,256]{1,0:T(8,128)(2,1)S(1)}, bf16[1024,256]{1,0:T(8,128)(2,1)S(1)}, u32[]{:S(2)}, u32[]{:S(2)}) collective-permute-start(bf16[1024,256]{1,0:T(8,128)(2,1)S(1)} %project_far.1.own), channel_id=1, source_target_pairs={{0,8},{8,0},{16,24},{24,16},{32,40},{40,32},{48,56},{56,48},{64,72... | collective-permute-start | bytes 1572872 | tf_op jit(solution)/shard_map/ppermute | solution.py:38
  92.4 21.0 %collective-permute-start.9 = (bf16[1024,256]{1,0:T(8,128)(2,1)S(1)}, bf16[1024,256]{1,0:T(8,128)(2,1)S(1)}, u32[]{:S(2)}, u32[]{:S(2)}) collective-permute-start(bf16[1024,256]{1,0:T(8,128)(2,1)S(1)} %get-tuple-element.45), channel_id=1, source_target_pairs={{0,128},{128,0},{8,136},{136,8},{16,144},{144,16},{24,152},{152,24... | collective-permute-start | bytes 1572872 | tf_op jit(solution)/shard_map/ppermute | solution.py:38
  94.5 22.4 %collective-permute-start.10 = (bf16[1024,256]{1,0:T(8,128)(2,1)S(1)}, bf16[1024,256]{1,0:T(8,128)(2,1)S(1)}, u32[]{:S(2)}, u32[]{:S(2)}) collective-permute-start(bf16[1024,256]{1,0:T(8,128)(2,1)S(1)} %get-tuple-element.46), channel_id=1, source_target_pairs={{0,256},{256,0},{8,264},{264,8},{16,272},{272,16},{24,280},{280,24... | collective-permute-start | bytes 1572872 | tf_op jit(solution)/shard_map/ppermute | solution.py:38
  98.4 18.6 %collective-permute-start.11 = (bf16[1024,256]{1,0:T(8,128)(2,1)S(1)}, bf16[1024,256]{1,0:T(8,128)(2,1)S(1)}, u32[]{:S(2)}, u32[]{:S(2)}) collective-permute-start(bf16[1024,256]{1,0:T(8,128)(2,1)S(1)} %get-tuple-element.47), channel_id=1, source_target_pairs={{0,8},{8,0},{16,24},{24,16},{32,40},{40,32},{48,56},{56,48},{64,72... | collective-permute-start | bytes 1572872 | tf_op jit(solution)/shard_map/ppermute | solution.py:38
  120.8 35.2 %all-to-all-start.1 = ((bf16[32,32,384]{2,1,0:T(8,128)(2,1)}), bf16[32,32,384]{2,1,0:T(8,128)(2,1)}, u32[]{:S(2)}, u32[]{:S(2)}) async-start(bf16[32,32,384]{2,1,0:T(8,128)(2,1)} %bitcast.8), calls=%async_computation.1 | async-start | bytes 1572864 | tf_op jit(solution)/shard_map/all_to_all | solution.py:55
  137.0 5.1 %collective-permute-start.12 = (bf16[512,1152]{1,0:T(8,128)(2,1)S(1)}, bf16[512,1152]{1,0:T(8,128)(2,1)S(1)}, u32[]{:S(2)}, u32[]{:S(2)}) collective-permute-start(bf16[512,1152]{1,0:T(8,128)(2,1)S(1)} %get-tuple-element.51), channel_id=1, source_target_pairs={{0,1},{1,0},{2,3},{3,2},{4,5},{5,4},{6,7},{7,6},{8,9},{9,8},{10,11... | collective-permute-start | bytes 3538952 | tf_op jit(solution)/shard_map/ppermute | solution.py:471
  142.2 9.3 %collective-permute-start.13 = (bf16[64,1280]{1,0:T(8,128)(2,1)S(1)}, bf16[64,1280]{1,0:T(8,128)(2,1)S(1)}, u32[]{:S(2)}, u32[]{:S(2)}) collective-permute-start(bf16[64,1280]{1,0:T(8,128)(2,1)S(1)} %get-tuple-element.53), channel_id=1, source_target_pairs={{0,2},{1,3},{2,4},{3,5},{4,6},{5,7},{6,0},{7,1},{8,10},{9,11},{10,... | collective-permute-start | bytes 491528 | tf_op jit(solution)/shard_map/ppermute | solution.py:480
  144.4 11.2 %collective-permute-start.14 = (bf16[64,1280]{1,0:T(8,128)(2,1)S(1)}, bf16[64,1280]{1,0:T(8,128)(2,1)S(1)}, u32[]{:S(2)}, u32[]{:S(2)}) collective-permute-start(bf16[64,1280]{1,0:T(8,128)(2,1)S(1)} %get-tuple-element.54), channel_id=1, source_target_pairs={{2,0},{3,1},{4,2},{5,3},{6,4},{7,5},{0,6},{1,7},{10,8},{11,9},{12,... | collective-permute-start | bytes 491528 | tf_op jit(solution)/shard_map/ppermute | solution.py:481
  157.3 8.7 %collective-permute-start.17 = (f32[32,384]{1,0:T(8,128)S(1)}, f32[32,384]{1,0:T(8,128)S(1)}, u32[]{:S(2)}, u32[]{:S(2)}) collective-permute-start(f32[32,384]{1,0:T(8,128)S(1)} %convert_reduce_fusion), channel_id=1, source_target_pairs={{0,256},{256,0},{8,264},{264,8},{16,272},{272,16},{24,280},{280,24... | collective-permute-start | bytes 147464 | tf_op jit(solution)/shard_map/ppermute | solution.py:38
  167.0 32.0 %all-to-all-start.2 = ((bf16[32,32,384]{2,1,0:T(8,128)(2,1)}), bf16[32,32,384]{2,1,0:T(8,128)(2,1)S(1)}, u32[]{:S(2)}, u32[]{:S(2)}) async-start(bf16[32,32,384]{2,1,0:T(8,128)(2,1)} %broadcast_in_dim.2), calls=%async_computation.2 | async-start | bytes 1572864 | tf_op jit(solution)/shard_map/all_to_all | solution.py:55
  176.3 11.8 %collective-permute-start.15 = (bf16[128,1408]{1,0:T(8,128)(2,1)S(1)}, bf16[128,1408]{1,0:T(8,128)(2,1)S(1)}, u32[]{:S(2)}, u32[]{:S(2)}) collective-permute-start(bf16[128,1408]{1,0:T(8,128)(2,1)S(1)} %get-tuple-element.57), channel_id=1, source_target_pairs={{0,2},{1,3},{2,4},{3,5},{4,6},{5,7},{6,0},{7,1},{8,10},{9,11},{10,... | collective-permute-start | bytes 1081352 | tf_op jit(solution)/shard_map/ppermute | solution.py:492
  179.3 18.8 %collective-permute-start.16 = (bf16[128,1408]{1,0:T(8,128)(2,1)S(1)}, bf16[128,1408]{1,0:T(8,128)(2,1)S(1)}, u32[]{:S(2)}, u32[]{:S(2)}) collective-permute-start(bf16[128,1408]{1,0:T(8,128)(2,1)S(1)} %get-tuple-element.58), channel_id=1, source_target_pairs={{2,0},{3,1},{4,2},{5,3},{6,4},{7,5},{0,6},{1,7},{10,8},{11,9},{12,... | collective-permute-start | bytes 1081352 | tf_op jit(solution)/shard_map/ppermute | solution.py:493

commit v6 on v5

--- a/solution.py
+++ b/solution.py
@@ -219,7 +219,7 @@
             target[places[which], width:] = dvalues[part].astype(target.dtype)
         return carry
 
-    lax.fori_loop(0, rows // BLOCK, one_block, 0, unroll=4)
+    lax.fori_loop(0, rows // BLOCK, one_block, 0, unroll=8)
 
 
 def restore_kernel(mixed, order_row, mixed_nodes):
@@ -246,26 +246,17 @@
     weight_part,
     pair_nodes,
     part_held,
-    own_held,
-    others_held,
     arrived,
 ):
     rows, pair_width = own.shape
     width = pair_width // 2
-    early = pltpu.make_async_copy(query_part, weight_part.at[:, pl.ds(0, width)], arrived.at[4])
+    early = pltpu.make_async_copy(query_part, weight_part.at[:, pl.ds(0, width)], arrived.at[1])
     early.start()
-    copies = [pltpu.make_async_copy(own, own_held, arrived.at[3])]
-    for at, source in enumerate((first, second, third)):
-        copies.append(pltpu.make_async_copy(source, others_held.at[at], arrived.at[at]))
-    for copy in copies:
-        copy.start()
     node = lax.broadcasted_iota(jnp.int32, (rows, rows), 0)
     restore = ones_where(node, order_row[...])
-    for copy in copies:
-        copy.wait()
-    total = own_held[...]
-    for at in range(3):
-        total = total + others_held[at].astype(F32)
+    total = own[...]
+    for other in (first, second, third):
+        total = total + other[...].astype(F32)
     pair_nodes[...] = mm(restore, total.astype(BF), NN).astype(BF)
     part_held[...] = mm(features[...], pair_nodes[...], TN).astype(BF)
     last = pltpu.make_async_copy(part_held, weight_part.at[:, pl.ds(width, 2 * width)], arrived.at[0])
@@ -444,13 +435,11 @@
     weight_part, pair_nodes = pl.pallas_call(
         finish_kernel,
         out_shape=(shape(depth, 3 * width), shape(rows, 2 * width)),
-        in_specs=[VMEM] * 3 + [ANY] * 4,
+        in_specs=[VMEM] * 7,
         out_specs=(ANY, VMEM),
         scratch_shapes=[
             pltpu.VMEM((depth, 2 * width), BF),
-            pltpu.VMEM((rows, 2 * width), F32),
-            pltpu.VMEM((3, rows, 2 * width), BF),
-            pltpu.SemaphoreType.DMA((5,)),
+            pltpu.SemaphoreType.DMA((2,)),
         ],
         compiler_params=params,
         name="finish",

time: 202 us -> 201 us (level)
  no operation moved by 1% of the time
where the time goes in v6:
time: 201 us; the launch traced here: 200 us
  starting transfers between devices  100 us (50%)
  waiting for transfers between devices  70.1 us (35%)
  Pallas kernels  23.2 us (12%)
  local copies, waits for them, and re-layouts  3.98 us (2%)
    ppermute x7, waiting for transfers between devices, from_partner(): return lax.ppermute(block, axis, route)  33.6 us
    ppermute x7, starting transfers between devices, from_partner(): return lax.ppermute(block, axis, route)  32.2 us
    all_to_all x2, starting transfers between devices, exchange(): lax.all_to_all(block, 'nodes', 0, 0, axis_index_groups=halves_of_nodes(),...  23.3 us
    ppermute x2, waiting for transfers between devices, local(): from_high = lax.ppermute(to_low, 'heads', down)  14.1 us
    ppermute x2, starting transfers between devices, local(): from_high = lax.ppermute(to_low, 'heads', down)  9.01 us
    pallas_call x1, Pallas kernels, local(): pl.pallas_call(attend_kernel, out_shape=(shape(rows, width), shape(rows,...  8.1 us
    ppermute x1, waiting for transfers between devices, gather_pieces(): from_high = lax.ppermute(block, 'heads', down)  7.12 us
    ppermute x2, waiting for transfers between devices, local(): from_low = lax.ppermute(to_high, 'heads', up)  6.89 us
  transfers between devices with their start and end apart: 21, of which 16 were waited for; matrix products, arithmetic and copies ran while one was open for 1% of the time, Pallas kernels for 4%

profile of v6, /device:TPU:1, one launch (start us, length us, event | category | flops | bytes accessed | tf_op | source)
XLA Modules:
  0.0 199.7 jit_solution(10559033840516817549)
XLA Ops:
  0.6 5.0 %collective-permute-start = (bf16[128,1024]{1,0:T(8,128)(2,1)}, bf16[128,1024]{1,0:T(8,128)(2,1)S(1)}, u32[]{:S(2)}, u32[]{:S(2)}) collective-permute-start(bf16[128,1024]{1,0:T(8,128)(2,1)} %param.7), channel_id=1, source_target_pairs={{0,2},{1,3},{2,4},{3,5},{4,6},{5,7},{6,0},{7,1},{8,10},{9,11},{10,... | collective-permute-start | bytes 786440 | tf_op jit(solution)/shard_map/ppermute | solution.py:73
  5.6 5.5 %collective-permute-start.1 = (bf16[128,1024]{1,0:T(8,128)(2,1)}, bf16[128,1024]{1,0:T(8,128)(2,1)S(1)}, u32[]{:S(2)}, u32[]{:S(2)}) collective-permute-start(bf16[128,1024]{1,0:T(8,128)(2,1)} %param.7), channel_id=1, source_target_pairs={{2,0},{3,1},{4,2},{5,3},{6,4},{7,5},{0,6},{1,7},{10,8},{11,9},{12,... | collective-permute-start | bytes 786440 | tf_op jit(solution)/shard_map/ppermute | solution.py:74
  11.2 1.1 copy.15
  12.3 0.9 copy.16
  13.4 7.1 %collective-permute-done.1 = bf16[128,1024]{1,0:T(8,128)(2,1)S(1)} collective-permute-done((bf16[128,1024]{1,0:T(8,128)(2,1)}, bf16[128,1024]{1,0:T(8,128)(2,1)S(1)}, u32[]{:S(2)}, u32[]{:S(2)}) %collective-permute-start.1) | collective-permute-done | bytes 262176 | tf_op jit(solution)/shard_map/ppermute | solution.py:74
  20.5 3.9 %collective-permute-start.4 = (bf16[384,1024]{1,0:T(8,128)(2,1)S(1)}, bf16[384,1024]{1,0:T(8,128)(2,1)S(1)}, u32[]{:S(2)}, u32[]{:S(2)}) collective-permute-start(bf16[384,1024]{1,0:T(8,128)(2,1)S(1)} %constant_dynamic-update-slice_fusion.near), channel_id=1, source_target_pairs={{0,1},{1,0},{2,3},{3,2},{4,5},{5,4},{6,7},{7,6},{8,9},{9,8},{10,11... | collective-permute-start | bytes 2359304 | tf_op jit(solution)/shard_map/ppermute | solution.py:80
  24.4 2.2 %collective-permute-start.2 = (bf16[64,1024]{1,0:T(8,128)(2,1)S(1)}, bf16[64,1024]{1,0:T(8,128)(2,1)S(1)}, u32[]{:S(2)}, u32[]{:S(2)}) collective-permute-start(bf16[64,1024]{1,0:T(8,128)(2,1)S(1)} %slice.6), channel_id=1, source_target_pairs={{0,2},{1,3},{2,4},{3,5},{4,6},{5,7},{6,0},{7,1},{8,10},{9,11},{10,... | collective-permute-start | bytes 393224 | tf_op jit(solution)/shard_map/ppermute | solution.py:76
  26.7 4.9 %collective-permute-start.3 = (bf16[64,1024]{1,0:T(8,128)(2,1)S(1)}, bf16[64,1024]{1,0:T(8,128)(2,1)S(1)}, u32[]{:S(2)}, u32[]{:S(2)}) collective-permute-start(bf16[64,1024]{1,0:T(8,128)(2,1)S(1)} %slice.8), channel_id=1, source_target_pairs={{2,0},{3,1},{4,2},{5,3},{6,4},{7,5},{0,6},{1,7},{10,8},{11,9},{12,... | collective-permute-start | bytes 393224 | tf_op jit(solution)/shard_map/ppermute | solution.py:77
  31.5 3.9 %all-to-all-start = ((bf16[8,128,128]{2,1,0:T(8,128)(2,1)}), bf16[8,128,128]{2,1,0:T(8,128)(2,1)S(1)}, u32[]{:S(2)}, u32[]{:S(2)}) async-start(bf16[8,128,128]{2,1,0:T(8,128)(2,1)} %bitcast.4), calls=%async_computation | async-start | bytes 524288 | tf_op jit(solution)/shard_map/all_to_all | solution.py:81
  35.4 0.9 collective-permute-done.3
  36.4 2.4 %collective-permute-start.5 = (bf16[128,1024]{1,0:T(8,128)(2,1)S(1)}, bf16[128,1024]{1,0:T(8,128)(2,1)S(1)}, u32[]{:S(2)}, u32[]{:S(2)}) collective-permute-start(bf16[128,1024]{1,0:T(8,128)(2,1)S(1)} %constant_dynamic-update-slice_fusion.3.far), channel_id=1, source_target_pairs={{0,1},{1,0},{2,3},{3,2},{4,5},{5,4},{6,7},{7,6},{8,9},{9,8},{10,11... | collective-permute-start | bytes 786440 | tf_op jit(solution)/shard_map/ppermute | solution.py:82
  39.0 0.9 collective-permute-done.5.far_across
  40.6 3.6 %all-to-all-done = bf16[8,128,128]{2,1,0:T(8,128)(2,1)S(1)} async-done(((bf16[8,128,128]{2,1,0:T(8,128)(2,1)}), bf16[8,128,128]{2,1,0:T(8,128)(2,1)S(1)}, u32[]{:S(2)}, u32[]{:S(2)}) %all-to-all-start) | async-done | bytes 262176 | tf_op jit(solution)/shard_map/all_to_all | solution.py:81
  44.2 1.1 project_near.1.near_pairs
  45.4 0.8 project_far.1.own
  46.2 7.5 %collective-permute-start.8 = (bf16[1024,256]{1,0:T(8,128)(2,1)S(1)}, bf16[1024,256]{1,0:T(8,128)(2,1)S(1)}, u32[]{:S(2)}, u32[]{:S(2)}) collective-permute-start(bf16[1024,256]{1,0:T(8,128)(2,1)S(1)} %project_far.1.own), channel_id=1, source_target_pairs={{0,128},{128,0},{8,136},{136,8},{16,144},{144,16},{24,152},{152,24... | collective-permute-start | bytes 1572872 | tf_op jit(solution)/shard_map/ppermute | solution.py:38
  53.6 8.2 %collective-permute-start.7 = (bf16[1024,256]{1,0:T(8,128)(2,1)S(1)}, bf16[1024,256]{1,0:T(8,128)(2,1)S(1)}, u32[]{:S(2)}, u32[]{:S(2)}) collective-permute-start(bf16[1024,256]{1,0:T(8,128)(2,1)S(1)} %project_far.1.own), channel_id=1, source_target_pairs={{0,256},{256,0},{8,264},{264,8},{16,272},{272,16},{24,280},{280,24... | collective-permute-start | bytes 1572872 | tf_op jit(solution)/shard_map/ppermute | solution.py:38
  61.8 3.1 %collective-permute-start.6 = (bf16[1024,256]{1,0:T(8,128)(2,1)S(1)}, bf16[1024,256]{1,0:T(8,128)(2,1)S(1)}, u32[]{:S(2)}, u32[]{:S(2)}) collective-permute-start(bf16[1024,256]{1,0:T(8,128)(2,1)S(1)} %project_far.1.own), channel_id=1, source_target_pairs={{0,8},{8,0},{16,24},{24,16},{32,40},{40,32},{48,56},{56,48},{64,72... | collective-permute-start | bytes 1572872 | tf_op jit(solution)/shard_map/ppermute | solution.py:38
  65.0 3.0 %order.1 = (bf16[1024,1024]{1,0:T(8,128)(2,1)S(1)}, bf16[1024,256]{1,0:T(8,128)(2,1)S(1)}) custom-call(s32[1]{0:T(128)} %bitcast.place, bf16[384,1024]{1,0:T(8,128)(2,1)S(1)} %constant_dynamic-update-slice_fusion.near, bf16[128,1024]{1,0:T(8,128)(2,1)S(1)} %constant_dynamic-update-slice_fusion.3.far, ...), custom_call_target="tpu_custom_call" | custom-call | tf_op jit(solution)/shard_map/order/pallas_call | solution.py:394
  68.3 15.8 %collective-permute-done.7.two = bf16[1024,256]{1,0:T(8,128)(2,1)S(1)} collective-permute-done((bf16[1024,256]{1,0:T(8,128)(2,1)S(1)}, bf16[1024,256]{1,0:T(8,128)(2,1)S(1)}, u32[]{:S(2)}, u32[]{:S(2)}) %collective-permute-start.7) | collective-permute-done | bytes 524320 | tf_op jit(solution)/shard_map/ppermute | solution.py:38
  84.1 8.1 %attend.1 = (bf16[1024,128]{1,0:T(8,128)(2,1)S(1)}, bf16[1024,128]{1,0:T(8,128)(2,1)S(1)}, f32[1024,256]{1,0:T(8,128)S(1)}, bf16[1024,256]{1,0:T(8,128)(2,1)S(1)...) custom-call(s32[3,8]{1,0:T(4,128)S(1)} %add_select_fusion.slots, ...), custom_call_target="tpu_custom_call" | custom-call | tf_op jit(solution)/shard_map/attend/pallas_call | solution.py:403
  92.2 2.1 %collective-permute-start.9 = (bf16[1024,256]{1,0:T(8,128)(2,1)S(1)}, bf16[1024,256]{1,0:T(8,128)(2,1)S(1)}, u32[]{:S(2)}, u32[]{:S(2)}) collective-permute-start(bf16[1024,256]{1,0:T(8,128)(2,1)S(1)} %get-tuple-element.45), channel_id=1, source_target_pairs={{0,128},{128,0},{8,136},{136,8},{16,144},{144,16},{24,152},{152,24... | collective-permute-start | bytes 1572872 | tf_op jit(solution)/shard_map/ppermute | solution.py:38
  94.3 3.9 %collective-permute-start.10 = (bf16[1024,256]{1,0:T(8,128)(2,1)S(1)}, bf16[1024,256]{1,0:T(8,128)(2,1)S(1)}, u32[]{:S(2)}, u32[]{:S(2)}) collective-permute-start(bf16[1024,256]{1,0:T(8,128)(2,1)S(1)} %get-tuple-element.46), channel_id=1, source_target_pairs={{0,256},{256,0},{8,264},{264,8},{16,272},{272,16},{24,280},{280,24... | collective-permute-start | bytes 1572872 | tf_op jit(solution)/shard_map/ppermute | solution.py:38
  98.2 3.3 %collective-permute-start.11 = (bf16[1024,256]{1,0:T(8,128)(2,1)S(1)}, bf16[1024,256]{1,0:T(8,128)(2,1)S(1)}, u32[]{:S(2)}, u32[]{:S(2)}) collective-permute-start(bf16[1024,256]{1,0:T(8,128)(2,1)S(1)} %get-tuple-element.47), channel_id=1, source_target_pairs={{0,8},{8,0},{16,24},{24,16},{32,40},{40,32},{48,56},{56,48},{64,72... | collective-permute-start | bytes 1572872 | tf_op jit(solution)/shard_map/ppermute | solution.py:38
  101.5 2.3 %query_grads.1 = (bf16[1024,128]{1,0:T(8,128)(2,1)S(1)}, bf16[1024,128]{1,0:T(8,128)(2,1)S(1)}) custom-call(bf16[1024,1024]{1,0:T(8,128)(2,1)S(1)} %get-tuple-element.39.features, s32[1,1024]{1,0:T(1,128)S(1)} %bitcast.17, bf16[1024,128]{1,0:T(8,128)(2,1)S(1)} %get-tuple-element.41.dquery), custom_call_target="tpu_custom_call" | custom-call | tf_op jit(solution)/shard_map/query_grads/pallas_call | solution.py:427
  103.7 9.4 %collective-permute-done.9.first = bf16[1024,256]{1,0:T(8,128)(2,1)S(1)} collective-permute-done((bf16[1024,256]{1,0:T(8,128)(2,1)S(1)}, bf16[1024,256]{1,0:T(8,128)(2,1)S(1)}, u32[]{:S(2)}, u32[]{:S(2)}) %collective-permute-start.9) | collective-permute-done | bytes 524320 | tf_op jit(solution)/shard_map/ppermute | solution.py:38
  113.1 3.6 %collective-permute-done.10.second = bf16[1024,256]{1,0:T(8,128)(2,1)S(1)} collective-permute-done((bf16[1024,256]{1,0:T(8,128)(2,1)S(1)}, bf16[1024,256]{1,0:T(8,128)(2,1)S(1)}, u32[]{:S(2)}, u32[]{:S(2)}) %collective-permute-start.10) | collective-permute-done | bytes 524320 | tf_op jit(solution)/shard_map/ppermute | solution.py:38
  116.8 3.1 %finish.1 = (bf16[1024,384]{1,0:T(8,128)(2,1)}, bf16[1024,256]{1,0:T(8,128)(2,1)S(1)}) custom-call(bf16[1024,1024]{1,0:T(8,128)(2,1)S(1)} %get-tuple-element.39.features, s32[1,1024]{1,0:T(1,128)S(1)} %bitcast.18, bf16[1024,128]{1,0:T(8,128)(2,1)S(1)} %get-tuple-element.43.query_part, f32[1024,256]{1,0:T(8,128)S(1)} %get-tuple-element.44.own, ...), custom_call_target="tpu_custom_call" | custom-call | tf_op jit(solution)/shard_map/finish/pallas_call | solution.py:435
  119.9 14.2 %all-to-all-start.1 = ((bf16[32,32,384]{2,1,0:T(8,128)(2,1)}), bf16[32,32,384]{2,1,0:T(8,128)(2,1)}, u32[]{:S(2)}, u32[]{:S(2)}) async-start(bf16[32,32,384]{2,1,0:T(8,128)(2,1)} %bitcast.8), calls=%async_computation.1 | async-start | bytes 1572864 | tf_op jit(solution)/shard_map/all_to_all | solution.py:55
  134.1 0.7 restore.1.mixed_nodes
  134.8 1.3 features.1
  136.1 2.7 %collective-permute-start.12 = (bf16[512,1152]{1,0:T(8,128)(2,1)S(1)}, bf16[512,1152]{1,0:T(8,128)(2,1)S(1)}, u32[]{:S(2)}, u32[]{:S(2)}) collective-permute-start(bf16[512,1152]{1,0:T(8,128)(2,1)S(1)} %get-tuple-element.51), channel_id=1, source_target_pairs={{0,1},{1,0},{2,3},{3,2},{4,5},{5,4},{6,7},{7,6},{8,9},{9,8},{10,11... | collective-permute-start | bytes 3538952 | tf_op jit(solution)/shard_map/ppermute | solution.py:460
  138.8 2.5 %collective-permute-done.12.got = bf16[512,1152]{1,0:T(8,128)(2,1)S(1)} collective-permute-done((bf16[512,1152]{1,0:T(8,128)(2,1)S(1)}, bf16[512,1152]{1,0:T(8,128)(2,1)S(1)}, u32[]{:S(2)}, u32[]{:S(2)}) %collective-permute-start.12) | collective-permute-done | bytes 1179680 | tf_op jit(solution)/shard_map/ppermute | solution.py:460
  141.3 2.2 %collective-permute-start.13 = (bf16[64,1280]{1,0:T(8,128)(2,1)S(1)}, bf16[64,1280]{1,0:T(8,128)(2,1)S(1)}, u32[]{:S(2)}, u32[]{:S(2)}) collective-permute-start(bf16[64,1280]{1,0:T(8,128)(2,1)S(1)} %get-tuple-element.53), channel_id=1, source_target_pairs={{0,2},{1,3},{2,4},{3,5},{4,6},{5,7},{6,0},{7,1},{8,10},{9,11},{10,... | collective-permute-start | bytes 491528 | tf_op jit(solution)/shard_map/ppermute | solution.py:469
  143.5 4.9 %collective-permute-start.14 = (bf16[64,1280]{1,0:T(8,128)(2,1)S(1)}, bf16[64,1280]{1,0:T(8,128)(2,1)S(1)}, u32[]{:S(2)}, u32[]{:S(2)}) collective-permute-start(bf16[64,1280]{1,0:T(8,128)(2,1)S(1)} %get-tuple-element.54), channel_id=1, source_target_pairs={{2,0},{3,1},{4,2},{5,3},{6,4},{7,5},{0,6},{1,7},{10,8},{11,9},{12,... | collective-permute-start | bytes 491528 | tf_op jit(solution)/shard_map/ppermute | solution.py:470
  148.4 2.2 %collective-permute-done.13.from_low = bf16[64,1280]{1,0:T(8,128)(2,1)S(1)} collective-permute-done((bf16[64,1280]{1,0:T(8,128)(2,1)S(1)}, bf16[64,1280]{1,0:T(8,128)(2,1)S(1)}, u32[]{:S(2)}, u32[]{:S(2)}) %collective-permute-start.13) | collective-permute-done | bytes 163872 | tf_op jit(solution)/shard_map/ppermute | solution.py:469
  150.6 4.2 %collective-permute-done.14.from_high = bf16[64,1280]{1,0:T(8,128)(2,1)S(1)} collective-permute-done((bf16[64,1280]{1,0:T(8,128)(2,1)S(1)}, bf16[64,1280]{1,0:T(8,128)(2,1)S(1)}, u32[]{:S(2)}, u32[]{:S(2)}) %collective-permute-start.14) | collective-permute-done | bytes 163872 | tf_op jit(solution)/shard_map/ppermute | solution.py:470
  155.1 1.3 convert_reduce_fusion
  156.3 4.2 %collective-permute-start.17 = (f32[32,384]{1,0:T(8,128)S(1)}, f32[32,384]{1,0:T(8,128)S(1)}, u32[]{:S(2)}, u32[]{:S(2)}) collective-permute-start(f32[32,384]{1,0:T(8,128)S(1)} %convert_reduce_fusion), channel_id=1, source_target_pairs={{0,256},{256,0},{8,264},{264,8},{16,272},{272,16},{24,280},{280,24... | collective-permute-start | bytes 147464 | tf_op jit(solution)/shard_map/ppermute | solution.py:38
  160.5 4.6 %collective-permute-done.17 = f32[32,384]{1,0:T(8,128)S(1)} collective-permute-done((f32[32,384]{1,0:T(8,128)S(1)}, f32[32,384]{1,0:T(8,128)S(1)}, u32[]{:S(2)}, u32[]{:S(2)}) %collective-permute-start.17) | collective-permute-done | bytes 49184 | tf_op jit(solution)/shard_map/ppermute | solution.py:38
  165.1 1.0 broadcast_in_dim.2
  166.0 9.1 %all-to-all-start.2 = ((bf16[32,32,384]{2,1,0:T(8,128)(2,1)}), bf16[32,32,384]{2,1,0:T(8,128)(2,1)S(1)}, u32[]{:S(2)}, u32[]{:S(2)}) async-start(bf16[32,32,384]{2,1,0:T(8,128)(2,1)} %broadcast_in_dim.2), calls=%async_computation.2 | async-start | bytes 1572864 | tf_op jit(solution)/shard_map/all_to_all | solution.py:55
  175.4 3.0 %collective-permute-start.15 = (bf16[128,1408]{1,0:T(8,128)(2,1)S(1)}, bf16[128,1408]{1,0:T(8,128)(2,1)S(1)}, u32[]{:S(2)}, u32[]{:S(2)}) collective-permute-start(bf16[128,1408]{1,0:T(8,128)(2,1)S(1)} %get-tuple-element.57), channel_id=1, source_target_pairs={{0,2},{1,3},{2,4},{3,5},{4,6},{5,7},{6,0},{7,1},{8,10},{9,11},{10,... | collective-permute-start | bytes 1081352 | tf_op jit(solution)/shard_map/ppermute | solution.py:481
  178.3 4.1 %collective-permute-start.16 = (bf16[128,1408]{1,0:T(8,128)(2,1)S(1)}, bf16[128,1408]{1,0:T(8,128)(2,1)S(1)}, u32[]{:S(2)}, u32[]{:S(2)}) collective-permute-start(bf16[128,1408]{1,0:T(8,128)(2,1)S(1)} %get-tuple-element.58), channel_id=1, source_target_pairs={{2,0},{3,1},{4,2},{5,3},{6,4},{7,5},{0,6},{1,7},{10,8},{11,9},{12,... | collective-permute-start | bytes 1081352 | tf_op jit(solution)/shard_map/ppermute | solution.py:482
  182.4 4.7 %collective-permute-done.15.from_low = bf16[128,1408]{1,0:T(8,128)(2,1)S(1)} collective-permute-done((bf16[128,1408]{1,0:T(8,128)(2,1)S(1)}, bf16[128,1408]{1,0:T(8,128)(2,1)S(1)}, u32[]{:S(2)}, u32[]{:S(2)}) %collective-permute-start.15) | collective-permute-done | bytes 360480 | tf_op jit(solution)/shard_map/ppermute | solution.py:481
  187.2 9.9 %collective-permute-done.16.from_high = bf16[128,1408]{1,0:T(8,128)(2,1)S(1)} collective-permute-done((bf16[128,1408]{1,0:T(8,128)(2,1)S(1)}, bf16[128,1408]{1,0:T(8,128)(2,1)S(1)}, u32[]{:S(2)}, u32[]{:S(2)}) %collective-permute-start.16) | collective-permute-done | bytes 360480 | tf_op jit(solution)/shard_map/ppermute | solution.py:482
  197.1 0.9 collect.1
  198.0 1.6 widen.1
  (36 shorter events, 2.1 us)
Async XLA Ops:
  0.6 12.5 %copy-start.6 = (bf16[128,1024]{1,0:T(8,128)(2,1)S(1)}, bf16[128,1024]{1,0:T(8,128)(2,1)}, u32[]{:S(2)}) copy-start(bf16[128,1024]{1,0:T(8,128)(2,1)} %param.7) | copy-start | bytes 786436
  0.6 12.7 %collective-permute-start = (bf16[128,1024]{1,0:T(8,128)(2,1)}, bf16[128,1024]{1,0:T(8,128)(2,1)S(1)}, u32[]{:S(2)}, u32[]{:S(2)}) collective-permute-start(bf16[128,1024]{1,0:T(8,128)(2,1)} %param.7), channel_id=1, source_target_pairs={{0,2},{1,3},{2,4},{3,5},{4,6},{5,7},{6,0},{7,1},{8,10},{9,11},{10,... | collective-permute-start | bytes 786440 | tf_op jit(solution)/shard_map/ppermute | solution.py:73
  5.6 14.9 %collective-permute-start.1 = (bf16[128,1024]{1,0:T(8,128)(2,1)}, bf16[128,1024]{1,0:T(8,128)(2,1)S(1)}, u32[]{:S(2)}, u32[]{:S(2)}) collective-permute-start(bf16[128,1024]{1,0:T(8,128)(2,1)} %param.7), channel_id=1, source_target_pairs={{2,0},{3,1},{4,2},{5,3},{6,4},{7,5},{0,6},{1,7},{10,8},{11,9},{12,... | collective-permute-start | bytes 786440 | tf_op jit(solution)/shard_map/ppermute | solution.py:74
  13.4 25.4 %copy-start.5 = (s32[1024]{0:T(1024)S(1)}, s32[1024]{0:T(1024)}, u32[]{:S(2)}) copy-start(s32[1024]{0:T(1024)} %param.8) | copy-start | bytes 12292
  20.5 23.6 %copy-start = (bf16[1024,128]{1,0:T(8,128)(2,1)S(1)}, bf16[1024,128]{1,0:T(8,128)(2,1)}, u32[]{:S(2)}) copy-start(bf16[1024,128]{1,0:T(8,128)(2,1)} %key_weight.5) | copy-start | bytes 786436
  20.5 23.6 %copy-start.1 = (bf16[1024,128]{1,0:T(8,128)(2,1)S(1)}, bf16[1024,128]{1,0:T(8,128)(2,1)}, u32[]{:S(2)}) copy-start(bf16[1024,128]{1,0:T(8,128)(2,1)} %value_weight.5) | copy-start | bytes 786436
  20.5 23.6 %collective-permute-start.4 = (bf16[384,1024]{1,0:T(8,128)(2,1)S(1)}, bf16[384,1024]{1,0:T(8,128)(2,1)S(1)}, u32[]{:S(2)}, u32[]{:S(2)}) collective-permute-start(bf16[384,1024]{1,0:T(8,128)(2,1)S(1)} %constant_dynamic-update-slice_fusion.near), channel_id=1, source_target_pairs={{0,1},{1,0},{2,3},{3,2},{4,5},{5,4},{6,7},{7,6},{8,9},{9,8},{10,11... | collective-permute-start | bytes 2359304 | tf_op jit(solution)/shard_map/ppermute | solution.py:80
  24.4 11.0 %collective-permute-start.2 = (bf16[64,1024]{1,0:T(8,128)(2,1)S(1)}, bf16[64,1024]{1,0:T(8,128)(2,1)S(1)}, u32[]{:S(2)}, u32[]{:S(2)}) collective-permute-start(bf16[64,1024]{1,0:T(8,128)(2,1)S(1)} %slice.6), channel_id=1, source_target_pairs={{0,2},{1,3},{2,4},{3,5},{4,6},{5,7},{6,0},{7,1},{8,10},{9,11},{10,... | collective-permute-start | bytes 393224 | tf_op jit(solution)/shard_map/ppermute | solution.py:76
  26.7 9.7 %collective-permute-start.3 = (bf16[64,1024]{1,0:T(8,128)(2,1)S(1)}, bf16[64,1024]{1,0:T(8,128)(2,1)S(1)}, u32[]{:S(2)}, u32[]{:S(2)}) collective-permute-start(bf16[64,1024]{1,0:T(8,128)(2,1)S(1)} %slice.8), channel_id=1, source_target_pairs={{2,0},{3,1},{4,2},{5,3},{6,4},{7,5},{0,6},{1,7},{10,8},{11,9},{12,... | collective-permute-start | bytes 393224 | tf_op jit(solution)/shard_map/ppermute | solution.py:77
  31.5 12.6 %all-to-all-start = ((bf16[8,128,128]{2,1,0:T(8,128)(2,1)}), bf16[8,128,128]{2,1,0:T(8,128)(2,1)S(1)}, u32[]{:S(2)}, u32[]{:S(2)}) async-start(bf16[8,128,128]{2,1,0:T(8,128)(2,1)} %bitcast.4), calls=%async_computation | async-start | bytes 524288 | tf_op jit(solution)/shard_map/all_to_all | solution.py:81
  36.4 3.5 %collective-permute-start.5 = (bf16[128,1024]{1,0:T(8,128)(2,1)S(1)}, bf16[128,1024]{1,0:T(8,128)(2,1)S(1)}, u32[]{:S(2)}, u32[]{:S(2)}) collective-permute-start(bf16[128,1024]{1,0:T(8,128)(2,1)S(1)} %constant_dynamic-update-slice_fusion.3.far), channel_id=1, source_target_pairs={{0,1},{1,0},{2,3},{3,2},{4,5},{5,4},{6,7},{7,6},{8,9},{9,8},{10,11... | collective-permute-start | bytes 786440 | tf_op jit(solution)/shard_map/ppermute | solution.py:82
  39.9 0.7 copy-start.3
  44.2 1.2 copy-start.4
  45.3 19.6 %copy-start.7 = (s32[3,8]{1,0:T(4,128)S(1)}, s32[3,8]{1,0:T(4,128)}, u32[]{:S(2)}) copy-start(s32[3,8]{1,0:T(4,128)} %param.9) | copy-start | bytes 292
  45.3 19.6 %copy-start.2 = (bf16[1024,128]{1,0:T(8,128)(2,1)S(1)}, bf16[1024,128]{1,0:T(8,128)(2,1)}, u32[]{:S(2)}) copy-start(bf16[1024,128]{1,0:T(8,128)(2,1)} %query_weight.1) | copy-start | bytes 786436
  46.2 22.1 %collective-permute-start.8 = (bf16[1024,256]{1,0:T(8,128)(2,1)S(1)}, bf16[1024,256]{1,0:T(8,128)(2,1)S(1)}, u32[]{:S(2)}, u32[]{:S(2)}) collective-permute-start(bf16[1024,256]{1,0:T(8,128)(2,1)S(1)} %project_far.1.own), channel_id=1, source_target_pairs={{0,128},{128,0},{8,136},{136,8},{16,144},{144,16},{24,152},{152,24... | collective-permute-start | bytes 1572872 | tf_op jit(solution)/shard_map/ppermute | solution.py:38
  53.6 30.4 %collective-permute-start.7 = (bf16[1024,256]{1,0:T(8,128)(2,1)S(1)}, bf16[1024,256]{1,0:T(8,128)(2,1)S(1)}, u32[]{:S(2)}, u32[]{:S(2)}) collective-permute-start(bf16[1024,256]{1,0:T(8,128)(2,1)S(1)} %project_far.1.own), channel_id=1, source_target_pairs={{0,256},{256,0},{8,264},{264,8},{16,272},{272,16},{24,280},{280,24... | collective-permute-start | bytes 1572872 | tf_op jit(solution)/shard_map/ppermute | solution.py:38
  61.8 22.2 %collective-permute-start.6 = (bf16[1024,256]{1,0:T(8,128)(2,1)S(1)}, bf16[1024,256]{1,0:T(8,128)(2,1)S(1)}, u32[]{:S(2)}, u32[]{:S(2)}) collective-permute-start(bf16[1024,256]{1,0:T(8,128)(2,1)S(1)} %project_far.1.own), channel_id=1, source_target_pairs={{0,8},{8,0},{16,24},{24,16},{32,40},{40,32},{48,56},{56,48},{64,72... | collective-permute-start | bytes 1572872 | tf_op jit(solution)/shard_map/ppermute | solution.py:38
  92.2 21.0 %collective-permute-start.9 = (bf16[1024,256]{1,0:T(8,128)(2,1)S(1)}, bf16[1024,256]{1,0:T(8,128)(2,1)S(1)}, u32[]{:S(2)}, u32[]{:S(2)}) collective-permute-start(bf16[1024,256]{1,0:T(8,128)(2,1)S(1)} %get-tuple-element.45), channel_id=1, source_target_pairs={{0,128},{128,0},{8,136},{136,8},{16,144},{144,16},{24,152},{152,24... | collective-permute-start | bytes 1572872 | tf_op jit(solution)/shard_map/ppermute | solution.py:38
  94.3 22.4 %collective-permute-start.10 = (bf16[1024,256]{1,0:T(8,128)(2,1)S(1)}, bf16[1024,256]{1,0:T(8,128)(2,1)S(1)}, u32[]{:S(2)}, u32[]{:S(2)}) collective-permute-start(bf16[1024,256]{1,0:T(8,128)(2,1)S(1)} %get-tuple-element.46), channel_id=1, source_target_pairs={{0,256},{256,0},{8,264},{264,8},{16,272},{272,16},{24,280},{280,24... | collective-permute-start | bytes 1572872 | tf_op jit(solution)/shard_map/ppermute | solution.py:38
  98.2 18.6 %collective-permute-start.11 = (bf16[1024,256]{1,0:T(8,128)(2,1)S(1)}, bf16[1024,256]{1,0:T(8,128)(2,1)S(1)}, u32[]{:S(2)}, u32[]{:S(2)}) collective-permute-start(bf16[1024,256]{1,0:T(8,128)(2,1)S(1)} %get-tuple-element.47), channel_id=1, source_target_pairs={{0,8},{8,0},{16,24},{24,16},{32,40},{40,32},{48,56},{56,48},{64,72... | collective-permute-start | bytes 1572872 | tf_op jit(solution)/shard_map/ppermute | solution.py:38
  119.9 35.2 %all-to-all-start.1 = ((bf16[32,32,384]{2,1,0:T(8,128)(2,1)}), bf16[32,32,384]{2,1,0:T(8,128)(2,1)}, u32[]{:S(2)}, u32[]{:S(2)}) async-start(bf16[32,32,384]{2,1,0:T(8,128)(2,1)} %bitcast.8), calls=%async_computation.1 | async-start | bytes 1572864 | tf_op jit(solution)/shard_map/all_to_all | solution.py:55
  136.1 5.1 %collective-permute-start.12 = (bf16[512,1152]{1,0:T(8,128)(2,1)S(1)}, bf16[512,1152]{1,0:T(8,128)(2,1)S(1)}, u32[]{:S(2)}, u32[]{:S(2)}) collective-permute-start(bf16[512,1152]{1,0:T(8,128)(2,1)S(1)} %get-tuple-element.51), channel_id=1, source_target_pairs={{0,1},{1,0},{2,3},{3,2},{4,5},{5,4},{6,7},{7,6},{8,9},{9,8},{10,11... | collective-permute-start | bytes 3538952 | tf_op jit(solution)/shard_map/ppermute | solution.py:460
  141.3 9.3 %collective-permute-start.13 = (bf16[64,1280]{1,0:T(8,128)(2,1)S(1)}, bf16[64,1280]{1,0:T(8,128)(2,1)S(1)}, u32[]{:S(2)}, u32[]{:S(2)}) collective-permute-start(bf16[64,1280]{1,0:T(8,128)(2,1)S(1)} %get-tuple-element.53), channel_id=1, source_target_pairs={{0,2},{1,3},{2,4},{3,5},{4,6},{5,7},{6,0},{7,1},{8,10},{9,11},{10,... | collective-permute-start | bytes 491528 | tf_op jit(solution)/shard_map/ppermute | solution.py:469
  143.5 11.2 %collective-permute-start.14 = (bf16[64,1280]{1,0:T(8,128)(2,1)S(1)}, bf16[64,1280]{1,0:T(8,128)(2,1)S(1)}, u32[]{:S(2)}, u32[]{:S(2)}) collective-permute-start(bf16[64,1280]{1,0:T(8,128)(2,1)S(1)} %get-tuple-element.54), channel_id=1, source_target_pairs={{2,0},{3,1},{4,2},{5,3},{6,4},{7,5},{0,6},{1,7},{10,8},{11,9},{12,... | collective-permute-start | bytes 491528 | tf_op jit(solution)/shard_map/ppermute | solution.py:470
  156.3 8.7 %collective-permute-start.17 = (f32[32,384]{1,0:T(8,128)S(1)}, f32[32,384]{1,0:T(8,128)S(1)}, u32[]{:S(2)}, u32[]{:S(2)}) collective-permute-start(f32[32,384]{1,0:T(8,128)S(1)} %convert_reduce_fusion), channel_id=1, source_target_pairs={{0,256},{256,0},{8,264},{264,8},{16,272},{272,16},{24,280},{280,24... | collective-permute-start | bytes 147464 | tf_op jit(solution)/shard_map/ppermute | solution.py:38
  166.0 32.0 %all-to-all-start.2 = ((bf16[32,32,384]{2,1,0:T(8,128)(2,1)}), bf16[32,32,384]{2,1,0:T(8,128)(2,1)S(1)}, u32[]{:S(2)}, u32[]{:S(2)}) async-start(bf16[32,32,384]{2,1,0:T(8,128)(2,1)} %broadcast_in_dim.2), calls=%async_computation.2 | async-start | bytes 1572864 | tf_op jit(solution)/shard_map/all_to_all | solution.py:55
  175.4 11.8 %collective-permute-start.15 = (bf16[128,1408]{1,0:T(8,128)(2,1)S(1)}, bf16[128,1408]{1,0:T(8,128)(2,1)S(1)}, u32[]{:S(2)}, u32[]{:S(2)}) collective-permute-start(bf16[128,1408]{1,0:T(8,128)(2,1)S(1)} %get-tuple-element.57), channel_id=1, source_target_pairs={{0,2},{1,3},{2,4},{3,5},{4,6},{5,7},{6,0},{7,1},{8,10},{9,11},{10,... | collective-permute-start | bytes 1081352 | tf_op jit(solution)/shard_map/ppermute | solution.py:481
  178.3 18.7 %collective-permute-start.16 = (bf16[128,1408]{1,0:T(8,128)(2,1)S(1)}, bf16[128,1408]{1,0:T(8,128)(2,1)S(1)}, u32[]{:S(2)}, u32[]{:S(2)}) collective-permute-start(bf16[128,1408]{1,0:T(8,128)(2,1)S(1)} %get-tuple-element.58), channel_id=1, source_target_pairs={{2,0},{3,1},{4,2},{5,3},{6,4},{7,5},{0,6},{1,7},{10,8},{11,9},{12,... | collective-permute-start | bytes 1081352 | tf_op jit(solution)/shard_map/ppermute | solution.py:482
